TPU v7x, 32 devices: a whole 2x2x4 slice. The times are simulated.
32 devices in a mesh: dp: 4 (over y, x), seq: 8 (over z, core).
Axes of the slice: x: 2, y: 2, z: 4, core: 2. Of those that a mesh axis runs over, the one named last changes fastest.
Arguments:
- layer_input: bfloat16 [8192, 2048], P(('dp', 'seq')), may hold values from -6 to 6
- attn_gain: bfloat16 [2048], P(('dp', 'seq')), may hold values from 0.5 to 1.5
- w_query: bfloat16 [2048, 4096], P('dp', 'seq'), may hold values from -0.125 to 0.125
- key_matrix: bfloat16 [2048, 512], P(('dp', 'seq')), may hold values from -0.125 to 0.125
- value_matrix: bfloat16 [2048, 512], P(('dp', 'seq')), may hold values from -0.125 to 0.125
- query_gain: bfloat16 [128], replicated, may hold values from 0.5 to 1.5
- key_gain: bfloat16 [128], replicated, may hold values from 0.5 to 1.5
- w_out: bfloat16 [4096, 2048], P(('dp', 'seq')), may hold values from -1.5 to 1.5
- moe_gain: bfloat16 [2048], P(('dp', 'seq')), may hold values from 0.5 to 1.5
- router: bfloat16 [2048, 32], P(('dp', 'seq')), may hold values from -0.06591797 to 0.06591797
- expert_gate: bfloat16 [32, 2048, 768], P(('dp', 'seq')), may hold values from -0.125 to 0.125
- expert_up: bfloat16 [32, 2048, 768], P(('dp', 'seq')), may hold values from -0.125 to 0.125
- expert_down: bfloat16 [32, 768, 2048], P(('dp', 'seq')), may hold values from -0.625 to 0.625
- expert_ids: int32 [8192, 8], P(('dp', 'seq')), may hold values from 0 to 31, all different within a row
- cont_segment: int32 [4, 1024], P('dp'), may hold values from 0 to 3, never falling along the last dimension, each value on 1 to 512 neighbouring positions
- out_grad: bfloat16 [8192, 2048], P(('dp', 'seq')), may hold values from -6 to 6
Outputs:
- layer_output: bfloat16 [8192, 2048], P(('dp', 'seq'))
- x_grad: float32 [8192, 2048], P(('dp', 'seq'))
- attn_gain_grad: float32 [2048], P(('dp', 'seq'))
- w_query_grad: float32 [2048, 4096], P('dp', 'seq')
- w_key_grad: float32 [2048, 512], P(('dp', 'seq'))
- w_value_grad: float32 [2048, 512], P(('dp', 'seq'))
- query_gain_grad: float32 [128], replicated
- key_gain_grad: float32 [128], replicated
- w_out_grad: float32 [4096, 2048], P(('dp', 'seq'))
- moe_gain_grad: float32 [2048], P(('dp', 'seq'))
- router_grad: float32 [2048, 32], P(('dp', 'seq'))
- expert_gate_grad: float32 [32, 2048, 768], P(('dp', 'seq'))
- expert_up_grad: float32 [32, 2048, 768], P(('dp', 'seq'))
- expert_down_grad: float32 [32, 768, 2048], P(('dp', 'seq'))
Inputs may be any that keep to these rules, and one draw needn't show every extreme that they name: `expert_ids`: each token names 8 different experts. `cont_segment`: continuation numbers never fall along a group; each continuation holds 1 to 512 tokens and one holds exactly that many.
All inputs are finite; a program needn't handle non-finite values.
Results may differ from a plain program's by a relative error of at most 0.022.
Values may be sent and summed in bfloat16 or wider, within the bound.
No kernel may reach another device: no remote copies, remote signals or barrier semaphores. Data moves between devices by JAX's collectives and lax.ppermute only.
A program may use at most 320 MiB of HBM per device.

v0:
```python
from functools import partial
import math

import jax
import jax.numpy as jnp
from jax import lax
from jax.sharding import PartitionSpec as P

HQ = 32
KEY_VALUE_HEADS = 4
TOP = 8
PROMPT = 1024
NCONT = 4
QBLK = 512


EPS = 1e-06
THETA = 1000000.0


def norm_rows(value, gain):
    factor = lax.rsqrt(jnp.mean(value * value, axis=-1, keepdims=True) + EPS)
    return value * factor * gain


def rotate(value, cosine, sine):
    middle = value.shape[-1] // 2
    turned = jnp.concatenate([-value[..., middle:], value[..., :middle]], axis=-1)
    return value * cosine + turned * sine


def angle_tables(where_at, head_width):
    ranks = jnp.arange(head_width // 2, dtype=jnp.float32) * (2.0 / head_width)
    inverse = jnp.exp(-ranks * math.log(THETA))
    angles = where_at.astype(jnp.float32)[:, None] * inverse[None, :]
    angles = jnp.concatenate([angles, angles], axis=-1)
    return (jnp.cos(angles)[:, None, :], jnp.sin(angles)[:, None, :])


def group_layout(segment):
    length = segment.shape[0]
    one_hot = (segment[:, None] == jnp.arange(NCONT, dtype=jnp.int32)[None, :]).astype(jnp.int32)
    counted = jnp.sum(one_hot, axis=0)
    starts = jnp.cumsum(counted) - counted
    begins = jnp.sum(one_hot * starts[None, :], axis=1)
    within = jnp.arange(length, dtype=jnp.int32) - begins
    where_at = jnp.concatenate([jnp.arange(PROMPT, dtype=jnp.int32), PROMPT + within])
    labels = jnp.concatenate([jnp.zeros((PROMPT,), jnp.int32), segment + 1])
    return (where_at, labels)


def block_mask(labels, start, rows):
    query_at = start + jnp.arange(rows, dtype=jnp.int32)
    key_at = jnp.arange(labels.shape[0], dtype=jnp.int32)
    query_label = lax.dynamic_slice_in_dim(labels, start, rows, 0)
    causal = key_at[None, :] <= query_at[:, None]
    same = (labels[None, :] == 0) | (labels[None, :] == query_label[:, None])
    return causal & same


def slot_plan(ids, experts, capacity):
    flat = ids.reshape(-1)
    one_hot = (flat[:, None] == jnp.arange(experts, dtype=jnp.int32)[None, :]).astype(jnp.int32)
    earlier = jnp.cumsum(one_hot, axis=0) - one_hot
    slots = jnp.sum(earlier * one_hot, axis=1)
    kept = slots < capacity
    target = jnp.where(kept, flat * capacity + slots, experts * capacity)
    return (target, kept.astype(jnp.float32))


def prep_heads(cosine, sine, raw, gain):
    return rotate(norm_rows(raw, gain), cosine, sine)


def choose_gates(ids, logits):
    return jax.nn.softmax(jnp.take_along_axis(logits, ids, axis=1), axis=-1)


def contract_rows(left, right):
    return lax.dot_general(
        left, right, (((0,), (0,)), ((), ())), preferred_element_type=jnp.float32
    )


def times_transposed(left, right):
    return lax.dot_general(
        left, right, (((1,), (1,)), ((), ())), preferred_element_type=jnp.float32
    )


def move_slots(rows):
    return lax.all_to_all(rows, ("dp", "seq"), split_axis=0, concat_axis=0, tiled=True)


def body(
    layer_input,
    attn_gain,
    w_query,
    key_matrix,
    value_matrix,
    query_gain,
    key_gain,
    w_out,
    moe_gain,
    router,
    expert_gate,
    expert_up,
    expert_down,
    expert_ids,
    cont_segment,
    out_grad,
):
    shared = (attn_gain, key_matrix, value_matrix, w_out, moe_gain, router)
    gathered = (
        lax.all_gather(shared[0], ("dp", "seq"), axis=0, tiled=True),
        lax.all_gather(shared[1], ("dp", "seq"), axis=0, tiled=True),
        lax.all_gather(shared[2], ("dp", "seq"), axis=0, tiled=True),
        lax.all_gather(shared[3], ("dp", "seq"), axis=0, tiled=True),
        lax.all_gather(shared[4], ("dp", "seq"), axis=0, tiled=True),
        lax.all_gather(shared[5], ("dp", "seq"), axis=0, tiled=True),
    )
    attn_gain_all, key_all, value_all, out_all, moe_gain_all, router_all = gathered
    query_cols = lax.all_gather(w_query, "dp", axis=0, tiled=True)
    tokens_per_device = layer_input.shape[0]
    width = layer_input.shape[1]
    sequence_count = lax.axis_size("seq")
    devices = lax.axis_size(("dp", "seq"))
    heads_dev = HQ // sequence_count
    replica_count = sequence_count // KEY_VALUE_HEADS
    experts = router_all.shape[1]
    capacity = tokens_per_device * TOP // experts
    slot_count = experts * capacity
    local_experts = expert_gate.shape[0]
    head_width = query_gain.shape[0]
    factor = 1.0 / math.sqrt(head_width)
    where_at, labels = group_layout(cont_segment[0])
    group_length = labels.shape[0]
    blocks = group_length // QBLK
    own_at = lax.dynamic_slice_in_dim(
        where_at, lax.axis_index("seq") * tokens_per_device, tokens_per_device, 0
    )
    cosine, sine = angle_tables(own_at, head_width)
    query_gain_f = query_gain.astype(jnp.float32)
    key_gain_f = key_gain.astype(jnp.float32)
    inputs = layer_input.astype(jnp.float32)
    normalized_input, attn_norm_pull = jax.vjp(norm_rows, inputs, attn_gain_all.astype(jnp.float32))
    normed_low = normalized_input.astype(jnp.bfloat16)
    key_unrotated = jnp.dot(normed_low, key_all, preferred_element_type=jnp.float32).reshape(
        tokens_per_device, KEY_VALUE_HEADS, head_width
    )
    key_rot, key_pull = jax.vjp(partial(prep_heads, cosine, sine), key_unrotated, key_gain_f)
    query_all = lax.all_gather(query_cols, "seq", axis=1, tiled=True)
    query_raw = jnp.dot(normed_low, query_all, preferred_element_type=jnp.float32).reshape(
        tokens_per_device, HQ, head_width
    )
    query_rot, query_pull = jax.vjp(partial(prep_heads, cosine, sine), query_raw, query_gain_f)
    value_unprojected = jnp.dot(normed_low, value_all, preferred_element_type=jnp.float32).reshape(
        tokens_per_device, KEY_VALUE_HEADS, head_width
    )
    query_send = query_rot.astype(jnp.bfloat16)
    key_send = jnp.repeat(key_rot, replica_count, axis=1).astype(jnp.bfloat16)
    value_send = jnp.repeat(value_unprojected, replica_count, axis=1).astype(jnp.bfloat16)
    query_heads, key_heads, value_heads = (
        lax.all_to_all(query_send, "seq", split_axis=1, concat_axis=0, tiled=True),
        lax.all_to_all(key_send, "seq", split_axis=1, concat_axis=0, tiled=True),
        lax.all_to_all(value_send, "seq", split_axis=1, concat_axis=0, tiled=True),
    )
    key_rows = key_heads[:, 0]
    value_rows = value_heads[:, 0]

    def attend_block(index):
        start = index * QBLK
        query_block = lax.dynamic_slice_in_dim(query_heads, start, QBLK, 0)
        scores = (
            jnp.einsum("qhd,kd->hqk", query_block, key_rows, preferred_element_type=jnp.float32)
            * factor
        )
        scores = jnp.where(block_mask(labels, start, QBLK)[None], scores, -jnp.inf)
        peak = jnp.max(scores, axis=-1, keepdims=True)
        raised = jnp.exp(scores - peak)
        total = jnp.sum(raised, axis=-1, keepdims=True)
        probs = (raised / total).astype(jnp.bfloat16)
        mixed = jnp.einsum("hqk,kd->qhd", probs, value_rows, preferred_element_type=jnp.float32)
        return (mixed.astype(jnp.bfloat16), (peak + jnp.log(total))[..., 0])

    attended, log_totals = lax.map(attend_block, jnp.arange(blocks, dtype=jnp.int32))
    attended = attended.reshape(group_length, heads_dev, head_width)
    mixed_rows = lax.all_to_all(attended, "seq", split_axis=0, concat_axis=1, tiled=True)
    mixed_flat = mixed_rows.reshape(tokens_per_device, HQ * head_width)
    resid = inputs + jnp.dot(mixed_flat, out_all, preferred_element_type=jnp.float32)
    moe_normed, moe_norm_pull = jax.vjp(norm_rows, resid, moe_gain_all.astype(jnp.float32))
    moe_low = moe_normed.astype(jnp.bfloat16)
    logits = jnp.dot(moe_low, router_all, preferred_element_type=jnp.float32)
    gates, gate_pull = jax.vjp(partial(choose_gates, expert_ids), logits)
    target, kept = slot_plan(expert_ids, experts, capacity)
    filled = (
        jnp.zeros((slot_count + 1, width), jnp.bfloat16)
        .at[target]
        .set(jnp.repeat(moe_low, TOP, axis=0))
    )
    outgoing = filled[:slot_count].reshape(devices, local_experts * capacity, width)
    arrived = move_slots(outgoing).reshape(devices, local_experts, capacity, width)
    gate_pre = jnp.einsum(
        "sxcd,xdf->sxcf", arrived, expert_gate, preferred_element_type=jnp.float32
    )
    up_pre = jnp.einsum("sxcd,xdf->sxcf", arrived, expert_up, preferred_element_type=jnp.float32)
    sigma = jax.nn.sigmoid(gate_pre)
    swish = gate_pre * sigma
    hidden = (swish * up_pre).astype(jnp.bfloat16)
    produced = jnp.einsum(
        "sxcf,xfd->sxcd", hidden, expert_down, preferred_element_type=jnp.float32
    ).astype(jnp.bfloat16)
    returned = move_slots(produced.reshape(devices, local_experts * capacity, width))
    returned = jnp.concatenate(
        [returned.reshape(slot_count, width), jnp.zeros((1, width), jnp.bfloat16)], axis=0
    )
    pair_out = returned[target].astype(jnp.float32)
    pair_weight = gates.reshape(-1) * kept
    moe_out = jnp.sum(
        (pair_weight[:, None] * pair_out).reshape(tokens_per_device, TOP, width), axis=1
    )
    output = (resid + moe_out).astype(jnp.bfloat16)
    upstream = out_grad.astype(jnp.float32)
    pair_up = jnp.repeat(upstream, TOP, axis=0)
    weight_grad = jnp.sum(pair_out * pair_up, axis=1) * kept
    back_rows = (
        jnp.zeros((slot_count + 1, width), jnp.float32)
        .at[target]
        .set(pair_weight[:, None] * pair_up)
    )
    back_rows = (
        back_rows[:slot_count]
        .astype(jnp.bfloat16)
        .reshape(devices, local_experts * capacity, width)
    )
    produced_grad = move_slots(back_rows).reshape(devices, local_experts, capacity, width)
    down_weight_grad = jnp.einsum(
        "sxcf,sxcd->xfd", hidden, produced_grad, preferred_element_type=jnp.float32
    )
    hidden_grad = jnp.einsum(
        "sxcd,xfd->sxcf", produced_grad, expert_down, preferred_element_type=jnp.float32
    )
    gate_pre_grad = (hidden_grad * up_pre * sigma * (1.0 + gate_pre * (1.0 - sigma))).astype(
        jnp.bfloat16
    )
    up_pre_grad = (hidden_grad * swish).astype(jnp.bfloat16)
    gate_weight_grad = jnp.einsum(
        "sxcd,sxcf->xdf", arrived, gate_pre_grad, preferred_element_type=jnp.float32
    )
    up_weight_grad = jnp.einsum(
        "sxcd,sxcf->xdf", arrived, up_pre_grad, preferred_element_type=jnp.float32
    )
    arrived_grad = jnp.einsum(
        "sxcf,xdf->sxcd", gate_pre_grad, expert_gate, preferred_element_type=jnp.float32
    )
    arrived_grad = arrived_grad + jnp.einsum(
        "sxcf,xdf->sxcd", up_pre_grad, expert_up, preferred_element_type=jnp.float32
    )
    arrived_grad = arrived_grad.astype(jnp.bfloat16).reshape(
        devices, local_experts * capacity, width
    )
    rows_grad = move_slots(arrived_grad)
    rows_grad = jnp.concatenate(
        [rows_grad.reshape(slot_count, width), jnp.zeros((1, width), jnp.bfloat16)], axis=0
    )
    moe_low_grad = jnp.sum(
        rows_grad[target].astype(jnp.float32).reshape(tokens_per_device, TOP, width), axis=1
    )
    logit_grad = gate_pull(weight_grad.reshape(tokens_per_device, TOP))[0].astype(jnp.bfloat16)
    router_grad = contract_rows(moe_low, logit_grad)
    moe_low_grad = moe_low_grad + times_transposed(logit_grad, router_all)
    resid_part, moe_gain_grad = moe_norm_pull(moe_low_grad)
    resid_grad = upstream + resid_part
    resid_low = resid_grad.astype(jnp.bfloat16)
    out_weight_grad = contract_rows(mixed_flat, resid_low)
    mixed_grad = (
        times_transposed(resid_low, out_all)
        .astype(jnp.bfloat16)
        .reshape(tokens_per_device, HQ, head_width)
    )
    mixed_heads_grad = lax.all_to_all(mixed_grad, "seq", split_axis=1, concat_axis=0, tiled=True)

    def attend_back(carry, index):
        key_acc, value_acc = carry
        start = index * QBLK
        query_block = lax.dynamic_slice_in_dim(query_heads, start, QBLK, 0)
        grad_block = lax.dynamic_slice_in_dim(mixed_heads_grad, start, QBLK, 0)
        scores = (
            jnp.einsum("qhd,kd->hqk", query_block, key_rows, preferred_element_type=jnp.float32)
            * factor
        )
        scores = jnp.where(block_mask(labels, start, QBLK)[None], scores, -jnp.inf)
        probs = jnp.exp(scores - log_totals[index][..., None])
        value_acc = value_acc + jnp.einsum(
            "hqk,qhd->kd",
            probs.astype(jnp.bfloat16),
            grad_block,
            preferred_element_type=jnp.float32,
        )
        prob_grad = jnp.einsum(
            "qhd,kd->hqk", grad_block, value_rows, preferred_element_type=jnp.float32
        )
        centre = jnp.sum(probs * prob_grad, axis=-1, keepdims=True)
        score_grad = (probs * (prob_grad - centre)).astype(jnp.bfloat16)
        query_grad = (
            jnp.einsum("hqk,kd->qhd", score_grad, key_rows, preferred_element_type=jnp.float32)
            * factor
        )
        key_acc = (
            key_acc
            + jnp.einsum("hqk,qhd->kd", score_grad, query_block, preferred_element_type=jnp.float32)
            * factor
        )
        return ((key_acc, value_acc), query_grad.astype(jnp.bfloat16))

    zeros_rows = jnp.zeros((group_length, head_width), jnp.float32)
    totals_back, query_grads = lax.scan(
        attend_back, (zeros_rows, zeros_rows), jnp.arange(blocks, dtype=jnp.int32)
    )
    query_heads_grad = query_grads.reshape(group_length, heads_dev, head_width)
    key_slot_low = totals_back[0].astype(jnp.bfloat16)
    value_slot_low = totals_back[1].astype(jnp.bfloat16)
    query_back, key_backward, value_backward = (
        lax.all_to_all(query_heads_grad, "seq", split_axis=0, concat_axis=1, tiled=True),
        lax.all_to_all(key_slot_low[:, None, :], "seq", split_axis=0, concat_axis=1, tiled=True),
        lax.all_to_all(value_slot_low[:, None, :], "seq", split_axis=0, concat_axis=1, tiled=True),
    )
    key_total = jnp.sum(
        key_backward.astype(jnp.float32).reshape(
            tokens_per_device, KEY_VALUE_HEADS, replica_count, head_width
        ),
        axis=2,
    )
    value_total = jnp.sum(
        value_backward.astype(jnp.float32).reshape(
            tokens_per_device, KEY_VALUE_HEADS, replica_count, head_width
        ),
        axis=2,
    )
    query_raw_grad, query_gain_grad = query_pull(query_back.astype(jnp.float32))
    query_low = query_raw_grad.reshape(tokens_per_device, HQ * head_width).astype(jnp.bfloat16)
    query_block_grad = lax.psum_scatter(
        contract_rows(normed_low, query_low).astype(jnp.bfloat16),
        "seq",
        scatter_dimension=1,
        tiled=True,
    )
    normed_query_part = times_transposed(query_low, query_all)
    key_unrotated_grad, key_gain_grad = key_pull(key_total)
    key_reduced = key_unrotated_grad.reshape(
        tokens_per_device, KEY_VALUE_HEADS * head_width
    ).astype(jnp.bfloat16)
    value_reduced = value_total.reshape(tokens_per_device, KEY_VALUE_HEADS * head_width).astype(
        jnp.bfloat16
    )
    key_weight_grad = contract_rows(normed_low, key_reduced)
    value_weight_grad = contract_rows(normed_low, value_reduced)
    normed_grad = (
        normed_query_part
        + times_transposed(key_reduced, key_all)
        + times_transposed(value_reduced, value_all)
    )
    input_part, attn_gain_grad = attn_norm_pull(normed_grad)
    input_grad = resid_grad + input_part
    summed = (
        lax.psum_scatter(attn_gain_grad, ("dp", "seq"), scatter_dimension=0, tiled=True),
        lax.psum_scatter(key_weight_grad, ("dp", "seq"), scatter_dimension=0, tiled=True),
        lax.psum_scatter(value_weight_grad, ("dp", "seq"), scatter_dimension=0, tiled=True),
        lax.psum_scatter(out_weight_grad, ("dp", "seq"), scatter_dimension=0, tiled=True),
        lax.psum_scatter(moe_gain_grad, ("dp", "seq"), scatter_dimension=0, tiled=True),
        lax.psum_scatter(router_grad, ("dp", "seq"), scatter_dimension=0, tiled=True),
    )
    query_weight_grad = lax.psum_scatter(
        query_block_grad, "dp", scatter_dimension=0, tiled=True
    ).astype(jnp.float32)
    gain_sums = lax.psum((query_gain_grad, key_gain_grad), ("dp", "seq"))
    return (
        output,
        input_grad,
        summed[0],
        query_weight_grad,
        summed[1],
        summed[2],
        gain_sums[0],
        gain_sums[1],
        summed[3],
        summed[4],
        summed[5],
        gate_weight_grad,
        up_weight_grad,
        down_weight_grad,
    )


def solution(mesh):
    placed = (
        P(("dp", "seq"), None),
        P(("dp", "seq")),
        P("dp", "seq"),
        P(("dp", "seq"), None),
        P(("dp", "seq"), None),
        P(),
        P(),
        P(("dp", "seq"), None),
        P(("dp", "seq")),
        P(("dp", "seq"), None),
        P(("dp", "seq"), None, None),
        P(("dp", "seq"), None, None),
        P(("dp", "seq"), None, None),
        P(("dp", "seq"), None),
        P("dp", None),
        P(("dp", "seq"), None),
    )
    return jax.shard_map(
        body,
        mesh=mesh,
        in_specs=placed,
        out_specs=(
            P(("dp", "seq"), None),
            P(("dp", "seq"), None),
            P(("dp", "seq")),
            P("dp", "seq"),
            P(("dp", "seq"), None),
            P(("dp", "seq"), None),
            P(),
            P(),
            P(("dp", "seq"), None),
            P(("dp", "seq")),
            P(("dp", "seq"), None),
            P(("dp", "seq"), None, None),
            P(("dp", "seq"), None, None),
            P(("dp", "seq"), None, None),
        ),
        check_vma=False,
    )
```

profile of v0, /device:TPU:0, one launch (start us, length us, event | category | flops | bytes accessed | tf_op | source)
XLA Modules:
  0.0 2867.5 jit_solution(18439879757663951132)
XLA Ops:
  8.8 39.2 %all-gather.7.cloned.1.call-done = bf16[2048,512]{1,0:T(8,128)(2,1)} async-done(((bf16[512,512]{1,0:T(8,128)(2,1)}), bf16[2048,512]{1,0:T(8,128)(2,1)}) %all-gather.7.cloned.1.call-update) | async-done | bytes 2097168 | tf_op jit(solution)/shard_map/all_gather | solution.py:123
  54.1 39.5 %all-reduce.12 = (bf16[2048]{0:T(1024)(128)(2,1)S(1)}, bf16[2048]{0:T(1024)(128)(2,1)}) all-reduce(bf16[2048]{0:T(1024)(128)(2,1)S(1)} %dynamic-update-slice, bf16[2048]{0:T(1024)(128)(2,1)S(1)} %dynamic-update-slice.1), channel_id=1, replica_groups=mesh['dp'=4,'seq'=8] {'dp','seq'}, use_global_device_ids=true, to_apply=%add.7 | all-reduce | flops 4096 | bytes 16384
  94.3 13.2 all-gather.13.cloned.1.call-done
  115.2 152.3 %all-gather.9.cloned.1.call-done = bf16[2048,4096]{1,0:T(8,128)(2,1)} async-done(((bf16[2048,512]{1,0:T(8,128)(2,1)}), bf16[2048,4096]{1,0:T(8,128)(2,1)}) %all-gather.9.cloned.1.call-update) | async-done | bytes 16777232 | tf_op jit(solution)/shard_map/all_gather | solution.py:152
  294.5 35.4 %all-gather.11.cloned.1.call-done = bf16[2048,512]{1,0:T(8,128)(2,1)} async-done(((bf16[64,512]{1,0:T(8,128)(2,1)}), bf16[2048,512]{1,0:T(8,128)(2,1)}) %all-gather.11.cloned.1.call-update) | async-done | bytes 2097168 | tf_op jit(solution)/shard_map/all_gather | solution.py:116
  340.5 21.8 all-to-all-done
  371.7 26.6 all-to-all-done.1
  400.1 77.1 %while.27 = (s32[]{:T(128)}, bf16[4,512,4,128]{3,1,0,2:T(8,128)(2,1)}, f32[4,4,512]{2,1,0:T(4,128)}, s32[4]{0:T(128)S(1)}, s32[2048]{0:T(1024)S(1)}, /*index=5*/...) while((s32[]{:T(128)}, ...), condition=%wide.region_9.10_spmd, body=%wide.region_6.9_spmd.sunk | while | flops 2202272256 | bytes 56719560 | solution.py:186
  488.6 15.9 reduce-window.19
  507.0 28.7 %all-to-all-done.3 = bf16[2048,4,128]{2,1,0:T(4,128)(2,1)} async-done(((bf16[2048,4,128]{2,1,0:T(4,128)(2,1)}), bf16[2048,4,128]{2,1,0:T(4,128)(2,1)}, u32[]{:S(2)}, u32[]{:S(2)}) %all-to-all-start.3) | async-done | bytes 2097184 | tf_op jit(solution)/shard_map/all_to_all | solution.py:188
  556.6 17.5 scatter_custom_fusion
  586.5 213.7 %all-gather = bf16[32,64,32]{1,2,0:T(8,128)(2,1)S(1)} all-gather(bf16[1,64,32]{1,2,0:T(8,128)(2,1)S(1)} %bitcast.468), channel_id=1, replica_groups=mesh['dp'=4,'seq'=8] {'dp','seq'}, dimensions={0}, use_global_device_ids=true | all-gather | bytes 135168 | tf_op jit(solution)/shard_map/all_gather | solution.py:120
  806.7 16.8 gather_fusion.2
  824.0 19.7 scatter_custom_fusion.1
  868.4 173.2 %all-to-all-done.6 = bf16[32,64,2048]{2,1,0:T(8,128)(2,1)} async-done(((bf16[32,64,2048]{2,1,0:T(8,128)(2,1)}), bf16[32,64,2048]{2,1,0:T(8,128)(2,1)}, u32[]{:S(2)}, u32[]{:S(2)}) %all-to-all-start.6) | async-done | bytes 8388640 | tf_op jit(solution)/shard_map/all_to_all | solution.py:92
  1051.8 15.5 fusion.77
  1106.9 160.2 %all-to-all-done.5 = bf16[32,64,2048]{2,1,0:T(8,128)(2,1)} async-done(((bf16[32,64,2048]{2,1,0:T(8,128)(2,1)}), bf16[32,64,2048]{2,1,0:T(8,128)(2,1)}, u32[]{:S(2)}, u32[]{:S(2)}) %all-to-all-start.5) | async-done | bytes 8388640 | tf_op jit(solution)/shard_map/all_to_all | solution.py:92
  1279.7 21.0 gather_fusion
  1330.4 125.2 %all-to-all-done.7 = bf16[32,64,2048]{2,1,0:T(8,128)(2,1)} async-done(((bf16[32,64,2048]{2,1,0:T(8,128)(2,1)}), bf16[32,64,2048]{2,1,0:T(8,128)(2,1)}, u32[]{:S(2)}, u32[]{:S(2)}) %all-to-all-start.7) | async-done | bytes 8388640 | tf_op jit(solution)/shard_map/all_to_all | solution.py:92
  1463.9 21.2 gather_fusion.1
  1519.5 49.0 %all-to-all-done.8 = bf16[256,32,128]{2,0,1:T(8,128)(2,1)} async-done(((bf16[256,32,128]{2,0,1:T(8,128)(2,1)}), bf16[256,32,128]{2,0,1:T(8,128)(2,1)}, u32[]{:S(2)}, u32[]{:S(2)}) %all-to-all-start.8) | async-done | bytes 2097184 | tf_op jit(solution)/shard_map/all_to_all | solution.py:281
  1573.4 217.2 %while.28 = (s32[]{:T(128)}, f32[2048,128]{1,0:T(8,128)S(1)}, f32[2048,128]{1,0:T(8,128)}, bf16[4,512,4,128]{3,1,0,2:T(8,128)(2,1)}, s32[4]{0:T(128)S(1)}, /*ind...) while((s32[]{:T(128)}, f32[2048,128]{1,0:T(8,128)S(1)}, ...), condition=%wide.region_26.27_spmd.clone, body=%wide.region_24.26_spmd.clone.sunk | while | flops 5437653504 | bytes 213997904 | solution.py:317
  1794.1 51.5 %all_to_all.128 = bf16[2048,4,128]{2,1,0:T(4,128)(2,1)S(1)} all-to-all(bf16[2048,4,128]{2,1,0:T(4,128)(2,1)S(1)} %copy.346), channel_id=1, replica_groups=mesh['dp'=4,'seq'=8] {'seq'}, dimensions={0} | all-to-all | bytes 4194304 | tf_op jit(solution)/shard_map/all_to_all | solution.py:324
  1877.5 162.6 %reduce-scatter.9.cloned.1.call-done = bf16[2048,512]{1,0:T(8,128)(2,1)} async-done(((bf16[2048,4096]{1,0:T(8,128)(2,1)}), bf16[2048,512]{1,0:T(8,128)(2,1)}) %reduce-scatter.9.cloned.1.call-update) | async-done | bytes 2097168 | tf_op jit(solution)/shard_map/reduce_scatter | solution.py:342
  2044.0 19.2 all_to_all.129
  2073.7 19.0 all_to_all.130
  2098.8 14.7 fusion.104
  2148.0 28.9 %reduce-scatter.19.cloned.1.call-done = f32[64,32]{1,0:T(8,128)} async-done(((f32[2048,32]{1,0:T(8,128)}), f32[64,32]{1,0:T(8,128)}) %reduce-scatter.19.cloned.1.call-update) | async-done | bytes 8208
  2193.9 37.5 %all-reduce.11 = (f32[2048]{0:T(1024)S(1)}, f32[128]{0:T(128)}, f32[128]{0:T(128)}, f32[2048]{0:T(1024)S(1)}) all-reduce(f32[2048]{0:T(1024)S(1)} %get-tuple-element.161, f32[128]{0:T(128)S(1)} %get-tuple-element.157, f32[128]{0:T(128)S(1)} %get-tuple-element.163, ...), channel_id=2, replica_groups=mesh['dp'=4,'seq'=8] {'dp','seq'}, use_global_device_ids=true, to_apply=%region_33.34.clone | all-reduce | flops 4352 | bytes 34816
  2239.3 118.5 %reduce-scatter.13.cloned.1.call-done = f32[64,512]{1,0:T(8,128)} async-done(((f32[2048,512]{1,0:T(8,128)}), f32[64,512]{1,0:T(8,128)}) %reduce-scatter.13.cloned.1.call-update) | async-done | bytes 131088 | tf_op jit(solution)/shard_map/reduce_scatter | solution.py:367
  2357.8 142.1 %reduce-scatter.15.cloned.1.call-done = f32[64,512]{1,0:T(8,128)} async-done(((f32[2048,512]{1,0:T(8,128)}), f32[64,512]{1,0:T(8,128)}) %reduce-scatter.15.cloned.1.call-update) | async-done | bytes 131088 | tf_op jit(solution)/shard_map/reduce_scatter | solution.py:368
  2499.9 360.8 %reduce-scatter.17.cloned.1.call-done = f32[128,2048]{1,0:T(8,128)} async-done(((f32[4096,2048]{1,0:T(8,128)}), f32[128,2048]{1,0:T(8,128)}) %reduce-scatter.17.cloned.1.call-update) | async-done | bytes 1048592 | tf_op jit(solution)/shard_map/reduce_scatter | solution.py:369
  (440 shorter events, 677.7 us)
Async XLA Ops:
  7.2 1044.6 %copy-start = (bf16[1,2048,768]{2,1,0:T(8,128)(2,1)S(1)}, bf16[1,2048,768]{2,1,0:T(8,128)(2,1)}, u32[]{:S(2)}) copy-start(bf16[1,2048,768]{2,1,0:T(8,128)(2,1)} %param.30) | copy-start | bytes 9437188
  7.2 40.7 %all-gather.7.cloned.1.call-start = ((), (), s32[]{:S(2)}) async-start(), calls=%async_computation.18 | async-start | bytes 2621440 | tf_op jit(solution)/shard_map/all_gather | solution.py:123
  8.0 99.5 %all-gather.13.cloned.1.call-start = ((), (), s32[]{:S(2)}) async-start(), calls=%async_computation.21 | async-start | bytes 2162688 | tf_op jit(solution)/shard_map/all_gather | solution.py:117
  8.7 258.8 %all-gather.9.cloned.1.call-start = ((), (), s32[]{:S(2)}) async-start(), calls=%async_computation.19 | async-start | bytes 18874368 | tf_op jit(solution)/shard_map/all_gather | solution.py:152
  48.0 282.0 %all-gather.11.cloned.1.call-start = ((), (), s32[]{:S(2)}) async-start(), calls=%async_computation.20 | async-start | bytes 2162688 | tf_op jit(solution)/shard_map/all_gather | solution.py:116
  48.6 494.3 %all-gather.15.cloned.1.call-start = ((), (), s32[]{:S(2)}) async-start(), calls=%async_computation.22 | async-start | bytes 17301504 | tf_op jit(solution)/shard_map/all_gather | solution.py:118
  53.4 276.5 %copy-start.41 = (f32[256]{0:T(256)}, f32[256]{0:T(256)S(1)}, u32[]{:S(2)}) copy-start(f32[256]{0:T(256)S(1)} %fusion.123) | copy-start | bytes 3076
  93.5 236.4 %copy-start.29 = (f32[2048]{0:T(1024)}, f32[2048]{0:T(1024)S(1)}, u32[]{:S(2)}) copy-start(f32[2048]{0:T(1024)S(1)} %convert_element_type.210) | copy-start | bytes 24580
  94.3 244.1 %copy-start.19 = (f32[256,128]{1,0:T(8,128)}, f32[256,128]{1,0:T(8,128)S(1)}, u32[]{:S(2)}) copy-start(f32[256,128]{1,0:T(8,128)S(1)} %get-tuple-element.232) | copy-start | bytes 393220
  94.3 244.1 %copy-start.21 = (f32[256,128]{1,0:T(8,128)}, f32[256,128]{1,0:T(8,128)S(1)}, u32[]{:S(2)}) copy-start(f32[256,128]{1,0:T(8,128)S(1)} %get-tuple-element.233) | copy-start | bytes 393220
  111.1 178.9 %all-to-all-start.2 = ((bf16[256,8,128]{2,0,1:T(8,128)(2,1)}), bf16[256,8,128]{2,0,1:T(8,128)(2,1)}, u32[]{:S(2)}, u32[]{:S(2)}) async-start(bf16[256,8,128]{2,0,1:T(8,128)(2,1)} %bitcast.455), calls=%async_computation.2 | async-start | bytes 1048576 | tf_op jit(solution)/shard_map/all_to_all | solution.py:166
  290.0 72.4 %all-to-all-start = ((bf16[256,32,128]{2,0,1:T(8,128)(2,1)}), bf16[256,32,128]{2,0,1:T(8,128)(2,1)}, u32[]{:S(2)}, u32[]{:S(2)}) async-start(bf16[256,32,128]{2,0,1:T(8,128)(2,1)} %fusion.71), calls=%async_computation | async-start | bytes 4194304 | tf_op jit(solution)/shard_map/all_to_all | solution.py:164
  364.2 34.2 %all-to-all-start.1 = ((bf16[256,8,128]{2,0,1:T(8,128)(2,1)}), bf16[256,8,128]{2,0,1:T(8,128)(2,1)}, u32[]{:S(2)}, u32[]{:S(2)}) async-start(bf16[256,8,128]{2,0,1:T(8,128)(2,1)} %bitcast.456), calls=%async_computation.1 | async-start | bytes 1048576 | tf_op jit(solution)/shard_map/all_to_all | solution.py:165
  481.9 53.8 %all-to-all-start.3 = ((bf16[2048,4,128]{2,1,0:T(4,128)(2,1)}), bf16[2048,4,128]{2,1,0:T(4,128)(2,1)}, u32[]{:S(2)}, u32[]{:S(2)}) async-start(bf16[2048,4,128]{2,1,0:T(4,128)(2,1)} %copy.325), calls=%async_computation.3 | async-start | bytes 4194304 | tf_op jit(solution)/shard_map/all_to_all | solution.py:188
  487.0 67.0 %copy-start.36 = (f32[2048]{0:T(1024)}, f32[2048]{0:T(1024)S(1)}, u32[]{:S(2)}) copy-start(f32[2048]{0:T(1024)S(1)} %convert_element_type.224) | copy-start | bytes 24580
  582.4 270.4 %all-to-all-start.4 = ((bf16[32,64,2048]{2,1,0:T(8,128)(2,1)}), bf16[32,64,2048]{2,1,0:T(8,128)(2,1)}, u32[]{:S(2)}, u32[]{:S(2)}) async-start(bf16[32,64,2048]{2,1,0:T(8,128)(2,1)} %bitcast.436), calls=%async_computation.4 | async-start | bytes 16777216 | tf_op jit(solution)/shard_map/all_to_all | solution.py:92
  852.8 188.8 %all-to-all-start.6 = ((bf16[32,64,2048]{2,1,0:T(8,128)(2,1)}), bf16[32,64,2048]{2,1,0:T(8,128)(2,1)}, u32[]{:S(2)}, u32[]{:S(2)}) async-start(bf16[32,64,2048]{2,1,0:T(8,128)(2,1)} %bitcast.437), calls=%async_computation.6 | async-start | bytes 16777216 | tf_op jit(solution)/shard_map/all_to_all | solution.py:92
  1078.1 189.0 %all-to-all-start.5 = ((bf16[32,64,2048]{2,1,0:T(8,128)(2,1)}), bf16[32,64,2048]{2,1,0:T(8,128)(2,1)}, u32[]{:S(2)}, u32[]{:S(2)}) async-start(bf16[32,64,2048]{2,1,0:T(8,128)(2,1)} %convolution_convert_fusion.1), calls=%async_computation.5 | async-start | bytes 16777216 | tf_op jit(solution)/shard_map/all_to_all | solution.py:92
  1106.9 163.9 %copy-start.43 = (s32[256,8,1]{0,1,2:T(8,128)S(1)}, s32[256,8,1]{0,1,2:T(8,128)}, u32[]{:S(2)}) copy-start(s32[256,8,1]{0,1,2:T(8,128)} %get-tuple-element.234) | copy-start | bytes 24580
  1106.9 163.9 %copy-start.61 = (s32[2]{0:T(128)S(1)}, s32[2]{0:T(128)}, u32[]{:S(2)}) copy-start(s32[2]{0:T(128)} %constant.149) | copy-start | bytes 28
  1106.9 164.0 %copy-start.60 = (s32[2]{0:T(128)S(1)}, s32[2]{0:T(128)}, u32[]{:S(2)}) copy-start(s32[2]{0:T(128)} %constant.152) | copy-start | bytes 28
  1267.0 188.6 %all-to-all-start.7 = ((bf16[32,64,2048]{2,1,0:T(8,128)(2,1)}), bf16[32,64,2048]{2,1,0:T(8,128)(2,1)}, u32[]{:S(2)}, u32[]{:S(2)}) async-start(bf16[32,64,2048]{2,1,0:T(8,128)(2,1)} %add_convert_fusion), calls=%async_computation.7 | async-start | bytes 16777216 | tf_op jit(solution)/shard_map/all_to_all | solution.py:92
  1317.7 178.9 %copy-start.34 = (bf16[32,256]{1,0:T(8,128)(2,1)}, bf16[32,256]{1,0:T(8,128)(2,1)S(1)}, u32[]{:S(2)}) copy-start(bf16[32,256]{1,0:T(8,128)(2,1)S(1)} %reshape.648) | copy-start | bytes 49156
  1515.1 53.4 %all-to-all-start.8 = ((bf16[256,32,128]{2,0,1:T(8,128)(2,1)}), bf16[256,32,128]{2,0,1:T(8,128)(2,1)}, u32[]{:S(2)}, u32[]{:S(2)}) async-start(bf16[256,32,128]{2,0,1:T(8,128)(2,1)} %bitcast.384), calls=%async_computation.8 | async-start | bytes 4194304 | tf_op jit(solution)/shard_map/all_to_all | solution.py:281
  1519.5 54.0 %copy-start.17 = (s32[2048]{0:T(1024)S(1)}, s32[2048]{0:T(1024)}, u32[]{:S(2)}) copy-start(s32[2048]{0:T(1024)} %copy-done.16) | copy-start | bytes 24580
  1519.5 520.6 %reduce-scatter.9.cloned.1.call-start = ((), (), s32[]{:S(2)}) async-start(), calls=%async_computation.23 | async-start | bytes 18874368 | tf_op jit(solution)/shard_map/reduce_scatter | solution.py:342
  1874.7 302.2 %reduce-scatter.19.cloned.1.call-start = ((), (), s32[]{:S(2)}) async-start(), calls=%async_computation.28 | async-start | bytes 1081344
  1877.4 359.7 %reduce-scatter.11.cloned.1.call-start = ((), (), s32[]{:S(2)}) async-start(), calls=%async_computation.24 | async-start | bytes 2621440 | tf_op jit(solution)/shard_map/reduce_scatter | solution.py:373
  2040.1 317.6 %reduce-scatter.13.cloned.1.call-start = ((), (), s32[]{:S(2)}) async-start(), calls=%async_computation.25 | async-start | bytes 4325376 | tf_op jit(solution)/shard_map/reduce_scatter | solution.py:367
  2071.5 428.4 %reduce-scatter.15.cloned.1.call-start = ((), (), s32[]{:S(2)}) async-start(), calls=%async_computation.26 | async-start | bytes 4325376 | tf_op jit(solution)/shard_map/reduce_scatter | solution.py:368
  2097.2 763.5 %reduce-scatter.17.cloned.1.call-start = ((), (), s32[]{:S(2)}) async-start(), calls=%async_computation.27 | async-start | bytes 34603008 | tf_op jit(solution)/shard_map/reduce_scatter | solution.py:369
  2232.6 628.2 %copy-start.1 = (bf16[1,2048,768]{2,1,0:T(8,128)(2,1)S(1)}, bf16[1,2048,768]{2,1,0:T(8,128)(2,1)}, u32[]{:S(2)}) copy-start(bf16[1,2048,768]{2,1,0:T(8,128)(2,1)} %param.30) | copy-start | bytes 9437188
  (65 other events, 657.3 us)
Sparse Core Ops, SparseCore 0:
  9.9 38.0 all-gather.6
  50.9 56.4 all-gather.12
  109.1 158.4 all-gather.8
  270.4 59.5 all-gather.10
  332.8 128.3 all-gather.14
  1874.8 165.2 reduce-scatter.8
  2042.3 134.4 reduce-scatter.18
  2180.1 32.3 reduce-scatter.10
  2215.4 142.3 reduce-scatter.12
  2360.5 139.3 reduce-scatter.14
  2502.8 357.9 reduce-scatter.16
where the time goes:
time: 2880 us; the launch traced here: 2870 us
  waiting for transfers between devices  1640 us (57%)
  blocking collectives  380 us (13%)
  matrix products  365 us (13%)
  other arithmetic  212 us (7%)
  local copies, waits for them, and re-layouts  203 us (7%)
  starting transfers between devices  38.1 us (1%)
    all_to_all x4, waiting for transfers between devices, move_slots(): lax.all_to_all(rows, ('dp', 'seq'), split_axis=0, concat_axis=0, tiled=True)  459 us
    reduce_scatter x1, waiting for transfers between devices, body(): lax.psum_scatter(out_weight_grad, ('dp', 'seq'), scatter_dimension=0, til...  361 us
    all_gather x1, blocking collectives, body(): lax.all_gather(shared[5], ('dp', 'seq'), axis=0, tiled=True)  214 us
    reduce_scatter x1, waiting for transfers between devices, body(): lax.psum_scatter(contract_rows(normed_low, query_low).astype(jnp.bfloat16...  163 us
    all_gather x1, waiting for transfers between devices, body(): query_all = lax.all_gather(query_cols, 'seq', axis=1, tiled=True)  152 us
    reduce_scatter x1, waiting for transfers between devices, body(): lax.psum_scatter(value_weight_grad, ('dp', 'seq'), scatter_dimension=0, t...  142 us
    reduce_scatter x1, waiting for transfers between devices, body(): lax.psum_scatter(key_weight_grad, ('dp', 'seq'), scatter_dimension=0, til...  118 us
    unnamed x2, blocking collectives  77 us
  transfers between devices with their start and end apart: 20, of which 16 were waited for; matrix products, arithmetic and copies ran while one was open for 14% of the time, Pallas kernels for 0%

commit v1 on v0

v1 whole, which is shorter than its diff:
```python
from functools import partial
import math

import jax
import jax.numpy as jnp
from jax import lax
from jax.experimental import pallas as pl
from jax.experimental.pallas import tpu as pltpu
from jax.sharding import Mesh, PartitionSpec as P

HQ = 32
KEY_VALUE_HEADS = 4
TOP = 8
PROMPT = 1024
NCONT = 4
HEAD = 128

EPS = 1e-06
THETA = 1000000.0
LOG2E = 1.4426950408889634
BF = jnp.bfloat16
F32 = jnp.float32

STEPS = 4
ORDER = ((0, 1, 2, 3), (1, 0, 2, 3), (2, 3, 1, 0), (3, 2, 1, 0))
PLANE = ("dp", "core")
ALL = ("dp", "z", "core")


def norm_rows(value, gain):
    factor = lax.rsqrt(jnp.mean(value * value, axis=-1, keepdims=True) + EPS)
    return value * factor * gain


def rotate(value, cosine, sine):
    middle = value.shape[-1] // 2
    turned = jnp.concatenate([-value[..., middle:], value[..., :middle]], axis=-1)
    return value * cosine + turned * sine


def angle_tables(where_at, head_width):
    ranks = jnp.arange(head_width // 2, dtype=F32) * (2.0 / head_width)
    inverse = jnp.exp(-ranks * math.log(THETA))
    angles = where_at.astype(F32)[:, None] * inverse[None, :]
    angles = jnp.concatenate([angles, angles], axis=-1)
    return (jnp.cos(angles)[:, None, :], jnp.sin(angles)[:, None, :])


def group_layout(segment):
    length = segment.shape[0]
    one_hot = (segment[:, None] == jnp.arange(NCONT, dtype=jnp.int32)[None, :]).astype(jnp.int32)
    counted = jnp.sum(one_hot, axis=0)
    before = jnp.arange(NCONT)[:, None] > jnp.arange(NCONT)[None, :]
    starts = jnp.sum(jnp.where(before, counted[None, :], 0), axis=1)
    begins = jnp.sum(one_hot * starts[None, :], axis=1)
    within = jnp.arange(length, dtype=jnp.int32) - begins
    where_at = jnp.concatenate([jnp.arange(PROMPT, dtype=jnp.int32), PROMPT + within])
    opens = jnp.concatenate([jnp.full((PROMPT,), PROMPT, jnp.int32), PROMPT + begins])
    return (where_at, opens)


def prep_heads(cosine, sine, raw, gain):
    return rotate(norm_rows(raw, gain), cosine, sine)


def contract_rows(left, right):
    return lax.dot_general(left, right, (((0,), (0,)), ((), ())), preferred_element_type=F32)


def times_transposed(left, right):
    return lax.dot_general(left, right, (((1,), (1,)), ((), ())), preferred_element_type=F32)


def line_gather(block, z):
    up = lax.ppermute(block, "z", [(0, 1), (1, 2), (2, 3)])
    down = lax.ppermute(block, "z", [(1, 0), (2, 1), (3, 2)])
    up2 = lax.ppermute(up, "z", [(1, 2), (2, 3)])
    down2 = lax.ppermute(down, "z", [(1, 0), (2, 1)])
    last = lax.ppermute(jnp.where(z == 2, up2, down2), "z", [(2, 3), (1, 0)])
    first = jnp.where(z % 2 == 0, down, up)
    second = jnp.where(z == 0, down2, jnp.where(z == 1, down, jnp.where(z == 2, up, up2)))
    third = jnp.where(z == 1, down2, jnp.where(z == 2, up2, last))
    return [block, first, second, third]


def line_scatter(parts, z):
    def added(part, got):
        return (part.astype(F32) + got.astype(F32)).astype(BF)

    own, first, second, third = parts
    got = lax.ppermute(third, "z", [(0, 1), (3, 2)])
    middle = added(jnp.where((z == 0) | (z == 3), second, third), got)
    up = lax.ppermute(middle, "z", [(0, 1), (1, 2)])
    down = lax.ppermute(middle, "z", [(3, 2), (2, 1)])
    up = lax.ppermute(added(jnp.where(z == 1, second, first), up), "z", [(0, 1), (1, 2), (2, 3)])
    down = lax.ppermute(added(jnp.where(z == 2, second, first), down), "z", [(3, 2), (2, 1), (1, 0)])
    return own.astype(F32) + up.astype(F32) + down.astype(F32)


def other_cores(value):
    cores = lax.axis_size("core")
    return [
        lax.ppermute(value, "core", [((i + k) % cores, i) for i in range(cores)])
        for k in range(1, cores)
    ]


def cores_in_order(value, c):
    cores = lax.axis_size("core")
    pieces = jnp.stack([value, *other_cores(value)])
    return jnp.concatenate(
        [
            lax.dynamic_index_in_dim(pieces, (n - c) % cores, 0, keepdims=True)
            for n in range(cores)
        ]
    )


def sum_over_cores(pieces):
    cores = lax.axis_size("core")
    total = pieces[0].astype(F32)
    for k in range(1, cores):
        got = lax.ppermute(pieces[k], "core", [(i, (i + k) % cores) for i in range(cores)])
        total = total + got.astype(F32)
    return total


def _mask_bias(at_ref, opens_ref, bias_ref, low, high):
    rows = bias_ref.shape[0]
    key_at = low + lax.broadcasted_iota(jnp.int32, (rows, high - low), 1)
    query_at = at_ref[...]
    allowed = (key_at <= query_at) & ((key_at < PROMPT) | (key_at >= opens_ref[...]))
    bias_ref[:, low:high] = jnp.where(allowed, 0.0, -1e30).astype(F32)


def _spans(number, chunk):
    low = min(number * chunk, PROMPT)
    return (number + 1) * chunk, low


def _attend_kernel(order, q_ref, k_ref, v_ref, at_ref, opens_ref, o_ref, l_ref, bias_ref, *, chunk):
    number = order[pl.program_id(0)]
    for n in range(STEPS):

        @pl.when(number == n)
        def _(n=n):
            keys, masked = _spans(n, chunk)

            @pl.when(pl.program_id(1) == 0)
            def _():
                _mask_bias(at_ref, opens_ref, bias_ref, masked, keys)

            query = q_ref[...]
            scores = []
            for low in range(0, keys, chunk):
                s = times_transposed(query, k_ref[low : low + chunk, :])
                if low >= masked:
                    s = s + bias_ref[:, low : low + chunk]
                scores.append(s)
            peak = scores[0].max(axis=-1, keepdims=True)
            for s in scores[1:]:
                peak = jnp.maximum(peak, s.max(axis=-1, keepdims=True))
            total, out = None, None
            for j, s in enumerate(scores):
                p = jnp.exp2(s - peak)
                t = jnp.sum(p, axis=-1, keepdims=True)
                o = jnp.dot(
                    p.astype(BF), v_ref[j * chunk : (j + 1) * chunk, :], preferred_element_type=F32
                )
                total = t if total is None else total + t
                out = o if out is None else out + o
            o_ref[...] = (out / total).astype(BF)
            l_ref[0] = jnp.broadcast_to(peak + jnp.log2(total), l_ref.shape[1:])


def attend(order, queries, keys, values, query_at, opens, rows):
    tokens, width = queries.shape
    heads = width // HEAD
    group = keys.shape[0]
    chunk = group // STEPS
    full = pl.BlockSpec((group, HEAD), lambda i, h, o: (0, 0))
    column = pl.BlockSpec((rows, 1), lambda i, h, o: (i, 0))
    tile = pl.BlockSpec((rows, HEAD), lambda i, h, o: (i, h))
    scores = heads * rows * group * STEPS * 5 // 8
    return pl.pallas_call(
        partial(_attend_kernel, chunk=chunk),
        grid_spec=pltpu.PrefetchScalarGridSpec(
            num_scalar_prefetch=1,
            grid=(STEPS, heads),
            in_specs=[tile, full, full, column, column],
            out_specs=[tile, pl.BlockSpec((1, rows, HEAD), lambda i, h, o: (h, i, 0))],
            scratch_shapes=[pltpu.VMEM((rows, group), F32)],
        ),
        out_shape=[
            jax.ShapeDtypeStruct((tokens, width), BF),
            jax.ShapeDtypeStruct((heads, tokens, HEAD), F32),
        ],
        compiler_params=pltpu.CompilerParams(vmem_limit_bytes=40 * 1024 * 1024),
        cost_estimate=pl.CostEstimate(
            flops=4 * scores * HEAD, bytes_accessed=12 * tokens * width, transcendentals=scores
        ),
        name="attend",
    )(order, queries, keys, values, query_at, opens)


def _attend_back_kernel(
    order, q_ref, do_ref, o_ref, l_ref, k_ref, v_ref, at_ref, opens_ref,
    dq_ref, dk_ref, dv_ref, bias_ref, *, chunk,
):
    number = order[pl.program_id(0)]

    @pl.when((pl.program_id(0) == 0) & (pl.program_id(1) == 0))
    def _():
        dk_ref[...] = jnp.zeros_like(dk_ref)
        dv_ref[...] = jnp.zeros_like(dv_ref)

    for n in range(STEPS):

        @pl.when(number == n)
        def _(n=n):
            keys, masked = _spans(n, chunk)

            @pl.when(pl.program_id(1) == 0)
            def _():
                _mask_bias(at_ref, opens_ref, bias_ref, masked, keys)

            query, grad = q_ref[...], do_ref[...]
            centre = jnp.sum(
                grad.astype(F32) * o_ref[...].astype(F32), axis=-1, keepdims=True
            )
            log_total = l_ref[0][:, :1]
            dq = None
            for low in range(0, keys, chunk):
                span = slice(low, low + chunk)
                key = k_ref[span, :]
                s = times_transposed(query, key)
                if low >= masked:
                    s = s + bias_ref[:, span]
                p = jnp.exp2(s - log_total)
                dp = times_transposed(grad, v_ref[span, :])
                ds = (p * (dp - centre)).astype(BF)
                dv_ref[span, :] += contract_rows(p.astype(BF), grad)
                dk_ref[span, :] += contract_rows(ds, query)
                part = jnp.dot(ds, key, preferred_element_type=F32)
                dq = part if dq is None else dq + part
            dq_ref[...] = dq.astype(dq_ref.dtype)


def attend_back(order, queries, grads, mixed, log_totals, keys, values, query_at, opens, rows):
    tokens, width = queries.shape
    heads = width // HEAD
    group = keys.shape[0]
    chunk = group // STEPS
    full = pl.BlockSpec((group, HEAD), lambda i, h, o: (0, 0))
    column = pl.BlockSpec((rows, 1), lambda i, h, o: (i, 0))
    tile = pl.BlockSpec((rows, HEAD), lambda i, h, o: (i, h))
    scores = heads * rows * group * STEPS * 5 // 8
    return pl.pallas_call(
        partial(_attend_back_kernel, chunk=chunk),
        grid_spec=pltpu.PrefetchScalarGridSpec(
            num_scalar_prefetch=1,
            grid=(STEPS, heads),
            in_specs=[
                tile,
                tile,
                tile,
                pl.BlockSpec((1, rows, HEAD), lambda i, h, o: (h, i, 0)),
                full,
                full,
                column,
                column,
            ],
            out_specs=[tile, full, full],
            scratch_shapes=[pltpu.VMEM((rows, group), F32)],
        ),
        out_shape=[
            jax.ShapeDtypeStruct((tokens, width), F32),
            jax.ShapeDtypeStruct((group, HEAD), F32),
            jax.ShapeDtypeStruct((group, HEAD), F32),
        ],
        compiler_params=pltpu.CompilerParams(vmem_limit_bytes=40 * 1024 * 1024),
        cost_estimate=pl.CostEstimate(
            flops=10 * scores * HEAD, bytes_accessed=18 * tokens * width, transcendentals=scores
        ),
        name="attend_back",
    )(order, queries, grads, mixed, log_totals, keys, values, query_at, opens)


def _expert_kernel(x_ref, pulled_ref, weight_ref, gate_ref, up_ref, dx_ref, dg_ref, du_ref, h_ref, c_ref):
    rows = x_ref[...]
    gate = jnp.dot(rows, gate_ref[...], preferred_element_type=F32)
    up = jnp.dot(rows, up_ref[...], preferred_element_type=F32)
    weight = weight_ref[...]
    sigma = jax.nn.sigmoid(gate)
    swish = gate * sigma
    hidden = swish * up
    pulled = pulled_ref[...].astype(F32)
    c_ref[...] = jnp.sum(hidden * pulled, axis=-1, keepdims=True)
    h_ref[...] = (weight * hidden).astype(BF)
    pulled = weight * pulled
    gate_grad = (pulled * up * sigma * (1.0 + gate * (1.0 - sigma))).astype(BF)
    up_grad = (pulled * swish).astype(BF)
    dg_ref[...] = gate_grad
    du_ref[...] = up_grad
    dx = times_transposed(gate_grad, gate_ref[...]) + times_transposed(up_grad, up_ref[...])
    dx_ref[...] = dx.astype(BF)


def expert(rows, pulled, weight, gate, up):
    count, width = rows.shape
    hidden = gate.shape[1]
    step = min(count, 256)
    across = pl.BlockSpec((step, width), lambda i: (i, 0))
    thin = pl.BlockSpec((step, hidden), lambda i: (i, 0))
    column = pl.BlockSpec((step, 1), lambda i: (i, 0))
    full = pl.BlockSpec((width, hidden), lambda i: (0, 0))
    return pl.pallas_call(
        _expert_kernel,
        grid=(count // step,),
        in_specs=[across, thin, column, full, full],
        out_specs=[across, thin, thin, thin, column],
        out_shape=[
            jax.ShapeDtypeStruct((count, width), BF),
            jax.ShapeDtypeStruct((count, hidden), BF),
            jax.ShapeDtypeStruct((count, hidden), BF),
            jax.ShapeDtypeStruct((count, hidden), BF),
            jax.ShapeDtypeStruct((count, 1), F32),
        ],
        compiler_params=pltpu.CompilerParams(vmem_limit_bytes=48 * 1024 * 1024),
        cost_estimate=pl.CostEstimate(
            flops=8 * count * width * hidden,
            bytes_accessed=4 * count * width + 8 * count * hidden + 4 * width * hidden,
            transcendentals=count * hidden,
        ),
        name="expert",
    )(rows, pulled, weight, gate, up)


def _rows_kernel(*refs):
    count = (len(refs) - 1) // 2
    total = None
    for left, right in zip(refs[:count], refs[count:-1]):
        part = contract_rows(left[...], right[...])
        total = part if total is None else total + part
    refs[-1][...] = total


def contract_chunks(lefts, rights):
    count, tall = lefts[0].shape
    wide = rights[0].shape[1]
    step = min(tall, 256)
    return pl.pallas_call(
        _rows_kernel,
        grid=(tall // step,),
        in_specs=[pl.BlockSpec((count, step), lambda i: (0, i))] * len(lefts)
        + [pl.BlockSpec((count, wide), lambda i: (0, 0))] * len(rights),
        out_specs=pl.BlockSpec((step, wide), lambda i: (i, 0)),
        out_shape=jax.ShapeDtypeStruct((tall, wide), F32),
        compiler_params=pltpu.CompilerParams(vmem_limit_bytes=48 * 1024 * 1024),
        cost_estimate=pl.CostEstimate(
            flops=2 * len(lefts) * count * tall * wide,
            bytes_accessed=2 * len(lefts) * count * (tall + wide) + 4 * tall * wide,
            transcendentals=0,
        ),
        name="contract_chunks",
    )(*lefts, *rights)


def body(
    layer_input,
    attn_gain,
    w_query,
    key_matrix,
    value_matrix,
    query_gain,
    key_gain,
    w_out,
    moe_gain,
    router,
    expert_gate,
    expert_up,
    expert_down,
    expert_ids,
    cont_segment,
    out_grad,
):
    tokens, width = layer_input.shape
    sizes = [lax.axis_size(a) for a in ALL]
    dps, _, cores = sizes
    devices = math.prod(sizes)
    dp, z, c = [lax.axis_index(a) for a in ALL]
    experts = router.shape[1]
    capacity = tokens * TOP // experts
    plane = dps * cores
    slots = plane * capacity
    order = jnp.array(ORDER, jnp.int32)[z]
    where_block = jnp.array([[o.index(b) for b in range(STEPS)] for o in ORDER], jnp.int32)[z]
    own_heads = HQ // (STEPS * cores)
    heads = HQ // STEPS
    head_cols = heads * HEAD

    router_pad = -(experts + 2) % 128
    small = jnp.concatenate(
        [router, attn_gain[:, None], moe_gain[:, None], jnp.zeros((router.shape[0], router_pad), BF)],
        axis=1,
    )
    rows_dev = small.shape[0]
    packed = jnp.concatenate(
        [
            key_matrix.reshape(rows_dev, STEPS, HEAD).transpose(1, 0, 2),
            value_matrix.reshape(rows_dev, STEPS, HEAD).transpose(1, 0, 2),
            jnp.broadcast_to(small[None], (STEPS, *small.shape)),
        ],
        axis=2,
    )
    packed = lax.all_to_all(packed, "z", split_axis=0, concat_axis=0, tiled=True)
    packed = cores_in_order(packed, c).transpose(1, 0, 2, 3).reshape(w_query.shape[0], -1)
    gathered = lax.all_gather(jnp.concatenate([w_query, packed], axis=1), "dp", axis=0, tiled=True)
    own_cols = own_heads * HEAD
    query_own = gathered[:, :own_cols]
    key_value = gathered[:, own_cols : own_cols + 2 * HEAD]
    rest = gathered[:, own_cols + 2 * HEAD :]
    router_all = rest[:, :experts]
    attn_gain_all = rest[:, experts].astype(F32)
    moe_gain_all = rest[:, experts + 1].astype(F32)
    w_in = jnp.concatenate([query_own, *other_cores(query_own), key_value], axis=1)

    flat = [(b, (b % dps) * (devices // dps) + b // dps) for b in range(devices)]
    out_own = lax.all_gather(lax.ppermute(w_out, ALL, flat), "dp", axis=0, tiled=True)
    w_back = jnp.concatenate([out_own, *other_cores(out_own)], axis=0)

    where_at, opens = group_layout(cont_segment[0])
    group = where_at.shape[0]

    def own_rows(table):
        mine = lax.dynamic_index_in_dim(table.reshape(STEPS, cores, tokens), c, 1, keepdims=False)
        return jnp.concatenate(
            [lax.dynamic_index_in_dim(mine, order[i], 0, keepdims=False) for i in range(STEPS)]
        )

    cosine, sine = angle_tables(own_rows(where_at), HEAD)
    query_at = own_rows(jnp.arange(group, dtype=jnp.int32))[:, None]
    opens = own_rows(opens)[:, None]

    ids = lax.all_gather(expert_ids, "z", axis=0)
    ids = jnp.concatenate(
        [lax.dynamic_index_in_dim(ids, order[i], 0, keepdims=True) for i in range(STEPS)]
    )
    chosen = jnp.any(
        ids[:, :, :, None] == jnp.arange(experts, dtype=jnp.int32)[None, None, None, :], axis=2
    )
    earlier = jnp.arange(tokens)[:, None] > jnp.arange(tokens)[None, :]
    ranks = jnp.einsum(
        "ij,bje->bie", earlier.astype(BF), chosen.astype(BF), preferred_element_type=F32
    ).astype(jnp.int32)
    ranks = jnp.where(chosen & (ranks < capacity), ranks, -1)
    in_plane = lax.dynamic_index_in_dim(
        ranks.reshape(STEPS, tokens, dps, STEPS, cores), z, 3, keepdims=False
    ).reshape(STEPS, tokens, plane)
    at_slot = jnp.arange(capacity, dtype=jnp.int32)
    pick = (in_plane[:, :, :, None] == at_slot).reshape(STEPS, tokens, slots).astype(BF)
    own_chosen = chosen[0]
    own_ranks = ranks[0]
    own_pick = own_ranks[:, :, None] == at_slot

    def to_plane(rows):
        return lax.all_to_all(rows, PLANE, split_axis=0, concat_axis=0, tiled=True)

    def dispatch(i, rows):
        return to_plane(contract_rows(pick[i], rows).astype(BF))

    def combine(i, rows):
        return jnp.dot(pick[i], to_plane(rows), preferred_element_type=F32).astype(BF)

    arrived = jnp.concatenate(line_gather(layer_input, z))
    upstream_slots = [dispatch(i, g) for i, g in enumerate(line_gather(out_grad, z))]
    inputs = arrived.astype(F32)
    input_factor = lax.rsqrt(jnp.mean(inputs * inputs, axis=-1, keepdims=True) + EPS)
    normed = (inputs * input_factor * attn_gain_all).astype(BF)
    raw = jnp.dot(normed, w_in, preferred_element_type=F32)
    query_gain_f = query_gain.astype(F32)
    key_gain_f = key_gain.astype(F32)
    scale = LOG2E / math.sqrt(HEAD)
    query_rot, query_pull = jax.vjp(
        partial(prep_heads, cosine, sine), raw[:, :head_cols].reshape(-1, heads, HEAD), query_gain_f
    )
    key_rot, key_pull = jax.vjp(
        partial(prep_heads, cosine, sine),
        raw[:, head_cols : head_cols + HEAD].reshape(-1, 1, HEAD),
        key_gain_f,
    )
    queries = (query_rot * scale).astype(BF).reshape(-1, head_cols)
    key_value_rows = jnp.concatenate([key_rot[:, 0], raw[:, head_cols + HEAD :]], axis=1).astype(BF)
    spread = cores_in_order(key_value_rows, c).reshape(cores, STEPS, tokens, 2 * HEAD)
    spread = jnp.concatenate(
        [
            lax.dynamic_index_in_dim(spread, where_block[b], 1, keepdims=False).reshape(-1, 2 * HEAD)
            for b in range(STEPS)
        ]
    )
    keys, values = spread[:, :HEAD], spread[:, HEAD:]
    mixed, log_totals = attend(order, queries, keys, values, query_at, opens, tokens)
    attended = jnp.dot(mixed, w_back, preferred_element_type=F32).astype(BF)
    own_input = layer_input.astype(F32)
    resid = own_input + line_scatter(
        [attended[i * tokens : (i + 1) * tokens] for i in range(STEPS)], z
    )

    moe_normed, moe_norm_pull = jax.vjp(norm_rows, resid, moe_gain_all)
    moe_low = moe_normed.astype(BF)
    logits = jnp.dot(moe_low, router_all, preferred_element_type=F32)
    logits = jnp.where(own_chosen, logits, -jnp.inf)
    raised = jnp.exp(logits - jnp.max(logits, axis=-1, keepdims=True))
    gates = raised / jnp.sum(raised, axis=-1, keepdims=True)
    slot_gates = jnp.sum(jnp.where(own_pick, gates[:, :, None], 0.0), axis=0)
    slot_gates = lax.all_to_all(slot_gates, ALL, split_axis=0, concat_axis=0, tiled=True)
    slot_gates = slot_gates.reshape(dps, STEPS, cores, capacity)

    gate_w, up_w, down_w = expert_gate[0], expert_up[0], expert_down[0]
    pulled = [times_transposed(g, down_w) for g in upstream_slots]
    rows, outs = [], []
    for i, block in enumerate(line_gather(moe_low, z)):
        rows.append(dispatch(i, block))
        weight = lax.dynamic_index_in_dim(slot_gates, order[i], 1, keepdims=False).reshape(slots, 1)
        outs.append(expert(rows[i], pulled[i], weight, gate_w, up_w))
    slot_grads, gate_grads, up_grads, hiddens, centres = zip(*outs)

    stacked = jnp.stack([v.reshape(dps, cores, capacity) for v in centres])
    centre_back = jnp.stack(
        [
            lax.dynamic_index_in_dim(stacked, where_block[b], 0, keepdims=False)
            for b in range(STEPS)
        ],
        axis=1,
    ).reshape(experts, capacity)
    centre_back = lax.all_to_all(centre_back, ALL, split_axis=0, concat_axis=0, tiled=True)
    weight_grad = jnp.sum(jnp.where(own_pick, centre_back[None], 0.0), axis=2)
    slot_sum = line_scatter([combine(i, slot_grads[i]) for i in range(STEPS)], z)
    logit_grad = (
        gates * (weight_grad - jnp.sum(gates * weight_grad, axis=-1, keepdims=True))
    ).astype(BF)
    moe_low_grad = slot_sum + times_transposed(logit_grad, router_all)
    router_grad = contract_rows(moe_low, logit_grad)
    upstream = out_grad.astype(F32)
    resid_part, moe_gain_grad = moe_norm_pull(moe_low_grad)
    resid_grad = upstream + resid_part
    resid_low = resid_grad.astype(BF)

    down_weight_grad = contract_chunks(hiddens, upstream_slots)
    gate_weight_grad = contract_chunks(rows, gate_grads)
    up_weight_grad = contract_chunks(rows, up_grads)
    produced = [
        combine(i, jnp.dot(h, down_w, preferred_element_type=F32).astype(BF))
        for i, h in enumerate(hiddens)
    ]
    output = (resid + line_scatter(produced, z)).astype(BF)

    resid_all = jnp.concatenate(line_gather(resid_low, z))
    out_weight_grad = contract_rows(mixed, resid_all).astype(BF)
    rows_own = own_heads * HEAD
    out_weight_grad = sum_over_cores(
        [out_weight_grad[k * rows_own : (k + 1) * rows_own] for k in range(cores)]
    ).astype(BF)
    out_weight_grad = lax.psum_scatter(out_weight_grad, "dp", scatter_dimension=0, tiled=True)
    out_weight_grad = lax.ppermute(out_weight_grad, ALL, [(b, a) for a, b in flat]).astype(F32)
    mixed_grad = times_transposed(resid_all, w_back).astype(BF)
    query_grads, key_sum, value_sum = attend_back(
        order, queries, mixed_grad, mixed, log_totals, keys, values, query_at, opens, tokens
    )
    both = jnp.concatenate([key_sum * (1.0 / LOG2E), value_sum], axis=1)
    both = both.reshape(STEPS, cores, tokens, 2 * HEAD)
    both = jnp.stack(
        [lax.dynamic_index_in_dim(both, order[i], 0, keepdims=False) for i in range(STEPS)], axis=1
    )
    both = sum_over_cores(
        [
            lax.dynamic_index_in_dim(both, (c + k) % cores, 0, keepdims=False)
            for k in range(cores)
        ]
    ).reshape(-1, 2 * HEAD)
    query_raw_grad, query_gain_grad = query_pull(
        query_grads.reshape(-1, heads, HEAD) * (1.0 / math.sqrt(HEAD))
    )
    key_raw_grad, key_gain_grad = key_pull(both[:, None, :HEAD])
    raw_grad = jnp.concatenate(
        [query_raw_grad.reshape(-1, head_cols), key_raw_grad[:, 0], both[:, HEAD:]], axis=1
    ).astype(BF)
    normed_grad = times_transposed(raw_grad, w_in)
    attn_gain_grad = jnp.sum(normed_grad * inputs * input_factor, axis=0)
    normed_grad = normed_grad.astype(BF)
    normed_grad = line_scatter(
        [normed_grad[i * tokens : (i + 1) * tokens] for i in range(STEPS)], z
    )
    _, attn_norm_pull = jax.vjp(lambda v: norm_rows(v, attn_gain_all), own_input)
    input_grad = resid_grad + attn_norm_pull(normed_grad)[0]

    in_grad = contract_rows(normed, raw_grad).astype(BF)
    query_share = sum_over_cores(
        [in_grad[:, k * own_cols : (k + 1) * own_cols] for k in range(cores)]
    ).astype(BF)
    key_value_grad = in_grad[:, head_cols:].reshape(dps, STEPS, cores, rows_dev, 2 * HEAD)
    key_value_grad = sum_over_cores(
        [
            lax.dynamic_index_in_dim(key_value_grad, (c + k) % cores, 2, keepdims=False)
            for k in range(cores)
        ]
    )
    key_value_grad = key_value_grad.astype(BF).reshape(dps, -1, own_cols)
    share = jnp.concatenate(
        [query_share.reshape(dps, -1, own_cols), key_value_grad], axis=1
    ).reshape(-1, own_cols)
    share = lax.psum_scatter(share, "dp", scatter_dimension=0, tiled=True)
    query_rows = w_query.shape[0]
    query_weight_grad = share[:query_rows].astype(F32)
    key_value_grad = share[query_rows:].reshape(STEPS, rows_dev, 2 * HEAD)
    key_value_grad = lax.all_to_all(key_value_grad, "z", split_axis=0, concat_axis=0, tiled=True)
    key_value_grad = key_value_grad.transpose(1, 0, 2).astype(F32)
    key_weight_grad = key_value_grad[:, :, :HEAD].reshape(rows_dev, -1)
    value_weight_grad = key_value_grad[:, :, HEAD:].reshape(rows_dev, -1)

    small_grads = jnp.concatenate(
        [
            router_grad,
            attn_gain_grad[:, None],
            moe_gain_grad[:, None],
            jnp.zeros((width, router_pad), F32),
        ],
        axis=1,
    )
    small_grads = lax.psum_scatter(small_grads, ALL, scatter_dimension=0, tiled=True)
    gain_sums = lax.psum(jnp.stack([query_gain_grad, key_gain_grad]), ALL)
    return (
        output,
        input_grad,
        small_grads[:, experts],
        query_weight_grad,
        key_weight_grad,
        value_weight_grad,
        gain_sums[0],
        gain_sums[1],
        out_weight_grad,
        small_grads[:, experts + 1],
        small_grads[:, :experts],
        gate_weight_grad[None],
        up_weight_grad[None],
        down_weight_grad[None],
    )


def solution(mesh):
    dps, sequence = mesh.devices.shape
    inner = Mesh(mesh.devices.reshape(dps, STEPS, sequence // STEPS), ALL)
    rows = P(ALL, None)
    placed = (
        rows,
        P(ALL),
        P("dp", ("z", "core")),
        rows,
        rows,
        P(),
        P(),
        rows,
        P(ALL),
        rows,
        P(ALL, None, None),
        P(ALL, None, None),
        P(ALL, None, None),
        rows,
        P("dp", None),
        rows,
    )
    return jax.shard_map(
        body,
        mesh=inner,
        in_specs=placed,
        out_specs=(
            rows,
            rows,
            P(ALL),
            P("dp", ("z", "core")),
            rows,
            rows,
            P(),
            P(),
            rows,
            P(ALL),
            rows,
            P(ALL, None, None),
            P(ALL, None, None),
            P(ALL, None, None),
        ),
        check_vma=False,
    )
```

time: 2880 us -> 1230 us (0.43)
  waiting for transfers between devices: 1640 us -> 288 us
  blocking collectives: 380 us -> 137 us
  matrix products: 365 us -> 133 us
  starting transfers between devices: 38.1 us -> 222 us
  Pallas kernels: 0 us -> 162 us
  local copies, waits for them, and re-layouts: 203 us -> 105 us
  other arithmetic: 212 us -> 140 us
    reduce_scatter x5 -> x2, waiting for transfers between devices: 784 us -> 0.02 us  [the longest x1 0.02 us: body(): lax.psum_scatter(out_weight_grad, 'dp', scatter_dimension=0, tiled=True)]
    all_to_all x9 -> x19, waiting for transfers between devices: 585 us -> 53.9 us  [the longest x16 30.9 us: to_plane(): return lax.all_to_all(rows, PLANE, split_axis=0, concat_axis=0, tiled=True)]
    dot_general x42 -> x16, matrix products: 303 us -> 59.2 us  [the longest x8 28.8 us: combine(): jnp.dot(pick[i], to_plane(rows), preferred_element_type=F32).astype(BF)]
    all_gather x5 -> x2, waiting for transfers between devices: 240 us -> 0.02 us  [the longest x1 0.02 us: body(): lax.all_gather(lax.ppermute(w_out, ALL, flat), 'dp', axis=0, tiled=True)]
    ppermute x0 -> x50, waiting for transfers between devices: none -> 234 us  [the longest x4 75 us: line_gather(): down2 = lax.ppermute(down, 'z', [(1, 0), (2, 1)])]
    all_gather x1, blocking collectives: 214 us -> 36.3 us  [body(): ids = lax.all_gather(expert_ids, 'z', axis=0)]
    pallas_call x0 -> x9, Pallas kernels: none -> 162 us  [the longest x1 51.5 us: attend_back(): pl.pallas_call(partial(_attend_back_kernel, chunk=chunk), grid_spec=pltpu...]
    ppermute x0 -> x50, starting transfers between devices: none -> 125 us  [the longest x4 31.7 us: line_scatter(): lax.ppermute(added(jnp.where(z == 1, second, first), up), 'z', [(0, 1), (...]
  transfers between devices with their start and end apart: 20 -> 74, of which waited for: 16 -> 28; matrix products, arithmetic and copies ran while one was open for 14% -> 27% of each run, Pallas kernels for 0% -> 13%
where the time goes in v1:
time: 1230 us; the launch traced here: 1220 us
  waiting for transfers between devices  288 us (23%)
  starting transfers between devices  222 us (18%)
  Pallas kernels  162 us (13%)
  other arithmetic  140 us (11%)
  blocking collectives  137 us (11%)
  matrix products  133 us (11%)
  local copies, waits for them, and re-layouts  105 us (9%)
  between operations  32 us (3%)
    ppermute x4, waiting for transfers between devices, line_gather(): down2 = lax.ppermute(down, 'z', [(1, 0), (2, 1)])  75 us
    all_to_all x16, starting transfers between devices, to_plane(): return lax.all_to_all(rows, PLANE, split_axis=0, concat_axis=0, tiled=True)  70.1 us
    psum x1, blocking collectives, body(): gain_sums = lax.psum(jnp.stack([query_gain_grad, key_gain_grad]), ALL)  57 us
    unnamed x325, local copies, waits for them, and re-layouts  53.4 us
    pallas_call x1, Pallas kernels, attend_back(): pl.pallas_call(partial(_attend_back_kernel, chunk=chunk), grid_spec=pltpu...  51.5 us
    ppermute x4, waiting for transfers between devices, line_gather(): last = lax.ppermute(jnp.where(z == 2, up2, down2), 'z', [(2, 3), (1, 0)])  46.4 us
    pallas_call x4, Pallas kernels, expert(): pl.pallas_call(_expert_kernel, grid=(count // step,), in_specs=[across, t...  46.3 us
    all_to_all x1, blocking collectives, body(): lax.all_to_all(packed, 'z', split_axis=0, concat_axis=0, tiled=True)  43.6 us
  transfers between devices with their start and end apart: 74, of which 28 were waited for; matrix products, arithmetic and copies ran while one was open for 27% of the time, Pallas kernels for 13%

profile of v1, /device:TPU:0, one launch (start us, length us, event | category | flops | bytes accessed | tf_op | source)
XLA Modules:
  0.0 1217.9 jit_solution(10986859593668264545)
XLA Ops:
  17.3 43.6 %all_to_all.212 = bf16[4,64,384]{2,1,0:T(8,128)(2,1)S(1)} all-to-all(bf16[4,64,384]{2,1,0:T(8,128)(2,1)S(1)} %copy.160), channel_id=1, replica_groups=mesh['dp'=4,'z'=4,'core'=2] {'z'}, dimensions={0} | all-to-all | bytes 393216 | tf_op jit(solution)/shard_map/all_to_all | solution.py:416
  89.6 36.3 %all-gather = s32[1024,8]{0,1:T(8,128)S(1)} all-gather(s32[256,8]{0,1:T(8,128)S(1)} %copy-done.142), channel_id=2, replica_groups=mesh['dp'=4,'z'=4,'core'=2] {'z'}, dimensions={0}, use_global_device_ids=true | all-gather | bytes 40960 | tf_op jit(solution)/shard_map/all_gather | solution.py:445
  141.8 22.9 %collective-permute-done.2 = bf16[256,2048]{1,0:T(8,128)(2,1)} collective-permute-done((bf16[256,2048]{1,0:T(8,128)(2,1)}, bf16[256,2048]{1,0:T(8,128)(2,1)}, u32[]{:S(2)}, u32[]{:S(2)}) %collective-permute-start.2) | collective-permute-done | bytes 1048608 | tf_op jit(solution)/shard_map/ppermute | solution.py:78
  205.3 7.9 fusion.42
  246.4 27.4 %attend.1 = (bf16[1024,1024]{1,0:T(8,128)(2,1)S(1)}, f32[8,1024,128]{2,1,0:T(8,128)S(1)}) custom-call(s32[4]{0:T(128)S(1)} %get-tuple-element.156.order, bf16[1024,1024]{1,0:T(8,128)(2,1)S(1)} %fusion.9.q_ref, bf16[2048,128]{1,0:T(8,128)(2,1)S(1)} %get-tuple-element.105.k_ref, bf16[2048,128]{1,0:T(8,128)(2,1)S(1)} %get-tuple-element.104.v_ref, ...), custom_call_target="tpu_custom_call" | custom-call | flops 5368709120 | bytes 12582912 | tf_op jit(solution)/shard_map/attend/pallas_call | solution.py:185
  294.9 11.8 collective-permute-done.10
  342.7 10.7 collective-permute-start.12
  363.3 15.5 %collective-permute-done.14 = bf16[256,2048]{1,0:T(8,128)(2,1)} collective-permute-done((bf16[256,2048]{1,0:T(8,128)(2,1)}, bf16[256,2048]{1,0:T(8,128)(2,1)}, u32[]{:S(2)}, u32[]{:S(2)}) %collective-permute-start.14) | collective-permute-done | bytes 1048608 | tf_op jit(solution)/shard_map/ppermute | solution.py:96
  413.2 21.6 %collective-permute-done.15 = bf16[256,2048]{1,0:T(8,128)(2,1)S(1)} collective-permute-done((bf16[256,2048]{1,0:T(8,128)(2,1)}, bf16[256,2048]{1,0:T(8,128)(2,1)S(1)}, u32[]{:S(2)}, u32[]{:S(2)}) %collective-permute-start.15) | collective-permute-done | bytes 1048608 | tf_op jit(solution)/shard_map/ppermute | solution.py:76
  445.6 26.1 %collective-permute-done.16 = bf16[256,2048]{1,0:T(8,128)(2,1)S(1)} collective-permute-done((bf16[256,2048]{1,0:T(8,128)(2,1)}, bf16[256,2048]{1,0:T(8,128)(2,1)S(1)}, u32[]{:S(2)}, u32[]{:S(2)}) %collective-permute-start.16) | collective-permute-done | bytes 1048608 | tf_op jit(solution)/shard_map/ppermute | solution.py:78
  483.0 27.0 %collective-permute-done.23 = bf16[256,2048]{1,0:T(8,128)(2,1)S(1)} collective-permute-done((bf16[256,2048]{1,0:T(8,128)(2,1)S(1)}, bf16[256,2048]{1,0:T(8,128)(2,1)S(1)}, u32[]{:S(2)}, u32[]{:S(2)}) %collective-permute-start.23) | collective-permute-done | bytes 1048608 | tf_op jit(solution)/shard_map/ppermute | solution.py:79
  525.7 11.6 expert.6
  556.2 11.6 expert.7
  587.4 11.6 expert.5
  624.2 11.6 expert.4
  658.9 13.6 %collective-permute-done.31 = bf16[256,2048]{1,0:T(8,128)(2,1)} collective-permute-done((bf16[256,2048]{1,0:T(8,128)(2,1)}, bf16[256,2048]{1,0:T(8,128)(2,1)}, u32[]{:S(2)}, u32[]{:S(2)}) %collective-permute-start.31) | collective-permute-done | bytes 1048608 | tf_op jit(solution)/shard_map/ppermute | solution.py:93
  678.4 9.1 collective-permute-start.32
  695.9 15.5 %all-to-all-done.18 = f32[32,1,64]{2,1,0:T(1,128)S(1)} async-done(((f32[32,1,64]{2,1,0:T(1,128)}), f32[32,1,64]{2,1,0:T(1,128)S(1)}, u32[]{:S(2)}, u32[]{:S(2)}) %all-to-all-start.18) | async-done | bytes 8224 | tf_op jit(solution)/shard_map/all_to_all | solution.py:536
  724.4 20.9 %collective-permute-done.35 = bf16[256,2048]{1,0:T(8,128)(2,1)S(1)} collective-permute-done((bf16[256,2048]{1,0:T(8,128)(2,1)S(1)}, bf16[256,2048]{1,0:T(8,128)(2,1)S(1)}, u32[]{:S(2)}, u32[]{:S(2)}) %collective-permute-start.35) | collective-permute-done | bytes 1048608 | tf_op jit(solution)/shard_map/ppermute | solution.py:76
  747.4 23.9 %collective-permute-done.37 = bf16[256,2048]{1,0:T(8,128)(2,1)S(1)} collective-permute-done((bf16[256,2048]{1,0:T(8,128)(2,1)S(1)}, bf16[256,2048]{1,0:T(8,128)(2,1)S(1)}, u32[]{:S(2)}, u32[]{:S(2)}) %collective-permute-start.37) | collective-permute-done | bytes 1048608 | tf_op jit(solution)/shard_map/ppermute | solution.py:78
  786.0 13.0 %collective-permute-done.39 = bf16[256,2048]{1,0:T(8,128)(2,1)} collective-permute-done((bf16[256,2048]{1,0:T(8,128)(2,1)}, bf16[256,2048]{1,0:T(8,128)(2,1)}, u32[]{:S(2)}, u32[]{:S(2)}) %collective-permute-start.39) | collective-permute-done | bytes 1048608 | tf_op jit(solution)/shard_map/ppermute | solution.py:79
  801.8 7.4 convolution_convert_fusion.19.do_ref
  809.3 51.5 %attend_back.1 = (f32[1024,1024]{1,0:T(8,128)}, f32[2048,128]{1,0:T(8,128)S(1)}, f32[2048,128]{1,0:T(8,128)S(1)}) custom-call(s32[4]{0:T(128)S(1)} %get-tuple-element.156.order, bf16[1024,1024]{1,0:T(8,128)(2,1)S(1)} %copy-done.2, bf16[1024,1024]{1,0:T(8,128)(2,1)S(1)} %convolution_convert_fusion.19.do_ref, bf16[1024,1024]{1,0:T(8,128)(2,1)S(1)} %copy-done.49, ...), custom_call_target="tpu_custom_call" | custom-call | flops 13421772800 | bytes 18874368 | tf_op jit(solution)/shard_map/attend_back/pallas_call | solution.py:258
  912.2 9.1 fusion.4
  942.0 19.4 %all-to-all-done.10 = bf16[8,64,2048]{2,1,0:T(8,128)(2,1)} async-done(((bf16[8,64,2048]{2,1,0:T(8,128)(2,1)}), bf16[8,64,2048]{2,1,0:T(8,128)(2,1)}, u32[]{:S(2)}, u32[]{:S(2)}) %all-to-all-start.10) | async-done | bytes 2097184 | tf_op jit(solution)/shard_map/all_to_all | solution.py:467
  965.8 8.5 convolution_convert_fusion
  989.6 12.1 contract_chunks.5
  1041.5 12.2 %contract_chunks.3 = f32[2048,768]{1,0:T(8,128)} custom-call(bf16[512,2048]{1,0:T(8,128)(2,1)} %bitcast.50.x_ref.refs_0_, bf16[512,2048]{1,0:T(8,128)(2,1)} %bitcast.72.x_ref.refs_1_, bf16[512,2048]{1,0:T(8,128)(2,1)} %bitcast.65.x_ref.refs_2_, bf16[512,2048]{1,0:T(8,128)(2,1)} %bitcast.79.x_ref.refs_3_, bf16[512,768]{1,0:T(8,128)(2,1)S(1)} %copy-done.46, ...), custom_call_target="tpu_custom_call" | custom-call | flops 6442450944 | bytes 17825792 | tf_op jit(solution)/shard_map/contract_chunks/pallas_call | solution.py:352
  1065.1 12.2 %contract_chunks.4 = f32[2048,768]{1,0:T(8,128)} custom-call(bf16[512,2048]{1,0:T(8,128)(2,1)} %bitcast.50.x_ref.refs_0_, bf16[512,2048]{1,0:T(8,128)(2,1)} %bitcast.72.x_ref.refs_1_, bf16[512,2048]{1,0:T(8,128)(2,1)} %bitcast.65.x_ref.refs_2_, bf16[512,2048]{1,0:T(8,128)(2,1)} %bitcast.79.x_ref.refs_3_, bf16[512,768]{1,0:T(8,128)(2,1)S(1)} %copy-done.42, ...), custom_call_target="tpu_custom_call" | custom-call | flops 6442450944 | bytes 17825792 | tf_op jit(solution)/shard_map/contract_chunks/pallas_call | solution.py:352
  1089.8 11.2 collective-permute-done.26
  1111.9 57.0 %psum.7 = f32[2,128]{1,0:T(2,128)S(1)} all-reduce(f32[2,128]{1,0:T(2,128)S(1)} %pad_maximum_fusion.22), channel_id=1, replica_groups=mesh['dp'=4,'z'=4,'core'=2] {'dp','z','core'}, use_global_device_ids=true, to_apply=%region_24.25 | all-reduce | flops 256 | bytes 2048 | tf_op jit(solution)/shard_map/psum | solution.py:631
  1187.6 16.2 %all-to-all-start.19 = ((bf16[4,64,256]{2,1,0:T(8,128)(2,1)}), bf16[4,64,256]{2,1,0:T(8,128)(2,1)S(1)}, u32[]{:S(2)}, u32[]{:S(2)}) async-start(bf16[4,64,256]{2,1,0:T(8,128)(2,1)} %reshape.564), calls=%async_computation.20 | async-start | bytes 262144 | tf_op jit(solution)/shard_map/all_to_all | solution.py:616
  (658 shorter events, 576.1 us)
Async XLA Ops:
  7.2 164.9 %all-gather.6.cloned.1.call-start = ((), (), s32[]{:S(2)}) async-start(), calls=%async_computation.24 | async-start | bytes 2621440 | tf_op jit(solution)/shard_map/all_gather | solution.py:429
  12.9 162.3 %all-gather.4.cloned.1.call-start = ((), (), s32[]{:S(2)}) async-start(), calls=%async_computation.23 | async-start | bytes 4587520 | tf_op jit(solution)/shard_map/all_gather | solution.py:418
  66.8 69.9 %collective-permute-start = (bf16[256,2048]{1,0:T(8,128)(2,1)}, bf16[256,2048]{1,0:T(8,128)(2,1)}, u32[]{:S(2)}, u32[]{:S(2)}) collective-permute-start(bf16[256,2048]{1,0:T(8,128)(2,1)} %param.18), channel_id=1, source_target_pairs={{2,0},{4,2},{6,4},{3,1},{5,3},{7,5},{10,8},{12,10},{14,12},{11,9},... | collective-permute-start | bytes 3145736 | tf_op jit(solution)/shard_map/ppermute | solution.py:76
  68.1 69.9 %collective-permute-start.1 = (bf16[256,2048]{1,0:T(8,128)(2,1)}, bf16[256,2048]{1,0:T(8,128)(2,1)}, u32[]{:S(2)}, u32[]{:S(2)}) collective-permute-start(bf16[256,2048]{1,0:T(8,128)(2,1)} %param.18), channel_id=1, source_target_pairs={{0,2},{2,4},{4,6},{1,3},{3,5},{5,7},{8,10},{10,12},{12,14},{9,11},... | collective-permute-start | bytes 3145736 | tf_op jit(solution)/shard_map/ppermute | solution.py:75
  73.7 210.6 %collective-permute-start.19 = (bf16[256,2048]{1,0:T(8,128)(2,1)}, bf16[256,2048]{1,0:T(8,128)(2,1)}, u32[]{:S(2)}, u32[]{:S(2)}) collective-permute-start(bf16[256,2048]{1,0:T(8,128)(2,1)} %param.33), channel_id=1, source_target_pairs={{2,0},{4,2},{6,4},{3,1},{5,3},{7,5},{10,8},{12,10},{14,12},{11,9},... | collective-permute-start | bytes 3145736 | tf_op jit(solution)/shard_map/ppermute | solution.py:76
  75.0 209.3 %collective-permute-start.21 = (bf16[256,2048]{1,0:T(8,128)(2,1)}, bf16[256,2048]{1,0:T(8,128)(2,1)}, u32[]{:S(2)}, u32[]{:S(2)}) collective-permute-start(bf16[256,2048]{1,0:T(8,128)(2,1)} %param.33), channel_id=1, source_target_pairs={{0,2},{2,4},{4,6},{1,3},{3,5},{5,7},{8,10},{10,12},{12,14},{9,11},... | collective-permute-start | bytes 3145736 | tf_op jit(solution)/shard_map/ppermute | solution.py:75
  132.2 155.4 %all-to-all-start.2 = ((bf16[8,64,2048]{2,1,0:T(8,128)(2,1)}), bf16[8,64,2048]{2,1,0:T(8,128)(2,1)}, u32[]{:S(2)}, u32[]{:S(2)}) async-start(bf16[8,64,2048]{2,1,0:T(8,128)(2,1)} %bitcast.322), calls=%async_computation.2 | async-start | bytes 4194304 | tf_op jit(solution)/shard_map/all_to_all | solution.py:467
  323.2 35.8 %all-to-all-start.6 = ((bf16[8,64,2048]{2,1,0:T(8,128)(2,1)}), bf16[8,64,2048]{2,1,0:T(8,128)(2,1)}, u32[]{:S(2)}, u32[]{:S(2)}) async-start(bf16[8,64,2048]{2,1,0:T(8,128)(2,1)} %bitcast.316), calls=%async_computation.6 | async-start | bytes 4194304 | tf_op jit(solution)/shard_map/all_to_all | solution.py:467
  341.5 37.3 %collective-permute-start.14 = (bf16[256,2048]{1,0:T(8,128)(2,1)}, bf16[256,2048]{1,0:T(8,128)(2,1)}, u32[]{:S(2)}, u32[]{:S(2)}) collective-permute-start(bf16[256,2048]{1,0:T(8,128)(2,1)} %get-tuple-element.85), channel_id=1, source_target_pairs={{6,4},{4,2},{2,0},{7,5},{5,3},{3,1},{14,12},{12,10},{10,8},{15,13}... | collective-permute-start | bytes 3145736 | tf_op jit(solution)/shard_map/ppermute | solution.py:96
  342.7 36.0 %collective-permute-start.12 = (bf16[256,2048]{1,0:T(8,128)(2,1)}, bf16[256,2048]{1,0:T(8,128)(2,1)}, u32[]{:S(2)}, u32[]{:S(2)}) collective-permute-start(bf16[256,2048]{1,0:T(8,128)(2,1)} %get-tuple-element.84), channel_id=1, source_target_pairs={{0,2},{2,4},{4,6},{1,3},{3,5},{5,7},{8,10},{10,12},{12,14},{9,11},... | collective-permute-start | bytes 3145736 | tf_op jit(solution)/shard_map/ppermute | solution.py:95
  402.9 36.3 %all-to-all-start.1 = ((bf16[8,64,2048]{2,1,0:T(8,128)(2,1)}), bf16[8,64,2048]{2,1,0:T(8,128)(2,1)}, u32[]{:S(2)}, u32[]{:S(2)}) async-start(bf16[8,64,2048]{2,1,0:T(8,128)(2,1)} %bitcast.325), calls=%async_computation.1 | async-start | bytes 4194304 | tf_op jit(solution)/shard_map/all_to_all | solution.py:467
  439.2 36.6 %all-to-all-start.8 = ((bf16[8,64,2048]{2,1,0:T(8,128)(2,1)}), bf16[8,64,2048]{2,1,0:T(8,128)(2,1)}, u32[]{:S(2)}, u32[]{:S(2)}) async-start(bf16[8,64,2048]{2,1,0:T(8,128)(2,1)} %bitcast.324), calls=%async_computation.8 | async-start | bytes 4194304 | tf_op jit(solution)/shard_map/all_to_all | solution.py:467
  475.8 36.3 %all-to-all-start.5 = ((bf16[8,64,2048]{2,1,0:T(8,128)(2,1)}), bf16[8,64,2048]{2,1,0:T(8,128)(2,1)}, u32[]{:S(2)}, u32[]{:S(2)}) async-start(bf16[8,64,2048]{2,1,0:T(8,128)(2,1)} %bitcast.319), calls=%async_computation.5 | async-start | bytes 4194304 | tf_op jit(solution)/shard_map/all_to_all | solution.py:467
  639.2 48.2 %all-to-all-start.14 = ((bf16[8,64,2048]{2,1,0:T(8,128)(2,1)}), bf16[8,64,2048]{2,1,0:T(8,128)(2,1)}, u32[]{:S(2)}, u32[]{:S(2)}) async-start(bf16[8,64,2048]{2,1,0:T(8,128)(2,1)} %bitcast.353), calls=%async_computation.14 | async-start | bytes 4194304 | tf_op jit(solution)/shard_map/all_to_all | solution.py:467
  677.0 36.7 %collective-permute-start.34 = (bf16[256,2048]{1,0:T(8,128)(2,1)}, bf16[256,2048]{1,0:T(8,128)(2,1)}, u32[]{:S(2)}, u32[]{:S(2)}) collective-permute-start(bf16[256,2048]{1,0:T(8,128)(2,1)} %get-tuple-element.98), channel_id=1, source_target_pairs={{6,4},{4,2},{2,0},{7,5},{5,3},{3,1},{14,12},{12,10},{10,8},{15,13}... | collective-permute-start | bytes 3145736 | tf_op jit(solution)/shard_map/ppermute | solution.py:96
  779.9 149.4 %all-to-all-start.4 = ((bf16[8,64,2048]{2,1,0:T(8,128)(2,1)}), bf16[8,64,2048]{2,1,0:T(8,128)(2,1)}, u32[]{:S(2)}, u32[]{:S(2)}) async-start(bf16[8,64,2048]{2,1,0:T(8,128)(2,1)} %bitcast.352), calls=%async_computation.4 | async-start | bytes 4194304 | tf_op jit(solution)/shard_map/all_to_all | solution.py:467
  784.2 385.2 %reduce-scatter.10.cloned.1.call-start = ((), (), s32[]{:S(2)}) async-start(), calls=%async_computation.27 | async-start | bytes 1081344
  871.7 66.4 %collective-permute-start.48 = (bf16[512,2048]{1,0:T(8,128)(2,1)}, bf16[512,2048]{1,0:T(8,128)(2,1)}, u32[]{:S(2)}, u32[]{:S(2)}) collective-permute-start(bf16[512,2048]{1,0:T(8,128)(2,1)} %slice.300), channel_id=1, source_target_pairs={{0,1},{1,0},{2,3},{3,2},{4,5},{5,4},{6,7},{7,6},{8,9},{9,8},{10,11... | collective-permute-start | bytes 6291464 | tf_op jit(solution)/shard_map/ppermute | solution.py:123
  933.7 242.3 %reduce-scatter.8.cloned.1.call-start = ((), (), s32[]{:S(2)}) async-start(), calls=%async_computation.26 | async-start | bytes 2621440 | tf_op jit(solution)/shard_map/reduce_scatter | solution.py:564
  961.4 45.1 %all-to-all-start.13 = ((bf16[8,64,2048]{2,1,0:T(8,128)(2,1)}), bf16[8,64,2048]{2,1,0:T(8,128)(2,1)}, u32[]{:S(2)}, u32[]{:S(2)}) async-start(bf16[8,64,2048]{2,1,0:T(8,128)(2,1)} %bitcast.357), calls=%async_computation.13 | async-start | bytes 4194304 | tf_op jit(solution)/shard_map/all_to_all | solution.py:467
  976.0 44.7 %collective-permute-start.46 = (bf16[2048,512]{1,0:T(8,128)(2,1)}, bf16[2048,512]{1,0:T(8,128)(2,1)}, u32[]{:S(2)}, u32[]{:S(2)}) collective-permute-start(bf16[2048,512]{1,0:T(8,128)(2,1)} %slice.293), channel_id=1, source_target_pairs={{0,1},{1,0},{2,3},{3,2},{4,5},{5,4},{6,7},{7,6},{8,9},{9,8},{10,11... | collective-permute-start | bytes 6291464 | tf_op jit(solution)/shard_map/ppermute | solution.py:123
  1006.5 47.2 %all-to-all-start.7 = ((bf16[8,64,2048]{2,1,0:T(8,128)(2,1)}), bf16[8,64,2048]{2,1,0:T(8,128)(2,1)}, u32[]{:S(2)}, u32[]{:S(2)}) async-start(bf16[8,64,2048]{2,1,0:T(8,128)(2,1)} %bitcast.354), calls=%async_computation.7 | async-start | bytes 4194304 | tf_op jit(solution)/shard_map/all_to_all | solution.py:467
  1010.8 175.2 %reduce-scatter.6.cloned.1.call-start = ((), (), s32[]{:S(2)}) async-start(), calls=%async_computation.25 | async-start | bytes 3276800 | tf_op jit(solution)/shard_map/reduce_scatter | solution.py:612
  1014.3 41.3 %collective-permute-start.25 = (bf16[256,2048]{1,0:T(8,128)(2,1)}, bf16[256,2048]{1,0:T(8,128)(2,1)}, u32[]{:S(2)}, u32[]{:S(2)}) collective-permute-start(bf16[256,2048]{1,0:T(8,128)(2,1)} %convolution_convert_fusion.15), channel_id=1, source_target_pairs={{0,2},{6,4},{1,3},{7,5},{8,10},{14,12},{9,11},{15,13},{16,18},{22,... | collective-permute-start | bytes 3145736 | tf_op jit(solution)/shard_map/ppermute | solution.py:91
  1034.5 44.2 %collective-permute-start.42 = (bf16[256,2048]{1,0:T(8,128)(2,1)}, bf16[256,2048]{1,0:T(8,128)(2,1)}, u32[]{:S(2)}, u32[]{:S(2)}) collective-permute-start(bf16[256,2048]{1,0:T(8,128)(2,1)} %add_convert_fusion.4), channel_id=1, source_target_pairs={{0,2},{2,4},{1,3},{3,5},{8,10},{10,12},{9,11},{11,13},{16,18},{18,... | collective-permute-start | bytes 3145736 | tf_op jit(solution)/shard_map/ppermute | solution.py:93
  1039.8 38.8 %collective-permute-start.44 = (bf16[256,2048]{1,0:T(8,128)(2,1)}, bf16[256,2048]{1,0:T(8,128)(2,1)}, u32[]{:S(2)}, u32[]{:S(2)}) collective-permute-start(bf16[256,2048]{1,0:T(8,128)(2,1)} %add_convert_fusion.4), channel_id=1, source_target_pairs={{6,4},{4,2},{7,5},{5,3},{14,12},{12,10},{15,13},{13,11},{22,20},{2... | collective-permute-start | bytes 3145736 | tf_op jit(solution)/shard_map/ppermute | solution.py:94
  1058.6 42.4 %collective-permute-start.26 = (bf16[256,2048]{1,0:T(8,128)(2,1)S(1)}, bf16[256,2048]{1,0:T(8,128)(2,1)S(1)}, u32[]{:S(2)}, u32[]{:S(2)}) collective-permute-start(bf16[256,2048]{1,0:T(8,128)(2,1)S(1)} %get-tuple-element.174), channel_id=1, source_target_pairs={{0,2},{2,4},{1,3},{3,5},{8,10},{10,12},{9,11},{11,13},{16,18},{18,... | collective-permute-start | bytes 3145736 | tf_op jit(solution)/shard_map/ppermute | solution.py:93
  1063.3 37.7 %collective-permute-start.28 = (bf16[256,2048]{1,0:T(8,128)(2,1)S(1)}, bf16[256,2048]{1,0:T(8,128)(2,1)}, u32[]{:S(2)}, u32[]{:S(2)}) collective-permute-start(bf16[256,2048]{1,0:T(8,128)(2,1)S(1)} %get-tuple-element.174), channel_id=1, source_target_pairs={{6,4},{4,2},{7,5},{5,3},{14,12},{12,10},{15,13},{13,11},{22,20},{2... | collective-permute-start | bytes 3145736 | tf_op jit(solution)/shard_map/ppermute | solution.py:94
  1082.6 90.3 %collective-permute-start.45 = (bf16[256,2048]{1,0:T(8,128)(2,1)}, bf16[256,2048]{1,0:T(8,128)(2,1)}, u32[]{:S(2)}, u32[]{:S(2)}) collective-permute-start(bf16[256,2048]{1,0:T(8,128)(2,1)} %get-tuple-element.81), channel_id=1, source_target_pairs={{6,4},{4,2},{2,0},{7,5},{5,3},{3,1},{14,12},{12,10},{10,8},{15,13}... | collective-permute-start | bytes 3145736 | tf_op jit(solution)/shard_map/ppermute | solution.py:96
  1083.9 89.1 %collective-permute-start.43 = (bf16[256,2048]{1,0:T(8,128)(2,1)}, bf16[256,2048]{1,0:T(8,128)(2,1)}, u32[]{:S(2)}, u32[]{:S(2)}) collective-permute-start(bf16[256,2048]{1,0:T(8,128)(2,1)} %get-tuple-element.80), channel_id=1, source_target_pairs={{0,2},{2,4},{4,6},{1,3},{3,5},{5,7},{8,10},{10,12},{12,14},{9,11},... | collective-permute-start | bytes 3145736 | tf_op jit(solution)/shard_map/ppermute | solution.py:95
  1104.4 73.3 %collective-permute-start.29 = (bf16[256,2048]{1,0:T(8,128)(2,1)}, bf16[256,2048]{1,0:T(8,128)(2,1)}, u32[]{:S(2)}, u32[]{:S(2)}) collective-permute-start(bf16[256,2048]{1,0:T(8,128)(2,1)} %get-tuple-element.100), channel_id=1, source_target_pairs={{6,4},{4,2},{2,0},{7,5},{5,3},{3,1},{14,12},{12,10},{10,8},{15,13}... | collective-permute-start | bytes 3145736 | tf_op jit(solution)/shard_map/ppermute | solution.py:96
  1105.9 71.9 %collective-permute-start.27 = (bf16[256,2048]{1,0:T(8,128)(2,1)}, bf16[256,2048]{1,0:T(8,128)(2,1)}, u32[]{:S(2)}, u32[]{:S(2)}) collective-permute-start(bf16[256,2048]{1,0:T(8,128)(2,1)} %get-tuple-element.99), channel_id=1, source_target_pairs={{0,2},{2,4},{4,6},{1,3},{3,5},{5,7},{8,10},{10,12},{12,14},{9,11},... | collective-permute-start | bytes 3145736 | tf_op jit(solution)/shard_map/ppermute | solution.py:95
  (197 other events, 4370.5 us)
Sparse Core Ops, SparseCore 0:
  13.0 70.3 all-gather.5
  85.9 48.3 all-gather.3
  925.2 140.6 reduce-scatter.9
  1069.0 31.4 reduce-scatter.7
  1103.3 40.0 reduce-scatter.5

commit v2 on v1

v2 whole, which is shorter than its diff:
```python
from functools import partial
import math

import jax
import jax.numpy as jnp
from jax import lax
from jax.experimental import pallas as pl
from jax.experimental.pallas import tpu as pltpu
from jax.sharding import Mesh, PartitionSpec as P

HQ = 32
KEY_VALUE_HEADS = 4
TOP = 8
PROMPT = 1024
NCONT = 4
HEAD = 128

EPS = 1e-06
THETA = 1000000.0
LOG2E = 1.4426950408889634
BF = jnp.bfloat16
F32 = jnp.float32

STEPS = 4
ORDER = ((0, 1, 2, 3), (1, 0, 2, 3), (2, 3, 1, 0), (3, 2, 1, 0))
PLANE = ("dp", "core")
ALL = ("dp", "z", "core")


def angle_tables(where_at, head_width):
    ranks = jnp.arange(head_width // 2, dtype=F32) * (2.0 / head_width)
    inverse = jnp.exp(-ranks * math.log(THETA))
    angles = where_at.astype(F32)[:, None] * inverse[None, :]
    cosine, sine = jnp.cos(angles), jnp.sin(angles)
    return (
        jnp.concatenate([cosine, cosine], axis=-1),
        jnp.concatenate([-sine, sine], axis=-1),
    )


def group_layout(segment):
    length = segment.shape[0]
    one_hot = (segment[:, None] == jnp.arange(NCONT, dtype=jnp.int32)[None, :]).astype(jnp.int32)
    counted = jnp.sum(one_hot, axis=0)
    before = jnp.arange(NCONT)[:, None] > jnp.arange(NCONT)[None, :]
    starts = jnp.sum(jnp.where(before, counted[None, :], 0), axis=1)
    begins = jnp.sum(one_hot * starts[None, :], axis=1)
    within = jnp.arange(length, dtype=jnp.int32) - begins
    where_at = jnp.concatenate([jnp.arange(PROMPT, dtype=jnp.int32), PROMPT + within])
    opens = jnp.concatenate([jnp.full((PROMPT,), PROMPT, jnp.int32), PROMPT + begins])
    return (where_at, opens)


def contract_rows(left, right):
    return lax.dot_general(left, right, (((0,), (0,)), ((), ())), preferred_element_type=F32)


def times_transposed(left, right):
    return lax.dot_general(left, right, (((1,), (1,)), ((), ())), preferred_element_type=F32)


def hold(*values):
    return lax.optimization_barrier(values)


def spread_first(block):
    return (
        lax.ppermute(block, "z", [(0, 1), (1, 2), (2, 3)]),
        lax.ppermute(block, "z", [(1, 0), (2, 1), (3, 2)]),
    )


def spread_second(up, down):
    return (
        lax.ppermute(up, "z", [(1, 2), (2, 3)]),
        lax.ppermute(down, "z", [(2, 1), (1, 0)]),
    )


def spread_third(up2, down2, z):
    return lax.ppermute(jnp.where(z == 2, up2, down2), "z", [(2, 3), (1, 0)])


FIRST = (1, 0, 1, 0)
SECOND = (3, 1, 0, 2)
THIRD = (2, 1, 0, 2)


def sum_first(third):
    return lax.ppermute(third, "z", [(0, 1), (3, 2)])


def sum_second(middle):
    return (
        lax.ppermute(middle, "z", [(0, 1), (1, 2)]),
        lax.ppermute(middle, "z", [(3, 2), (2, 1)]),
    )


def sum_third(up, down):
    return (
        lax.ppermute(up, "z", [(0, 1), (1, 2), (2, 3)]),
        lax.ppermute(down, "z", [(3, 2), (2, 1), (1, 0)]),
    )


def over_dps(value, dp):
    dps = value.shape[0]
    total = lax.dynamic_index_in_dim(value, dp, 0, keepdims=False).astype(F32)
    for k in range(1, dps):
        piece = lax.dynamic_index_in_dim(value, dp ^ k, 0, keepdims=False)
        total = total + lax.ppermute(piece, "dp", [(i, i ^ k) for i in range(dps)]).astype(F32)
    return total


def from_dps(value, dp):
    dps = lax.axis_size("dp")
    whole = jnp.zeros((dps, *value.shape), value.dtype)
    whole = lax.dynamic_update_index_in_dim(whole, value, dp, 0)
    for k in range(1, dps):
        got = lax.ppermute(value, "dp", [(i, i ^ k) for i in range(dps)])
        whole = lax.dynamic_update_index_in_dim(whole, got, dp ^ k, 0)
    return whole


def other_cores(value):
    cores = lax.axis_size("core")
    return [
        lax.ppermute(value, "core", [((i + k) % cores, i) for i in range(cores)])
        for k in range(1, cores)
    ]


def cores_in_order(value, c):
    cores = lax.axis_size("core")
    pieces = [value, *other_cores(value)]
    ordered = []
    for n in range(cores):
        piece = pieces[0]
        for k in range(1, cores):
            piece = jnp.where((n - c) % cores == k, pieces[k], piece)
        ordered.append(piece)
    return ordered


def sum_over_cores(pieces):
    cores = lax.axis_size("core")
    total = pieces[0].astype(F32)
    for k in range(1, cores):
        got = lax.ppermute(pieces[k], "core", [(i, (i + k) % cores) for i in range(cores)])
        total = total + got.astype(F32)
    return total


CHEAP = pl.CostEstimate(flops=1, bytes_accessed=1, transcendentals=0)


def run(kernel, name, grid, operands, in_specs, outs, out_specs, scalars=None, scratch=(), aliases=None):
    prefetch = () if scalars is None else (scalars,)
    aliases = {i + len(prefetch): o for i, o in (aliases or {}).items()}
    got = pl.pallas_call(
        kernel,
        grid_spec=pltpu.PrefetchScalarGridSpec(
            num_scalar_prefetch=len(prefetch),
            grid=grid,
            in_specs=in_specs,
            out_specs=out_specs,
            scratch_shapes=scratch,
        ),
        out_shape=[pltpu.HBM(shape, kind) for shape, kind in outs],
        input_output_aliases=aliases,
        compiler_params=pltpu.CompilerParams(vmem_limit_bytes=52 * 1024 * 1024),
        cost_estimate=CHEAP,
        name=name,
    )(*prefetch, *[pltpu.with_memory_space_constraint(v, pltpu.HBM) for v in operands])
    return got


def full(*shape):
    return pl.BlockSpec(shape, lambda *_: (0,) * len(shape))


def _matmul_kernel(a_ref, b_ref, o_ref, *, dims):
    part = lax.dot_general(a_ref[...], b_ref[...], (dims, ((), ())), preferred_element_type=F32)
    o_ref[...] = part.astype(o_ref.dtype)


def matmul(a, b, kind, steps, by, out=BF):
    dims = {"nn": ((1,), (0,)), "nt": ((1,), (1,)), "tn": ((0,), (0,))}[kind]
    rows = a.shape[1 - dims[0][0]]
    columns = b.shape[1 - dims[1][0]]
    a_spec, b_spec = full(*a.shape), full(*b.shape)
    if by == "rows":
        size = rows // steps
        if kind == "tn":
            a_spec = pl.BlockSpec((a.shape[0], size), lambda i: (0, i))
        else:
            a_spec = pl.BlockSpec((size, a.shape[1]), lambda i: (i, 0))
        o_spec = pl.BlockSpec((size, columns), lambda i: (i, 0))
    else:
        size = columns // steps
        if kind == "nt":
            b_spec = pl.BlockSpec((size, b.shape[1]), lambda i: (i, 0))
        else:
            b_spec = pl.BlockSpec((b.shape[0], size), lambda i: (0, i))
        o_spec = pl.BlockSpec((rows, size), lambda i: (0, i))
    return run(
        partial(_matmul_kernel, dims=dims),
        "matmul_" + kind,
        (steps,),
        (a, b),
        [a_spec, b_spec],
        [((rows, columns), out)],
        [o_spec],
    )[0]


def _dispatch_kernel(s_ref, pick_ref, *refs, sources):
    z, rows = s_ref[0], refs[0][...]
    for n in range(1, len(refs) - 1):
        here = False
        for at, source in enumerate(sources):
            if source == n:
                here = here | (z == at)
        rows = jnp.where(here, refs[n][...], rows)
    refs[-1][...] = jnp.dot(pick_ref[...], rows, preferred_element_type=F32).astype(BF)


def dispatch(scalars, pick, blocks, sources):
    slots, tokens = pick.shape
    width = blocks[0].shape[1]
    tile = pl.BlockSpec((tokens, 1024), lambda j, s: (0, j))
    return run(
        partial(_dispatch_kernel, sources=sources),
        "dispatch",
        (width // 1024,),
        (pick, *blocks),
        [full(slots, tokens)] + [tile] * len(blocks),
        [((slots, width), BF)],
        [pl.BlockSpec((slots, 1024), lambda j, s: (0, j))],
        scalars=scalars,
    )[0]


def _part_kernel(s_ref, a_ref, b_ref, *refs, step):
    z = s_ref[0]
    part = jnp.dot(a_ref[...], b_ref[...], preferred_element_type=F32)
    if step == 0:
        refs[0][...] = part.astype(BF)
    elif step == 1:
        third, got, part_ref, middle_ref = refs
        part_ref[...] = part.astype(BF)
        middle = jnp.where((z == 0) | (z == 3), part, third[...].astype(F32))
        middle_ref[...] = (middle + got[...].astype(F32)).astype(BF)
    else:
        second, up, down, up_ref, down_ref = refs
        other = second[...].astype(F32)
        up_ref[...] = (jnp.where(z == 1, other, part) + up[...].astype(F32)).astype(BF)
        down_ref[...] = (jnp.where(z == 2, other, part) + down[...].astype(F32)).astype(BF)


def line_part(scalars, a, b, tokens, step=0, more=()):
    width = b.shape[1]
    tile = pl.BlockSpec((tokens, 1024), lambda j, s: (0, j))
    return run(
        partial(_part_kernel, step=step),
        "line_part",
        (width // 1024,),
        (a, b, *more),
        [
            pl.BlockSpec((tokens, a.shape[1]), lambda j, s: (s[1], 0)),
            pl.BlockSpec((b.shape[0], 1024), lambda j, s: (0, j)),
        ]
        + [tile] * len(more),
        [((tokens, width), BF)] * (1 if step == 0 else 2),
        [tile] * (1 if step == 0 else 2),
        scalars=scalars,
    )


def _norm_kernel(x_ref, gain_ref, *refs):
    terms, (resid_ref, low_ref) = refs[:-2], refs[-2:]
    value = x_ref[...].astype(F32)
    for term in terms:
        value = value + term[...].astype(F32)
    resid_ref[...] = value
    factor = lax.rsqrt(jnp.mean(value * value, axis=-1, keepdims=True) + EPS)
    low_ref[...] = (value * factor * gain_ref[...]).astype(BF)


def add_and_norm(x, gain, terms):
    tokens, width = x.shape
    step = min(tokens, 64)
    tile = pl.BlockSpec((step, width), lambda i: (i, 0))
    return run(
        _norm_kernel,
        "add_and_norm",
        (tokens // step,),
        (x, gain, *terms),
        [tile, full(1, width)] + [tile] * len(terms),
        [((tokens, width), F32), ((tokens, width), BF)],
        [tile, tile],
    )


def _norm_back_kernel(v_ref, gain_ref, above_ref, *refs, logits):
    if logits:
        logit_ref, router_ref, *terms, total_ref, low_ref, gain_grad_ref = refs
    else:
        *terms, total_ref = refs
    grad = sum([term[...].astype(F32) for term in terms])
    if logits:
        grad = grad + times_transposed(logit_ref[...], router_ref[...])
    value = v_ref[...].astype(F32)
    factor = lax.rsqrt(jnp.mean(value * value, axis=-1, keepdims=True) + EPS)
    unit = value * factor
    if logits:

        @pl.when(pl.program_id(0) == 0)
        def _():
            gain_grad_ref[...] = jnp.zeros_like(gain_grad_ref)

        gain_grad_ref[...] += jnp.sum(grad * unit, axis=0, keepdims=True)
    grad = grad * gain_ref[...]
    shift = jnp.mean(grad * unit, axis=-1, keepdims=True)
    total = above_ref[...].astype(F32) + factor * (grad - unit * shift)
    total_ref[...] = total
    if logits:
        low_ref[...] = total.astype(BF)


def norm_back(value, gain, above, terms, logit_grad=None, router=None):
    tokens, width = value.shape
    step = min(tokens, 64)
    tile = pl.BlockSpec((step, width), lambda i: (i, 0))
    operands, specs = [value, gain, above], [tile, full(1, width), tile]
    outs, out_specs = [((tokens, width), F32)], [tile]
    if logit_grad is not None:
        lanes = logit_grad.shape[1]
        operands += [logit_grad, router]
        specs += [pl.BlockSpec((step, lanes), lambda i: (i, 0)), full(width, lanes)]
        outs += [((tokens, width), BF), ((1, width), F32)]
        out_specs += [tile, full(1, width)]
    return run(
        partial(_norm_back_kernel, logits=logit_grad is not None),
        "norm_back",
        (tokens // step,),
        (*operands, *terms),
        specs + [tile] * len(terms),
        outs,
        out_specs,
    )


def _project_kernel(
    x_ref, gain_ref, w_ref, cos_ref, sin_ref, qg_ref, kg_ref, n_ref, raw_ref, q_ref, kv_ref
):
    x = x_ref[...].astype(F32)
    factor = lax.rsqrt(jnp.mean(x * x, axis=-1, keepdims=True) + EPS)
    normed = (x * factor * gain_ref[...]).astype(BF)
    n_ref[...] = normed
    raw_ref[...] = jnp.dot(normed, w_ref[...], preferred_element_type=F32)
    cosine, sine = cos_ref[...], sin_ref[...]
    heads = q_ref.shape[1] // HEAD
    for h in range(heads + 1):
        cols = slice(h * HEAD, (h + 1) * HEAD)
        value = raw_ref[:, cols]
        factor = lax.rsqrt(jnp.mean(value * value, axis=-1, keepdims=True) + EPS)
        value = value * factor * (qg_ref[...] if h < heads else kg_ref[...])
        value = (value * cosine + pltpu.roll(value, HEAD // 2, 1) * sine).astype(BF)
        if h < heads:
            q_ref[:, cols] = value
        else:
            kv_ref[:, :HEAD] = value
    kv_ref[:, HEAD:] = raw_ref[:, (heads + 1) * HEAD :].astype(BF)


def project(x, gain, w_in, cosine, sine, query_gain, key_gain, rows):
    tokens, width = x.shape
    columns = w_in.shape[1]

    def tile(size):
        return pl.BlockSpec((rows, size), lambda i: (i, 0))

    return run(
        _project_kernel,
        "project",
        (tokens // rows,),
        (x, gain, w_in, cosine, sine, query_gain, key_gain),
        [tile(width), full(1, width), full(width, columns), tile(HEAD), tile(HEAD)]
        + [full(1, HEAD)] * 2,
        [
            ((tokens, width), BF),
            ((tokens, columns), F32),
            ((tokens, columns - 2 * HEAD), BF),
            ((tokens, 2 * HEAD), BF),
        ],
        [tile(width), tile(columns), tile(columns - 2 * HEAD), tile(2 * HEAD)],
    )


def _project_back_kernel(
    raw_ref, dq_ref, dkv_ref, w_ref, cos_ref, sin_ref, qg_ref, kg_ref, ng_ref, rg_ref, dqg_ref, dkg_ref
):
    @pl.when(pl.program_id(0) == 0)
    def _():
        dqg_ref[...] = jnp.zeros_like(dqg_ref)
        dkg_ref[...] = jnp.zeros_like(dkg_ref)

    cosine, sine = cos_ref[...], sin_ref[...]
    heads = dq_ref.shape[1] // HEAD
    for h in range(heads + 1):
        cols = slice(h * HEAD, (h + 1) * HEAD)
        value = raw_ref[:, cols]
        factor = lax.rsqrt(jnp.mean(value * value, axis=-1, keepdims=True) + EPS)
        unit = value * factor
        if h < heads:
            grad = dq_ref[:, cols].astype(F32) * (1.0 / math.sqrt(HEAD))
        else:
            grad = dkv_ref[:, :HEAD]
        grad = grad * cosine + pltpu.roll(grad * sine, HEAD // 2, 1)
        gain_grad = jnp.sum(grad * unit, axis=0, keepdims=True)
        if h < heads:
            dqg_ref[...] += gain_grad
            grad = grad * qg_ref[...]
        else:
            dkg_ref[...] += gain_grad
            grad = grad * kg_ref[...]
        shift = jnp.mean(grad * unit, axis=-1, keepdims=True)
        rg_ref[:, cols] = (factor * (grad - unit * shift)).astype(BF)
    rg_ref[:, (heads + 1) * HEAD :] = dkv_ref[:, HEAD:].astype(BF)
    ng_ref[...] = times_transposed(rg_ref[...], w_ref[...]).astype(BF)


def project_back(raw, query_grads, key_value_grads, w_in, cosine, sine, query_gain, key_gain, rows):
    tokens, columns = raw.shape
    width = w_in.shape[0]

    def tile(size):
        return pl.BlockSpec((rows, size), lambda i: (i, 0))

    return run(
        _project_back_kernel,
        "project_back",
        (tokens // rows,),
        (raw, query_grads, key_value_grads, w_in, cosine, sine, query_gain, key_gain),
        [
            tile(columns),
            tile(columns - 2 * HEAD),
            tile(2 * HEAD),
            full(width, columns),
            tile(HEAD),
            tile(HEAD),
            full(1, HEAD),
            full(1, HEAD),
        ],
        [((tokens, width), BF), ((tokens, columns), BF), ((1, HEAD), F32), ((1, HEAD), F32)],
        [tile(width), tile(columns), full(1, HEAD), full(1, HEAD)],
    )


def _mask_bias(at_ref, opens_ref, bias_ref, low, high):
    rows = at_ref.shape[0]
    key_at = low + lax.broadcasted_iota(jnp.int32, (rows, high - low), 1)
    query_at = at_ref[...]
    allowed = (key_at <= query_at) & ((key_at < PROMPT) | (key_at >= opens_ref[...]))
    bias = jnp.where(allowed, 0.0, -1e30).astype(F32)
    bias_ref[:rows, low:high] = bias
    bias_ref[rows:, low:high] = bias


def _spans(number, chunk):
    return (number + 1) * chunk, min(number * chunk, PROMPT)


def _place_keys(table, pieces, k_ref, v_ref, rows):
    for k, piece in enumerate(pieces):
        for i in range(STEPS):
            place = pl.ds(pl.multiple_of(table[k * STEPS + i], rows), rows)
            k_ref[place, :HEAD] = piece[i * rows : (i + 1) * rows, :HEAD]
            v_ref[place, :HEAD] = piece[i * rows : (i + 1) * rows, HEAD:]


def _two_heads(ref, pair):
    first = pl.multiple_of(pair * 2 * HEAD, 2 * HEAD)
    return jnp.concatenate([ref[:, pl.ds(first, HEAD)], ref[:, pl.ds(first + HEAD, HEAD)]])


def _store_heads(ref, pair, value):
    first = pl.multiple_of(pair * 2 * HEAD, 2 * HEAD)
    rows = ref.shape[0]
    ref[:, pl.ds(first, HEAD)] = value[:rows].astype(ref.dtype)
    ref[:, pl.ds(first + HEAD, HEAD)] = value[rows:].astype(ref.dtype)


def _attend_kernel(table, *refs, cores, chunk, rows):
    pieces, refs = refs[:cores], refs[cores:]
    q_ref, at_ref, opens_ref, o_ref, l_ref, bias_ref, k_ref, v_ref = refs

    @pl.when(pl.program_id(0) == 0)
    def _():
        _place_keys(table, pieces, k_ref, v_ref, rows)
        v_ref[:, HEAD:] = jnp.ones((v_ref.shape[0], HEAD), BF)

    number = pl.program_id(0)
    for n in range(STEPS):

        @pl.when(number == n)
        def _(n=n):
            keys, masked = _spans(n, chunk)
            _mask_bias(at_ref, opens_ref, bias_ref, masked, keys)

            def pair_of_heads(pair, carry):
                query = _two_heads(q_ref, pair)
                out = None
                for low in range(0, keys, chunk):
                    s = times_transposed(query, k_ref[low : low + chunk, :])
                    if low >= masked:
                        s = s + bias_ref[:, low : low + chunk]
                    o = jnp.dot(
                        jnp.exp2(s).astype(BF),
                        v_ref[low : low + chunk, :],
                        preferred_element_type=F32,
                    )
                    out = o if out is None else out + o
                total = out[:, HEAD:]
                _store_heads(o_ref, pair, out[:, :HEAD] / total)
                log_total = jnp.log2(total)
                l_ref[2 * pair] = log_total[:rows]
                l_ref[2 * pair + 1] = log_total[rows:]
                return carry

            lax.fori_loop(0, q_ref.shape[1] // (2 * HEAD), pair_of_heads, 0, unroll=2)


def attend(table, queries, pieces, query_at, opens, rows):
    tokens, width = queries.shape
    heads, cores = width // HEAD, len(pieces)
    group = cores * tokens
    chunk = group // STEPS
    column = pl.BlockSpec((rows, 1), lambda i, o: (i, 0))
    tile = pl.BlockSpec((rows, width), lambda i, o: (i, 0))
    return run(
        partial(_attend_kernel, cores=cores, chunk=chunk, rows=rows),
        "attend",
        (STEPS,),
        (*pieces, queries, query_at, opens),
        [full(tokens, 2 * HEAD)] * cores + [tile, column, column],
        [((tokens, width), BF), ((heads, tokens, HEAD), F32)],
        [tile, pl.BlockSpec((heads, rows, HEAD), lambda i, o: (0, i, 0))],
        scalars=table,
        scratch=[
            pltpu.VMEM((2 * rows, group), F32),
            pltpu.VMEM((group, HEAD), BF),
            pltpu.VMEM((group, 2 * HEAD), BF),
        ],
    )


def _beside(value, column):
    high = column.astype(BF)
    low = (column - high.astype(F32)).astype(BF)
    lane = lax.broadcasted_iota(jnp.int32, value.shape, 1)
    zero = jnp.zeros(value.shape, BF)
    extra = jnp.where(lane == 0, -high, jnp.where(lane == 1, -low, zero))
    return jnp.concatenate([value, extra], axis=1)


def _attend_back_kernel(table, *refs, cores, chunk, rows):
    pieces, refs = refs[:cores], refs[cores:]
    q_ref, do_ref, o_ref, l_ref, at_ref, opens_ref, dq_ref = refs[:7]
    sums, refs = refs[7 : 7 + cores], refs[7 + cores :]
    bias_ref, k_ref, v_ref, dk_ref, dv_ref = refs

    @pl.when(pl.program_id(0) == 0)
    def _():
        _place_keys(table, pieces, k_ref, v_ref, rows)
        ones = jnp.ones((k_ref.shape[0], HEAD), BF)
        k_ref[:, HEAD:] = ones
        v_ref[:, HEAD:] = ones
        dk_ref[...] = jnp.zeros_like(dk_ref)
        dv_ref[...] = jnp.zeros_like(dv_ref)

    number = pl.program_id(0)
    for n in range(STEPS):

        @pl.when(number == n)
        def _(n=n):
            keys, masked = _spans(n, chunk)
            _mask_bias(at_ref, opens_ref, bias_ref, masked, keys)

            def pair_of_heads(pair, carry):
                query, grad = _two_heads(q_ref, pair), _two_heads(do_ref, pair)
                out = _two_heads(o_ref, pair)
                centre = jnp.sum(grad.astype(F32) * out.astype(F32), axis=-1, keepdims=True)
                log_total = jnp.concatenate([l_ref[2 * pair], l_ref[2 * pair + 1]])
                query_wide = _beside(query, log_total)
                grad_wide = _beside(grad, jnp.broadcast_to(centre, grad.shape))
                dq = None
                for low in range(0, keys, chunk):
                    span = slice(low, low + chunk)
                    s = times_transposed(query_wide, k_ref[span, :])
                    if low >= masked:
                        s = s + bias_ref[:, span]
                    p = jnp.exp2(s)
                    ds = (p * times_transposed(grad_wide, v_ref[span, :])).astype(BF)
                    dv_ref[span, :] += contract_rows(p.astype(BF), grad)
                    dk_ref[span, :] += contract_rows(ds, query)
                    part = jnp.dot(ds, k_ref[span, :HEAD], preferred_element_type=F32)
                    dq = part if dq is None else dq + part
                _store_heads(dq_ref, pair, dq)
                return carry

            lax.fori_loop(0, q_ref.shape[1] // (2 * HEAD), pair_of_heads, 0)

    @pl.when(number == STEPS - 1)
    def _():
        for k, piece in enumerate(sums):
            for i in range(STEPS):
                place = pl.ds(pl.multiple_of(table[k * STEPS + i], rows), rows)
                piece[i * rows : (i + 1) * rows, :HEAD] = dk_ref[place, :] * (1.0 / LOG2E)
                piece[i * rows : (i + 1) * rows, HEAD:] = dv_ref[place, :]


def attend_back(table, queries, grads, mixed, log_totals, pieces, query_at, opens, rows):
    tokens, width = queries.shape
    heads, cores = width // HEAD, len(pieces)
    group = cores * tokens
    chunk = group // STEPS
    piece = full(tokens, 2 * HEAD)
    column = pl.BlockSpec((rows, 1), lambda i, o: (i, 0))
    tile = pl.BlockSpec((rows, width), lambda i, o: (i, 0))
    return run(
        partial(_attend_back_kernel, cores=cores, chunk=chunk, rows=rows),
        "attend_back",
        (STEPS,),
        (*pieces, queries, grads, mixed, log_totals, query_at, opens),
        [piece] * cores
        + [tile, tile, tile, pl.BlockSpec((heads, rows, HEAD), lambda i, o: (0, i, 0))]
        + [column, column],
        [((tokens, width), BF)] + [((tokens, 2 * HEAD), F32)] * cores,
        [tile] + [piece] * cores,
        scalars=table,
        scratch=[
            pltpu.VMEM((2 * rows, group), F32),
            pltpu.VMEM((group, 2 * HEAD), BF),
            pltpu.VMEM((group, 2 * HEAD), BF),
            pltpu.VMEM((group, HEAD), F32),
            pltpu.VMEM((group, HEAD), F32),
        ],
    )


def _expert_kernel(
    x_ref, pulled_ref, chosen_ref, own_ref, router_ref, gate_ref, up_ref,
    dx_ref, dg_ref, du_ref, h_ref, c_ref,
):
    rows = x_ref[...]
    logits = jnp.dot(rows, router_ref[...], preferred_element_type=F32)
    chosen = chosen_ref[...].astype(F32)
    logits = jnp.where(chosen > 0.0, logits, -1e30)
    raised = jnp.exp(logits - jnp.max(logits, axis=-1, keepdims=True)) * chosen
    weight = jnp.sum(raised * own_ref[...], axis=-1, keepdims=True)
    weight = weight / jnp.maximum(jnp.sum(raised, axis=-1, keepdims=True), 1e-30)
    gate = jnp.dot(rows, gate_ref[...], preferred_element_type=F32)
    up = jnp.dot(rows, up_ref[...], preferred_element_type=F32)
    sigma = jax.nn.sigmoid(gate)
    swish = gate * sigma
    hidden = swish * up
    pulled = pulled_ref[...].astype(F32)
    c_ref[...] = jnp.sum(hidden * pulled, axis=-1, keepdims=True)
    h_ref[...] = (weight * hidden).astype(BF)
    pulled = weight * pulled
    gate_grad = (pulled * up * sigma * (1.0 + gate * (1.0 - sigma))).astype(BF)
    up_grad = (pulled * swish).astype(BF)
    dg_ref[...] = gate_grad
    du_ref[...] = up_grad
    dx = times_transposed(gate_grad, gate_ref[...]) + times_transposed(up_grad, up_ref[...])
    dx_ref[...] = dx.astype(BF)


def expert(rows, pulled, chosen, own, router, gate, up):
    count, width = rows.shape
    hidden = gate.shape[1]
    lanes = chosen.shape[1]
    step = min(count, 256)
    across = pl.BlockSpec((step, width), lambda i: (i, 0))
    thin = pl.BlockSpec((step, hidden), lambda i: (i, 0))
    column = pl.BlockSpec((step, 1), lambda i: (i, 0))
    return run(
        _expert_kernel,
        "expert",
        (count // step,),
        (rows, pulled, chosen, own, router, gate, up),
        [across, thin, pl.BlockSpec((step, lanes), lambda i: (i, 0)), full(1, lanes)]
        + [full(width, lanes), full(width, hidden), full(width, hidden)],
        [((count, width), BF)] + [((count, hidden), BF)] * 3 + [((count, 1), F32)],
        [across, thin, thin, thin, column],
    )


def _rows_kernel(*refs):
    count = (len(refs) - 1) // 2
    total = None
    for left, right in zip(refs[:count], refs[count:-1]):
        part = contract_rows(left[...], right[...])
        total = part if total is None else total + part
    refs[-1][...] = total


def contract_chunks(lefts, rights):
    count, tall = lefts[0].shape
    wide = rights[0].shape[1]
    step = min(tall, 256)
    return run(
        _rows_kernel,
        "contract_chunks",
        (tall // step,),
        (*lefts, *rights),
        [pl.BlockSpec((count, step), lambda i: (0, i))] * len(lefts)
        + [full(count, wide)] * len(rights),
        [((tall, wide), F32)],
        [pl.BlockSpec((step, wide), lambda i: (i, 0))],
    )[0]


def body(
    layer_input,
    attn_gain,
    w_query,
    key_matrix,
    value_matrix,
    query_gain,
    key_gain,
    w_out,
    moe_gain,
    router,
    expert_gate,
    expert_up,
    expert_down,
    expert_ids,
    cont_segment,
    out_grad,
):
    tokens, width = layer_input.shape
    dps, _, cores = sizes = [lax.axis_size(a) for a in ALL]
    devices = math.prod(sizes)
    dp, z, c = [lax.axis_index(a) for a in ALL]
    experts = router.shape[1]
    capacity = tokens * TOP // experts
    plane = dps * cores
    slots = plane * capacity
    order = jnp.array(ORDER, jnp.int32)[z]
    where_block = jnp.array([[o.index(b) for b in range(STEPS)] for o in ORDER], jnp.int32)[z]
    own_heads = HQ // (STEPS * cores)
    heads = HQ // STEPS
    head_cols = heads * HEAD
    own_cols = own_heads * HEAD

    rows_dev = router.shape[0]
    id_cols = tokens * TOP // rows_dev
    router_pad = -(experts + 2 + id_cols) % 128
    small = jnp.concatenate(
        [
            router,
            attn_gain[:, None],
            moe_gain[:, None],
            expert_ids.astype(BF).reshape(rows_dev, id_cols),
            jnp.zeros((rows_dev, router_pad), BF),
        ],
        axis=1,
    )
    packed = jnp.concatenate(
        [
            key_matrix.reshape(rows_dev, STEPS, HEAD).transpose(1, 0, 2),
            value_matrix.reshape(rows_dev, STEPS, HEAD).transpose(1, 0, 2),
            jnp.broadcast_to(small[None], (STEPS, *small.shape)),
        ],
        axis=2,
    )
    flat = [(b, (b % dps) * (devices // dps) + b // dps) for b in range(devices)]
    w_back = lax.ppermute(w_out, ALL, flat)
    query_own = from_dps(w_query, dp).reshape(width, own_cols)
    packed = lax.all_to_all(packed, "z", split_axis=0, concat_axis=0, tiled=True)
    packed, w_back, own_input, order, where_block = hold(
        packed, w_back, layer_input, order, where_block
    )
    arrived = lax.all_gather(own_input, "z", axis=0, tiled=True)
    w_back = lax.all_gather(w_back, PLANE, axis=0, tiled=True)

    at_slot = jnp.arange(capacity, dtype=jnp.int32)
    earlier = (jnp.arange(tokens)[:, None] > jnp.arange(tokens)[None, :]).astype(BF)

    def plan(ids):
        chosen = jnp.any(ids[:, :, None] == jnp.arange(experts, dtype=jnp.int32), axis=1)
        ranks = jnp.dot(earlier, chosen.astype(BF), preferred_element_type=F32).astype(jnp.int32)
        ranks = jnp.where(chosen & (ranks < capacity), ranks, -1)
        in_plane = lax.dynamic_index_in_dim(
            ranks.reshape(tokens, dps, STEPS, cores), z, 2, keepdims=False
        ).reshape(tokens, plane)
        pick = (in_plane[:, :, None] == at_slot).reshape(tokens, slots).astype(BF)
        back = (in_plane.T[:, None, :] == at_slot[:, None]).reshape(slots, tokens).astype(BF)
        return chosen, ranks, pick, back

    def to_plane(rows):
        return lax.all_to_all(rows, PLANE, split_axis=0, concat_axis=0, tiled=True)

    zs = jnp.stack([z, jnp.int32(0)])
    own_chosen, own_ranks, own_pick, own_back = plan(expert_ids)
    own_slots = own_ranks[:, :, None] == at_slot
    first_id = 2 * HEAD + experts + 2
    ids = packed[:, :, first_id : first_id + id_cols].astype(jnp.int32)
    ids = ids.reshape(STEPS, tokens, TOP)
    ids = [lax.dynamic_index_in_dim(ids, order[i], 0, keepdims=False) for i in range(STEPS)]
    packed = jnp.stack(cores_in_order(packed, c), axis=1).reshape(w_query.shape[0], -1)
    packed = from_dps(packed, dp).reshape(width, -1)
    w_in = cores_in_order(query_own, c)
    *w_in, packed, ids, upstream_block = hold(*w_in, packed, ids, out_grad)
    g0 = to_plane(dispatch(zs, own_back, [upstream_block], (0, 0, 0, 0)))
    rest = packed[:, 2 * HEAD :]
    lanes = rest.shape[1]
    router_all = rest[:, :experts]
    attn_gain_all = rest[:, experts].astype(F32)[None, :]
    moe_gain_all = rest[:, experts + 1].astype(F32)[None, :]
    w_in = jnp.concatenate([*w_in, packed[:, : 2 * HEAD]], axis=1)
    plans = [(own_chosen, own_ranks, own_pick, own_back)] + [plan(i) for i in ids[1:]]
    pick = [p[2] for p in plans]
    back = [p[3] for p in plans]
    slot_chosen = jnp.stack(
        [
            jnp.dot(back[i], jnp.pad(p[0].astype(BF), ((0, 0), (0, lanes - experts))))
            for i, p in enumerate(plans)
        ]
    ).reshape(STEPS, plane, capacity, lanes)
    slot_chosen = slot_chosen.transpose(1, 0, 2, 3)
    own_expert = dp * (STEPS * cores) + z * cores + c
    own_expert = (jnp.arange(lanes)[None, :] == own_expert).astype(F32)

    where_at, opens = group_layout(cont_segment[0])
    group = where_at.shape[0]

    def own_rows(table):
        mine = lax.dynamic_index_in_dim(table.reshape(STEPS, cores, tokens), c, 1, keepdims=False)
        return mine.reshape(-1)

    cosine, sine = angle_tables(own_rows(where_at), HEAD)
    query_at = own_rows(jnp.arange(group, dtype=jnp.int32))[:, None]
    opens = own_rows(opens)[:, None]
    numbers = jnp.arange(STEPS, dtype=jnp.int32)
    table = jnp.concatenate([(numbers * cores + (c + k) % cores) * tokens for k in range(cores)])
    query_gain_f = query_gain.astype(F32)[None, :]
    key_gain_f = key_gain.astype(F32)[None, :]
    scale = LOG2E / math.sqrt(HEAD)
    query_gain_s = query_gain_f * scale
    gate_w, up_w, down_w = expert_gate[0], expert_up[0], expert_down[0]
    at_block = [jnp.stack([z, order[i]]) for i in range(STEPS)]

    (
        arrived, upstream_block, w_in, pick, back, slot_chosen, cosine, sine, query_at, opens, table,
        query_gain_s, key_gain_f, at_block, own_expert, attn_gain_all, moe_gain_all, g0,
    ) = hold(
        arrived, upstream_block, w_in, pick, back, slot_chosen, cosine, sine, query_at, opens, table,
        query_gain_s, key_gain_f, at_block, own_expert, attn_gain_all, moe_gain_all, g0,
    )
    g_up, g_down = spread_first(upstream_block)
    normed, raw, queries, key_value_rows = project(
        arrived, attn_gain_all, w_in, cosine, sine, query_gain_s, key_gain_f, tokens
    )
    pieces = [key_value_rows, *other_cores(key_value_rows)]
    pulled0 = matmul(g0, down_w, "nt", 2, "rows", F32)
    queries, g_up, g_down, pulled0, *pieces = hold(queries, g_up, g_down, pulled0, *pieces)
    g_up2, g_down2 = spread_second(g_up, g_down)
    g1 = to_plane(dispatch(zs, back[1], [g_up, g_down], FIRST))
    mixed, log_totals = attend(table, queries, pieces, query_at, opens, tokens)
    mixed, g1, w_back, g_up2, g_down2 = hold(mixed, g1, w_back, g_up2, g_down2)
    g_last = spread_third(g_up2, g_down2, z)
    w_back = w_back.reshape(dps, cores, -1, width).transpose(1, 0, 2, 3).reshape(head_cols, width)
    attended = matmul(mixed, w_back, "nn", 4, "columns")
    attended, g1, g_up2, g_down2, g_last = hold(attended, g1, g_up2, g_down2, g_last)
    attended = lax.psum_scatter(attended, "z", scatter_dimension=0, tiled=True)
    g2 = to_plane(dispatch(zs, back[2], [g_up, g_down, g_up2, g_down2], SECOND))
    pulled1 = matmul(g1, down_w, "nt", 2, "rows", F32)
    g2, g_last, pulled1 = hold(g2, g_last, pulled1)
    g3 = to_plane(dispatch(zs, back[3], [g_up2, g_down2, g_last], THIRD))
    pulled2 = matmul(g2, down_w, "nt", 2, "rows", F32)
    g3, pulled2, slot_chosen = hold(g3, pulled2, slot_chosen)
    slot_chosen = to_plane(slot_chosen)
    slot_chosen = slot_chosen.transpose(1, 0, 2, 3).reshape(STEPS, slots, lanes)
    pulled3 = matmul(g3, down_w, "nt", 2, "rows", F32)
    attended, pulled3, slot_chosen = hold(attended, pulled3, slot_chosen)
    upstream_slots = [g0, g1, g2, g3]
    resid, moe_low = add_and_norm(layer_input, moe_gain_all, (attended,))

    def through(i, rows, pulled):
        return expert(rows, pulled, slot_chosen[i], own_expert, rest, gate_w, up_w)

    m_up, m_down = spread_first(moe_low)
    r0 = to_plane(dispatch(zs, back[0], [moe_low], (0, 0, 0, 0)))
    m_up, m_down = hold(m_up, m_down)
    m_up2, m_down2 = spread_second(m_up, m_down)
    r1 = dispatch(zs, back[1], [m_up, m_down], FIRST)
    r1, r0 = hold(r1, r0)
    r1 = to_plane(r1)
    e0 = through(0, r0, pulled0)
    m_up2, m_down2, e0 = hold(m_up2, m_down2, e0)
    m_last = spread_third(m_up2, m_down2, z)
    r2 = dispatch(zs, back[2], [m_up, m_down, m_up2, m_down2], SECOND)
    r2, r1 = hold(r2, r1)
    r2 = to_plane(r2)
    e1 = through(1, r1, pulled1)
    m_last, e1 = hold(m_last, e1)
    r3 = dispatch(zs, back[3], [m_up2, m_down2, m_last], THIRD)
    r3, r2 = hold(r3, r2)
    r3 = to_plane(r3)
    e2 = through(2, r2, pulled2)
    r3, e2 = hold(r3, e2)
    e3 = through(3, r3, pulled3)
    rows = [r0, r1, r2, r3]
    slot_grads, gate_grads, up_grads, hiddens, centres = [list(v) for v in zip(e0, e1, e2, e3)]
    d0, d1, d2, d3 = slot_grads
    b3 = to_plane(d3)
    moe_row, d2, centres, hiddens = hold(moe_low, d2, centres, hiddens)
    logits = jnp.dot(moe_row, router_all, preferred_element_type=F32)
    logits = jnp.where(own_chosen, logits, -jnp.inf)
    raised = jnp.exp(logits - jnp.max(logits, axis=-1, keepdims=True))
    gates = raised / jnp.sum(raised, axis=-1, keepdims=True)
    stacked = jnp.stack([v.reshape(dps, cores, capacity) for v in centres])
    centre_back = jnp.stack(
        [
            lax.dynamic_index_in_dim(stacked, where_block[b], 0, keepdims=False)
            for b in range(STEPS)
        ],
        axis=1,
    ).reshape(experts, capacity)
    p3, p2, p1, p0 = [matmul(hiddens[i], down_w, "nn", 4, "columns") for i in (3, 2, 1, 0)]
    b3, d2, p3, p2, p1, p0, centre_back, gates = hold(
        b3, d2, p3, p2, p1, p0, centre_back, gates
    )
    (c3,) = line_part(zs, pick[3], b3, tokens)
    c3, d2 = hold(c3, d2)
    got = sum_first(c3)
    b2 = to_plane(d2)
    got, b2, d1 = hold(got, b2, d1)
    c2, middle = line_part(zs, pick[2], b2, tokens, 1, (c3, got))
    middle, c2, d1 = hold(middle, c2, d1)
    s_up, s_down = sum_second(middle)
    b1 = to_plane(d1)
    s_up, s_down, b1, centre_back, d0 = hold(s_up, s_down, b1, centre_back, d0)
    s_up, s_down = line_part(zs, pick[1], b1, tokens, 2, (c2, s_up, s_down))
    s_up, s_down, d0, centre_back = hold(s_up, s_down, d0, centre_back)
    s_up, s_down = sum_third(s_up, s_down)
    b0 = to_plane(d0)
    b0, centre_back = hold(b0, centre_back)
    centre_back = lax.all_to_all(centre_back, ALL, split_axis=0, concat_axis=0, tiled=True)
    (c0,) = line_part(zs, pick[0], b0, tokens)
    weight_grad = jnp.sum(jnp.where(own_slots, centre_back[None], 0.0), axis=2)
    logit_grad = (
        gates * (weight_grad - jnp.sum(gates * weight_grad, axis=-1, keepdims=True))
    ).astype(BF)
    logit_wide = jnp.pad(logit_grad, ((0, 0), (0, lanes - experts)))
    s_up, s_down, c0, logit_wide = hold(s_up, s_down, c0, logit_wide)
    resid_grad, resid_low, moe_gain_grad = norm_back(
        resid, moe_gain_all, out_grad, (c0, s_up, s_down), logit_wide, rest
    )

    def by_core(value, axis):
        size = value.shape[axis] // cores
        return [
            lax.dynamic_slice_in_dim(value, (c + k) % cores * size, size, axis)
            for k in range(cores)
        ]

    resid_low, p3, logit_grad, hiddens, rows = hold(resid_low, p3, logit_grad, hiddens, rows)
    resid_all = lax.all_gather(resid_low, "z", axis=0, tiled=True)
    o3 = to_plane(p3)
    down_weight_grad = contract_chunks(hiddens, upstream_slots)
    router_grad = contract_rows(moe_low, logit_grad)
    o3, p2, rows, down_weight_grad, router_grad = hold(
        o3, p2, rows, down_weight_grad, router_grad
    )
    (o3,) = line_part(zs, pick[3], o3, tokens)
    t_got = sum_first(o3)
    o2 = to_plane(p2)
    up_weight_grad = contract_chunks(rows, up_grads)
    o2, o3, t_got, p1, rows, up_weight_grad = hold(o2, o3, t_got, p1, rows, up_weight_grad)
    o2, middle = line_part(zs, pick[2], o2, tokens, 1, (o3, t_got))
    middle, o2, p1 = hold(middle, o2, p1)
    t_up, t_down = sum_second(middle)
    o1 = to_plane(p1)
    gate_weight_grad = contract_chunks(rows, gate_grads)
    resid_all, o2, gate_weight_grad = hold(resid_all, o2, gate_weight_grad)
    mixed_grad = matmul(resid_all, w_back, "nt", 4, "rows")
    mixed_grad, resid_all = hold(mixed_grad, resid_all)
    out_weight_grad = matmul(mixed, resid_all, "tn", 4, "columns")
    out_weight_grad = out_weight_grad.reshape(cores, dps, -1, width).transpose(1, 0, 2, 3)
    out_weight_grad = out_weight_grad.reshape(head_cols, width)
    mixed_grad, t_up, t_down, o1, o2, p0, out_weight_grad = hold(
        mixed_grad, t_up, t_down, o1, o2, p0, out_weight_grad
    )
    out_weight_grad = lax.psum_scatter(out_weight_grad, PLANE, scatter_dimension=0, tiled=True)
    t_up, t_down = line_part(zs, pick[1], o1, tokens, 2, (o2, t_up, t_down))
    t_up, t_down, p0 = hold(t_up, t_down, p0)
    t_up, t_down = sum_third(t_up, t_down)
    o0 = to_plane(p0)
    query_grads, *sums = attend_back(
        table, queries, mixed_grad, mixed, log_totals, pieces, query_at, opens, tokens
    )
    query_grads, t_up, t_down, o0, out_weight_grad, *sums = hold(
        query_grads, t_up, t_down, o0, out_weight_grad, *sums
    )
    out_weight_grad = lax.ppermute(out_weight_grad, ALL, [(b, a) for a, b in flat]).astype(F32)
    sums = sum_over_cores(sums)
    normed_grad, raw_grad, query_gain_grad, key_gain_grad = project_back(
        raw, query_grads, sums, w_in, cosine, sine, query_gain_f, key_gain_f, tokens
    )
    normed_grad, raw_grad, o0, out_weight_grad = hold(normed_grad, raw_grad, o0, out_weight_grad)
    normed_sum = lax.psum_scatter(normed_grad, "z", scatter_dimension=0, tiled=True)
    in_grad = matmul(normed, raw_grad, "tn", 4, "rows")
    inputs = arrived.astype(F32)
    input_factor = lax.rsqrt(jnp.mean(inputs * inputs, axis=-1, keepdims=True) + EPS)
    attn_gain_grad = jnp.sum(normed_grad.astype(F32) * inputs * input_factor, axis=0)[None, :]
    query_share = sum_over_cores(by_core(in_grad[:, :head_cols], 1)).astype(BF)
    key_value_grad = in_grad[:, head_cols:].reshape(dps, STEPS, cores, rows_dev, 2 * HEAD)
    key_value_grad = sum_over_cores(
        [part[:, :, 0] for part in by_core(key_value_grad, 2)]
    ).astype(BF)
    query_share, key_value_grad, o0, attn_gain_grad = hold(
        query_share, key_value_grad, o0, attn_gain_grad
    )
    query_weight_grad = over_dps(query_share.reshape(dps, -1, own_cols), dp)
    key_value_grad = over_dps(key_value_grad, dp).astype(BF)
    (o0,) = line_part(zs, pick[0], o0, tokens)
    output = resid + (o0.astype(F32) + t_up.astype(F32) + t_down.astype(F32))
    output = output.astype(BF)

    def to_owners(value):
        columns = value.shape[0]
        split = value.reshape(columns, devices, rows_dev).transpose(1, 0, 2)
        return split.reshape(devices, columns * rows_dev)

    gain_row = jnp.concatenate([query_gain_grad, key_gain_grad], axis=1)
    late = jnp.concatenate(
        [
            to_owners(jnp.concatenate([router_grad.T, moe_gain_grad, attn_gain_grad])),
            jnp.broadcast_to(gain_row, (devices, 2 * HEAD)),
        ],
        axis=1,
    )
    late = jnp.sum(lax.all_to_all(late, ALL, split_axis=0, concat_axis=0, tiled=True), axis=0)
    gain_sums = late[-2 * HEAD :].reshape(2, HEAD)
    owned = late[: -2 * HEAD].reshape(experts + 2, rows_dev)
    key_value_grad = lax.all_to_all(key_value_grad, "z", split_axis=0, concat_axis=0, tiled=True)
    key_value_grad = key_value_grad.transpose(1, 0, 2).astype(F32)
    key_weight_grad = key_value_grad[:, :, :HEAD].reshape(rows_dev, -1)
    value_weight_grad = key_value_grad[:, :, HEAD:].reshape(rows_dev, -1)
    (input_grad,) = norm_back(layer_input, attn_gain_all, resid_grad, (normed_sum,))
    return (
        output,
        input_grad,
        owned[experts + 1],
        query_weight_grad,
        key_weight_grad,
        value_weight_grad,
        gain_sums[0],
        gain_sums[1],
        out_weight_grad,
        owned[experts],
        owned[:experts].T,
        gate_weight_grad[None],
        up_weight_grad[None],
        down_weight_grad[None],
    )


def solution(mesh):
    dps, sequence = mesh.devices.shape
    inner = Mesh(mesh.devices.reshape(dps, STEPS, sequence // STEPS), ALL)
    rows = P(ALL, None)
    placed = (
        rows,
        P(ALL),
        P("dp", ("z", "core")),
        rows,
        rows,
        P(),
        P(),
        rows,
        P(ALL),
        rows,
        P(ALL, None, None),
        P(ALL, None, None),
        P(ALL, None, None),
        rows,
        P("dp", None),
        rows,
    )
    return jax.shard_map(
        body,
        mesh=inner,
        in_specs=placed,
        out_specs=(
            rows,
            rows,
            P(ALL),
            P("dp", ("z", "core")),
            rows,
            rows,
            P(),
            P(),
            rows,
            P(ALL),
            rows,
            P(ALL, None, None),
            P(ALL, None, None),
            P(ALL, None, None),
        ),
        check_vma=False,
    )
```

time: 1230 us -> 1030 us (0.84)
  Pallas kernels: 162 us -> 340 us
  blocking collectives: 137 us -> 0 us
  matrix products: 133 us -> 4.38 us
  other arithmetic: 140 us -> 51.2 us
  waiting for transfers between devices: 288 us -> 353 us
  starting transfers between devices: 222 us -> 174 us
  local copies, waits for them, and re-layouts: 105 us -> 68.9 us
    pallas_call x9 -> x42, Pallas kernels: 162 us -> 340 us  [run(): pl.pallas_call(kernel, grid_spec=pltpu.PrefetchScalarGridSpec(num_scalar_...]
    dot_general x23 -> x9, matrix products: 95.6 us -> 4.06 us  [the longest x4 1.74 us: body(): jnp.dot(back[i], jnp.pad(p[0].astype(BF), ((0, 0), (0, lanes - experts))))]
    all_to_all x16 -> x17, waiting for transfers between devices: 30.9 us -> 116 us  [to_plane(): return lax.all_to_all(rows, PLANE, split_axis=0, concat_axis=0, tiled=True)]
    psum x1 -> x0, blocking collectives: 57 us -> none  [body(): gain_sums = lax.psum(jnp.stack([query_gain_grad, key_gain_grad]), ALL)]
    ppermute x41 -> x33, waiting for transfers between devices: 233 us -> 178 us  [the longest x2 55.2 us: sum_first(): return lax.ppermute(third, 'z', [(0, 1), (3, 2)])]
    ppermute x41 -> x33, starting transfers between devices: 119 us -> 71.8 us  [the longest x6 15.9 us: over_dps(): lax.ppermute(piece, 'dp', [(i, i ^ k) for i in range(dps)]).astype(F32)]
    all_to_all x1 -> x0, blocking collectives: 43.6 us -> none  [body(): lax.all_to_all(packed, 'z', split_axis=0, concat_axis=0, tiled=True)]
    all_to_all x1 -> x2, waiting for transfers between devices: 3.72 us -> 44.7 us  [the longest x1 28.4 us: body(): lax.all_to_all(packed, 'z', split_axis=0, concat_axis=0, tiled=True)]
  transfers between devices with their start and end apart: 74 -> 67, of which waited for: 28 -> 29; matrix products, arithmetic and copies ran while one was open for 27% -> 10% of each run, Pallas kernels for 13% -> 27%
where the time goes in v2:
time: 1030 us; the launch traced here: 1020 us
  waiting for transfers between devices  353 us (34%)
  Pallas kernels  340 us (33%)
  starting transfers between devices  174 us (17%)
  local copies, waits for them, and re-layouts  68.9 us (7%)
  other arithmetic  51.2 us (5%)
  between operations  29.2 us (3%)
    pallas_call x42, Pallas kernels, run(): pl.pallas_call(kernel, grid_spec=pltpu.PrefetchScalarGridSpec(num_scalar_...  340 us
    all_to_all x17, waiting for transfers between devices, to_plane(): return lax.all_to_all(rows, PLANE, split_axis=0, concat_axis=0, tiled=True)  116 us
    all_to_all x17, starting transfers between devices, to_plane(): return lax.all_to_all(rows, PLANE, split_axis=0, concat_axis=0, tiled=True)  67.3 us
    ppermute x2, waiting for transfers between devices, sum_first(): return lax.ppermute(third, 'z', [(0, 1), (3, 2)])  55.2 us
    ppermute x6, waiting for transfers between devices, from_dps(): got = lax.ppermute(value, 'dp', [(i, i ^ k) for i in range(dps)])  29.8 us
    all_to_all x1, waiting for transfers between devices, body(): lax.all_to_all(packed, 'z', split_axis=0, concat_axis=0, tiled=True)  28.4 us
    ppermute x2, waiting for transfers between devices, spread_third(): return lax.ppermute(jnp.where(z == 2, up2, down2), 'z', [(2, 3), (1, 0)])  25.5 us
    ppermute x2, waiting for transfers between devices, sum_second(): lax.ppermute(middle, 'z', [(0, 1), (1, 2)])  22.4 us
  transfers between devices with their start and end apart: 67, of which 29 were waited for; matrix products, arithmetic and copies ran while one was open for 10% of the time, Pallas kernels for 27%

profile of v2, /device:TPU:0, one launch (start us, length us, event | category | flops | bytes accessed | tf_op | source)
XLA Modules:
  0.0 1019.9 jit_solution(1499282780383407022)
XLA Ops:
  23.5 28.4 %all-to-all-done = bf16[4,64,384]{2,1,0:T(8,128)(2,1)S(1)} async-done(((bf16[4,64,384]{2,1,0:T(8,128)(2,1)}), bf16[4,64,384]{2,1,0:T(8,128)(2,1)S(1)}, u32[]{:S(2)}, u32[]{:S(2)}) %all-to-all-start) | async-done | bytes 196640 | tf_op jit(solution)/shard_map/all_to_all | solution.py:784
  68.2 10.4 %collective-permute-done.2 = bf16[512,512]{1,0:T(8,128)(2,1)} collective-permute-done((bf16[512,512]{1,0:T(8,128)(2,1)}, bf16[512,512]{1,0:T(8,128)(2,1)}, u32[]{:S(2)}, u32[]{:S(2)}) %collective-permute-start.2) | collective-permute-done | bytes 524320 | tf_op jit(solution)/shard_map/ppermute | solution.py:121
  99.8 9.1 collective-permute-done.7
  137.9 18.5 %all-to-all-done.1 = bf16[8,64,2048]{2,1,0:T(8,128)(2,1)S(1)} async-done(((bf16[8,64,2048]{2,1,0:T(8,128)(2,1)}), bf16[8,64,2048]{2,1,0:T(8,128)(2,1)S(1)}, u32[]{:S(2)}, u32[]{:S(2)}) %all-to-all-start.1) | async-done | bytes 2097184 | tf_op jit(solution)/shard_map/all_to_all | solution.py:806
  162.5 12.6 %project.1 = (bf16[1024,2048]{1,0:T(8,128)(2,1)}, f32[1024,1280]{1,0:T(8,128)}, bf16[1024,1024]{1,0:T(8,128)(2,1)}, bf16[1024,256]{1,0:T(8,128)(2,1)}) custom-call(bf16[1024,2048]{1,0:T(8,128)(2,1)} %all-gather.4.cloned.1.call-done.x_ref, f32[1,2048]{1,0:T(1,128)} %bitcast.328, bf16[2048,1280]{1,0:T(8,128)(2,1)} %pad_maximum_fusion.w_ref, ...), custom_call_target="tpu_custom_call" | custom-call | flops 1 | bytes 1 | tf_op jit(solution)/shard_map/project/pallas_call | solution.py:161
  195.0 19.1 %attend.1 = (bf16[1024,1024]{1,0:T(8,128)(2,1)}, f32[8,1024,128]{2,1,0:T(8,128)}) custom-call(s32[8]{0:T(128)S(1)} %pad_add_fusion.table, bf16[1024,256]{1,0:T(8,128)(2,1)} %get-tuple-element.272.refs_0_, bf16[1024,256]{1,0:T(8,128)(2,1)} %copy-done.35, bf16[1024,1024]{1,0:T(8,128)(2,1)} %get-tuple-element.274.refs_2_, s32[1024,1]{1,0:T(8,128)} %copy.219.refs_3_.refs_6_, ...), custom_call_target="tpu_custom_call" | custom-call | flops 1 | bytes 1 | tf_op jit(solution)/shard_map/attend/pallas_call | solution.py:161
  239.2 12.1 %collective-permute-done.14.refs_2_ = bf16[256,2048]{1,0:T(8,128)(2,1)} collective-permute-done((bf16[256,2048]{1,0:T(8,128)(2,1)}, bf16[256,2048]{1,0:T(8,128)(2,1)}, u32[]{:S(2)}, u32[]{:S(2)}) %collective-permute-start.14) | collective-permute-done | bytes 1048608 | tf_op jit(solution)/shard_map/ppermute | solution.py:81
  264.5 21.4 %all-to-all-done.3 = bf16[8,64,2048]{2,1,0:T(8,128)(2,1)S(1)} async-done(((bf16[8,64,2048]{2,1,0:T(8,128)(2,1)}), bf16[8,64,2048]{2,1,0:T(8,128)(2,1)S(1)}, u32[]{:S(2)}, u32[]{:S(2)}) %all-to-all-start.3) | async-done | bytes 2097184 | tf_op jit(solution)/shard_map/all_to_all | solution.py:806
  299.2 21.3 %all-to-all-done.4 = bf16[8,64,2048]{2,1,0:T(8,128)(2,1)S(1)} async-done(((bf16[8,64,2048]{2,1,0:T(8,128)(2,1)}), bf16[8,64,2048]{2,1,0:T(8,128)(2,1)S(1)}, u32[]{:S(2)}, u32[]{:S(2)}) %all-to-all-start.4) | async-done | bytes 2097184 | tf_op jit(solution)/shard_map/all_to_all | solution.py:806
  352.7 21.4 %collective-permute-done.16.refs_1_ = bf16[256,2048]{1,0:T(8,128)(2,1)S(1)} collective-permute-done((bf16[256,2048]{1,0:T(8,128)(2,1)S(1)}, bf16[256,2048]{1,0:T(8,128)(2,1)S(1)}, u32[]{:S(2)}, u32[]{:S(2)}) %collective-permute-start.16) | collective-permute-done | bytes 1048608 | tf_op jit(solution)/shard_map/ppermute | solution.py:69
  391.5 12.6 %expert.4 = (bf16[512,2048]{1,0:T(8,128)(2,1)}, bf16[512,768]{1,0:T(8,128)(2,1)}, bf16[512,768]{1,0:T(8,128)(2,1)}, bf16[512,768]{1,0:T(8,128)(2,1)}, f32[512,1]{1,0:T(8,128)}) custom-call(bf16[512,2048]{1,0:T(8,128)(2,1)} %bitcast.264, f32[512,768]{1,0:T(8,128)} %matmul_nt.5.pulled_ref, bf16[512,128]{1,0:T(8,128)(2,1)} %get-tuple-element.497.chosen_ref, ...), custom_call_target="tpu_custom_call" | custom-call | flops 1 | bytes 1 | tf_op jit(solution)/shard_map/expert/pallas_call | solution.py:161
  404.1 11.6 %collective-permute-done.18.refs_3_.refs_1_ = bf16[256,2048]{1,0:T(8,128)(2,1)S(1)} collective-permute-done((bf16[256,2048]{1,0:T(8,128)(2,1)S(1)}, bf16[256,2048]{1,0:T(8,128)(2,1)S(1)}, u32[]{:S(2)}, u32[]{:S(2)}) %collective-permute-start.18) | collective-permute-done | bytes 1048608 | tf_op jit(solution)/shard_map/ppermute | solution.py:76
  428.0 12.6 %expert.5 = (bf16[512,2048]{1,0:T(8,128)(2,1)}, bf16[512,768]{1,0:T(8,128)(2,1)}, bf16[512,768]{1,0:T(8,128)(2,1)}, bf16[512,768]{1,0:T(8,128)(2,1)}, f32[512,1]{1,0:T(8,128)}) custom-call(bf16[512,2048]{1,0:T(8,128)(2,1)} %bitcast.73.x_ref.refs_1_, f32[512,768]{1,0:T(8,128)} %matmul_nt.6.pulled_ref, bf16[512,128]{1,0:T(8,128)(2,1)} %get-tuple-element.496.chosen_ref, ...), custom_call_target="tpu_custom_call" | custom-call | flops 1 | bytes 1 | tf_op jit(solution)/shard_map/expert/pallas_call | solution.py:161
  440.6 13.4 %collective-permute-done.19.refs_2_ = bf16[256,2048]{1,0:T(8,128)(2,1)S(1)} collective-permute-done((bf16[256,2048]{1,0:T(8,128)(2,1)S(1)}, bf16[256,2048]{1,0:T(8,128)(2,1)S(1)}, u32[]{:S(2)}, u32[]{:S(2)}) %collective-permute-start.19) | collective-permute-done | bytes 1048608 | tf_op jit(solution)/shard_map/ppermute | solution.py:81
  464.9 12.6 %expert.6 = (bf16[512,2048]{1,0:T(8,128)(2,1)}, bf16[512,768]{1,0:T(8,128)(2,1)}, bf16[512,768]{1,0:T(8,128)(2,1)}, bf16[512,768]{1,0:T(8,128)(2,1)}, f32[512,1]{1,0:T(8,128)}) custom-call(bf16[512,2048]{1,0:T(8,128)(2,1)} %bitcast.267, f32[512,768]{1,0:T(8,128)} %matmul_nt.7.pulled_ref, bf16[512,128]{1,0:T(8,128)(2,1)} %get-tuple-element.495.chosen_ref, ...), custom_call_target="tpu_custom_call" | custom-call | flops 1 | bytes 1 | tf_op jit(solution)/shard_map/expert/pallas_call | solution.py:161
  477.5 14.0 %all-to-all-done.9 = bf16[8,64,2048]{2,1,0:T(8,128)(2,1)} async-done(((bf16[8,64,2048]{2,1,0:T(8,128)(2,1)}), bf16[8,64,2048]{2,1,0:T(8,128)(2,1)}, u32[]{:S(2)}, u32[]{:S(2)}) %all-to-all-start.9) | async-done | bytes 2097184 | tf_op jit(solution)/shard_map/all_to_all | solution.py:806
  491.6 12.6 %expert.7 = (bf16[512,2048]{1,0:T(8,128)(2,1)}, bf16[512,768]{1,0:T(8,128)(2,1)}, bf16[512,768]{1,0:T(8,128)(2,1)}, bf16[512,768]{1,0:T(8,128)(2,1)}, f32[512,1]{1,0:T(8,128)}) custom-call(bf16[512,2048]{1,0:T(8,128)(2,1)} %bitcast.78.x_ref.refs_3_, f32[512,768]{1,0:T(8,128)} %matmul_nt.8.pulled_ref, bf16[512,128]{1,0:T(8,128)(2,1)} %get-tuple-element.494.chosen_ref, ...), custom_call_target="tpu_custom_call" | custom-call | flops 1 | bytes 1 | tf_op jit(solution)/shard_map/expert/pallas_call | solution.py:161
  556.1 22.2 %collective-permute-done.20.refs_1_ = bf16[256,2048]{1,0:T(8,128)(2,1)} collective-permute-done((bf16[256,2048]{1,0:T(8,128)(2,1)S(1)}, bf16[256,2048]{1,0:T(8,128)(2,1)}, u32[]{:S(2)}, u32[]{:S(2)}) %collective-permute-start.20) | collective-permute-done | bytes 1048608 | tf_op jit(solution)/shard_map/ppermute | solution.py:90
  594.5 22.4 %collective-permute-done.21.refs_1_ = bf16[256,2048]{1,0:T(8,128)(2,1)} collective-permute-done((bf16[256,2048]{1,0:T(8,128)(2,1)}, bf16[256,2048]{1,0:T(8,128)(2,1)}, u32[]{:S(2)}, u32[]{:S(2)}) %collective-permute-start.21) | collective-permute-done | bytes 1048608 | tf_op jit(solution)/shard_map/ppermute | solution.py:95
  632.6 20.9 %all-to-all-done.13 = bf16[8,64,2048]{2,1,0:T(8,128)(2,1)S(1)} async-done(((bf16[8,64,2048]{2,1,0:T(8,128)(2,1)}), bf16[8,64,2048]{2,1,0:T(8,128)(2,1)S(1)}, u32[]{:S(2)}, u32[]{:S(2)}) %all-to-all-start.13) | async-done | bytes 2097184 | tf_op jit(solution)/shard_map/all_to_all | solution.py:806
  677.9 13.2 %contract_chunks.3 = f32[768,2048]{1,0:T(8,128)} custom-call(bf16[512,768]{1,0:T(8,128)(2,1)} %get-tuple-element.405.a_ref.refs_0_, bf16[512,768]{1,0:T(8,128)(2,1)} %get-tuple-element.406.a_ref.refs_1_, bf16[512,768]{1,0:T(8,128)(2,1)} %get-tuple-element.407.a_ref.refs_2_, bf16[512,768]{1,0:T(8,128)(2,1)} %get-tuple-element.408.a_ref.refs_3_, ...), custom_call_target="tpu_custom_call" | custom-call | flops 1 | bytes 1 | tf_op jit(solution)/shard_map/contract_chunks/pallas_call | solution.py:161
  691.4 13.0 %all-to-all-done.15 = bf16[8,64,2048]{2,1,0:T(8,128)(2,1)S(1)} async-done(((bf16[8,64,2048]{2,1,0:T(8,128)(2,1)}), bf16[8,64,2048]{2,1,0:T(8,128)(2,1)S(1)}, u32[]{:S(2)}, u32[]{:S(2)}) %all-to-all-start.15) | async-done | bytes 2097184 | tf_op jit(solution)/shard_map/all_to_all | solution.py:806
  716.2 13.0 %contract_chunks.4 = f32[2048,768]{1,0:T(8,128)} custom-call(bf16[512,2048]{1,0:T(8,128)(2,1)} %bitcast.265, bf16[512,2048]{1,0:T(8,128)(2,1)} %bitcast.73.x_ref.refs_1_, bf16[512,2048]{1,0:T(8,128)(2,1)} %bitcast.268, bf16[512,2048]{1,0:T(8,128)(2,1)} %bitcast.78.x_ref.refs_3_, bf16[512,768]{1,0:T(8,128)(2,1)} %get-tuple-element.417.refs_4_, ...), custom_call_target="tpu_custom_call" | custom-call | flops 1 | bytes 1 | tf_op jit(solution)/shard_map/contract_chunks/pallas_call | solution.py:161
  729.2 33.0 %collective-permute-done.25.refs_1_ = bf16[256,2048]{1,0:T(8,128)(2,1)S(1)} collective-permute-done((bf16[256,2048]{1,0:T(8,128)(2,1)}, bf16[256,2048]{1,0:T(8,128)(2,1)S(1)}, u32[]{:S(2)}, u32[]{:S(2)}) %collective-permute-start.25) | collective-permute-done | bytes 1048608 | tf_op jit(solution)/shard_map/ppermute | solution.py:90
  778.5 13.0 %contract_chunks.5 = f32[2048,768]{1,0:T(8,128)} custom-call(bf16[512,2048]{1,0:T(8,128)(2,1)} %bitcast.266, bf16[512,2048]{1,0:T(8,128)(2,1)} %bitcast.73.x_ref.refs_1_, bf16[512,2048]{1,0:T(8,128)(2,1)} %bitcast.269, bf16[512,2048]{1,0:T(8,128)(2,1)} %bitcast.78.x_ref.refs_3_, bf16[512,768]{1,0:T(8,128)(2,1)} %get-tuple-element.432.refs_4_, ...), custom_call_target="tpu_custom_call" | custom-call | flops 1 | bytes 1 | tf_op jit(solution)/shard_map/contract_chunks/pallas_call | solution.py:161
  791.5 8.6 matmul_nt.9.refs_3_
  829.0 40.1 %attend_back.1 = (bf16[1024,1024]{1,0:T(8,128)(2,1)}, f32[1024,256]{1,0:T(8,128)}, f32[1024,256]{1,0:T(8,128)}) custom-call(s32[8]{0:T(128)S(1)} %pad_add_fusion.table, bf16[1024,256]{1,0:T(8,128)(2,1)} %get-tuple-element.272.refs_0_, bf16[1024,256]{1,0:T(8,128)(2,1)} %copy-done.35, bf16[1024,1024]{1,0:T(8,128)(2,1)} %get-tuple-element.274.refs_2_, ...), custom_call_target="tpu_custom_call" | custom-call | flops 1 | bytes 1 | tf_op jit(solution)/shard_map/attend_back/pallas_call | solution.py:161
  879.4 21.4 %project_back.1 = (bf16[1024,2048]{1,0:T(8,128)(2,1)}, bf16[1024,1280]{1,0:T(8,128)(2,1)}, f32[1,128]{1,0:T(1,128)}, f32[1,128]{1,0:T(1,128)}) custom-call(f32[1024,1280]{1,0:T(8,128)} %get-tuple-element.303.raw_ref, bf16[1024,1024]{1,0:T(8,128)(2,1)} %get-tuple-element.459.dq_ref, f32[1024,256]{1,0:T(8,128)} %add.217.dkv_ref, ...), custom_call_target="tpu_custom_call" | custom-call | flops 1 | bytes 1 | tf_op jit(solution)/shard_map/project_back/pallas_call | solution.py:161
  900.8 9.7 matmul_tn.3
  915.1 11.7 %collective-permute-start.32 = (bf16[2048,512]{1,0:T(8,128)(2,1)S(1)}, bf16[2048,512]{1,0:T(8,128)(2,1)}, u32[]{:S(2)}, u32[]{:S(2)}) collective-permute-start(bf16[2048,512]{1,0:T(8,128)(2,1)S(1)} %constant_dynamic-slice_fusion), channel_id=1, source_target_pairs={{0,1},{1,0},{2,3},{3,2},{4,5},{5,4},{6,7},{7,6},{8,9},{9,8},{10,11... | collective-permute-start | bytes 6291464 | tf_op jit(solution)/shard_map/ppermute | solution.py:150
  944.6 10.9 %collective-permute-start.37 = (bf16[4,64,256]{2,1,0:T(8,128)(2,1)S(1)}, bf16[4,64,256]{2,1,0:T(8,128)(2,1)S(1)}, u32[]{:S(2)}, u32[]{:S(2)}) collective-permute-start(bf16[4,64,256]{2,1,0:T(8,128)(2,1)S(1)} %get-tuple-element.491), channel_id=1, source_target_pairs={{0,8},{8,0},{16,24},{24,16},{1,9},{9,1},{17,25},{25,17},{2,10},{10... | collective-permute-start | bytes 393224 | tf_op jit(solution)/shard_map/ppermute | solution.py:112
  990.0 16.3 %all-to-all-done.19 = f32[32,1,2432]{2,1,0:T(1,128)S(1)} async-done(((f32[32,1,2432]{2,1,0:T(1,128)}), f32[32,1,2432]{2,1,0:T(1,128)S(1)}, u32[]{:S(2)}, u32[]{:S(2)}) %all-to-all-start.19) | async-done | bytes 311328 | tf_op jit(solution)/shard_map/all_to_all | solution.py:1049
  (431 shorter events, 457.6 us)
Async XLA Ops:
  7.2 44.7 %collective-permute-start = (bf16[128,2048]{1,0:T(8,128)(2,1)}, bf16[128,2048]{1,0:T(8,128)(2,1)S(1)}, u32[]{:S(2)}, u32[]{:S(2)}) collective-permute-start(bf16[128,2048]{1,0:T(8,128)(2,1)} %param.25), channel_id=1, source_target_pairs={{0,0},{1,8},{2,16},{3,24},{4,1},{5,9},{6,17},{7,25},{8,2},{9,10},{... | collective-permute-start | bytes 1572872 | tf_op jit(solution)/shard_map/ppermute | solution.py:782
  15.0 36.9 %all-to-all-start = ((bf16[4,64,384]{2,1,0:T(8,128)(2,1)}), bf16[4,64,384]{2,1,0:T(8,128)(2,1)S(1)}, u32[]{:S(2)}, u32[]{:S(2)}) async-start(bf16[4,64,384]{2,1,0:T(8,128)(2,1)} %copy.206), calls=%async_computation | async-start | bytes 393216 | tf_op jit(solution)/shard_map/all_to_all | solution.py:784
  22.1 134.2 %all-gather.4.cloned.1.call-start = ((), (), s32[]{:S(2)}) async-start(), calls=%async_computation.24 | async-start | bytes 5242880 | tf_op jit(solution)/shard_map/all_gather | solution.py:788
  51.9 162.2 %all-gather.6.cloned.1.call-start = ((), (), s32[]{:S(2)}) async-start(), calls=%async_computation.25 | async-start | bytes 4718592 | tf_op jit(solution)/shard_map/all_gather | solution.py:789
  120.2 36.2 %all-to-all-start.1 = ((bf16[8,64,2048]{2,1,0:T(8,128)(2,1)}), bf16[8,64,2048]{2,1,0:T(8,128)(2,1)S(1)}, u32[]{:S(2)}, u32[]{:S(2)}) async-start(bf16[8,64,2048]{2,1,0:T(8,128)(2,1)} %bitcast.289), calls=%async_computation.1 | async-start | bytes 4194304 | tf_op jit(solution)/shard_map/all_to_all | solution.py:806
  186.2 35.1 %all-to-all-start.2 = ((bf16[8,64,2048]{2,1,0:T(8,128)(2,1)}), bf16[8,64,2048]{2,1,0:T(8,128)(2,1)S(1)}, u32[]{:S(2)}, u32[]{:S(2)}) async-start(bf16[8,64,2048]{2,1,0:T(8,128)(2,1)} %bitcast.293), calls=%async_computation.2 | async-start | bytes 4194304 | tf_op jit(solution)/shard_map/all_to_all | solution.py:806
  190.8 144.7 %reduce-scatter.4.cloned.1.call-start = ((), (), s32[]{:S(2)}) async-start(), calls=%async_computation.26 | async-start | bytes 5242880 | tf_op jit(solution)/shard_map/reduce_scatter | solution.py:880
  191.6 29.7 %collective-permute-start.13 = (bf16[256,2048]{1,0:T(8,128)(2,1)}, bf16[256,2048]{1,0:T(8,128)(2,1)}, u32[]{:S(2)}, u32[]{:S(2)}) collective-permute-start(bf16[256,2048]{1,0:T(8,128)(2,1)} %copy-done.28), channel_id=1, source_target_pairs={{4,2},{2,0},{5,3},{3,1},{12,10},{10,8},{13,11},{11,9},{20,18},{18,... | collective-permute-start | bytes 3145736 | tf_op jit(solution)/shard_map/ppermute | solution.py:76
  255.8 30.2 %all-to-all-start.3 = ((bf16[8,64,2048]{2,1,0:T(8,128)(2,1)}), bf16[8,64,2048]{2,1,0:T(8,128)(2,1)S(1)}, u32[]{:S(2)}, u32[]{:S(2)}) async-start(bf16[8,64,2048]{2,1,0:T(8,128)(2,1)} %bitcast.301), calls=%async_computation.4 | async-start | bytes 4194304 | tf_op jit(solution)/shard_map/all_to_all | solution.py:806
  290.3 30.2 %all-to-all-start.4 = ((bf16[8,64,2048]{2,1,0:T(8,128)(2,1)}), bf16[8,64,2048]{2,1,0:T(8,128)(2,1)S(1)}, u32[]{:S(2)}, u32[]{:S(2)}) async-start(bf16[8,64,2048]{2,1,0:T(8,128)(2,1)} %bitcast.300), calls=%async_computation.5 | async-start | bytes 4194304 | tf_op jit(solution)/shard_map/all_to_all | solution.py:806
  343.0 37.0 %all-to-all-start.6 = ((bf16[8,64,2048]{2,1,0:T(8,128)(2,1)}), bf16[8,64,2048]{2,1,0:T(8,128)(2,1)S(1)}, u32[]{:S(2)}, u32[]{:S(2)}) async-start(bf16[8,64,2048]{2,1,0:T(8,128)(2,1)} %bitcast.297), calls=%async_computation.7 | async-start | bytes 4194304 | tf_op jit(solution)/shard_map/all_to_all | solution.py:806
  381.3 39.9 %all-to-all-start.7 = ((bf16[8,64,2048]{2,1,0:T(8,128)(2,1)}), bf16[8,64,2048]{2,1,0:T(8,128)(2,1)}, u32[]{:S(2)}, u32[]{:S(2)}) async-start(bf16[8,64,2048]{2,1,0:T(8,128)(2,1)} %bitcast.291), calls=%async_computation.8 | async-start | bytes 4194304 | tf_op jit(solution)/shard_map/all_to_all | solution.py:806
  421.2 38.1 %all-to-all-start.8 = ((bf16[8,64,2048]{2,1,0:T(8,128)(2,1)}), bf16[8,64,2048]{2,1,0:T(8,128)(2,1)S(1)}, u32[]{:S(2)}, u32[]{:S(2)}) async-start(bf16[8,64,2048]{2,1,0:T(8,128)(2,1)} %bitcast.292), calls=%async_computation.9 | async-start | bytes 4194304 | tf_op jit(solution)/shard_map/all_to_all | solution.py:806
  460.6 31.0 %all-to-all-start.9 = ((bf16[8,64,2048]{2,1,0:T(8,128)(2,1)}), bf16[8,64,2048]{2,1,0:T(8,128)(2,1)}, u32[]{:S(2)}, u32[]{:S(2)}) async-start(bf16[8,64,2048]{2,1,0:T(8,128)(2,1)} %bitcast.298), calls=%async_computation.10 | async-start | bytes 4194304 | tf_op jit(solution)/shard_map/all_to_all | solution.py:806
  504.2 40.3 %all-to-all-start.10 = ((bf16[8,64,2048]{2,1,0:T(8,128)(2,1)}), bf16[8,64,2048]{2,1,0:T(8,128)(2,1)S(1)}, u32[]{:S(2)}, u32[]{:S(2)}) async-start(bf16[8,64,2048]{2,1,0:T(8,128)(2,1)} %bitcast.312), calls=%async_computation.11 | async-start | bytes 4194304 | tf_op jit(solution)/shard_map/all_to_all | solution.py:806
  549.4 30.9 %all-to-all-start.11 = ((bf16[8,64,2048]{2,1,0:T(8,128)(2,1)}), bf16[8,64,2048]{2,1,0:T(8,128)(2,1)S(1)}, u32[]{:S(2)}, u32[]{:S(2)}) async-start(bf16[8,64,2048]{2,1,0:T(8,128)(2,1)} %bitcast.311), calls=%async_computation.12 | async-start | bytes 4194304 | tf_op jit(solution)/shard_map/all_to_all | solution.py:806
  585.9 31.0 %all-to-all-start.12 = ((bf16[8,64,2048]{2,1,0:T(8,128)(2,1)}), bf16[8,64,2048]{2,1,0:T(8,128)(2,1)S(1)}, u32[]{:S(2)}, u32[]{:S(2)}) async-start(bf16[8,64,2048]{2,1,0:T(8,128)(2,1)} %bitcast.310), calls=%async_computation.13 | async-start | bytes 4194304 | tf_op jit(solution)/shard_map/all_to_all | solution.py:806
  623.0 30.5 %all-to-all-start.13 = ((bf16[8,64,2048]{2,1,0:T(8,128)(2,1)}), bf16[8,64,2048]{2,1,0:T(8,128)(2,1)S(1)}, u32[]{:S(2)}, u32[]{:S(2)}) async-start(bf16[8,64,2048]{2,1,0:T(8,128)(2,1)} %bitcast.309), calls=%async_computation.14 | async-start | bytes 4194304 | tf_op jit(solution)/shard_map/all_to_all | solution.py:806
  626.8 40.0 %collective-permute-start.23 = (bf16[256,2048]{1,0:T(8,128)(2,1)}, bf16[256,2048]{1,0:T(8,128)(2,1)S(1)}, u32[]{:S(2)}, u32[]{:S(2)}) collective-permute-start(bf16[256,2048]{1,0:T(8,128)(2,1)} %get-tuple-element.385), channel_id=1, source_target_pairs={{0,2},{2,4},{4,6},{1,3},{3,5},{5,7},{8,10},{10,12},{12,14},{9,11},... | collective-permute-start | bytes 3145736 | tf_op jit(solution)/shard_map/ppermute | solution.py:102
  631.3 35.6 %collective-permute-start.24 = (bf16[256,2048]{1,0:T(8,128)(2,1)}, bf16[256,2048]{1,0:T(8,128)(2,1)}, u32[]{:S(2)}, u32[]{:S(2)}) collective-permute-start(bf16[256,2048]{1,0:T(8,128)(2,1)} %get-tuple-element.386), channel_id=1, source_target_pairs={{6,4},{4,2},{2,0},{7,5},{5,3},{3,1},{14,12},{12,10},{10,8},{15,13}... | collective-permute-start | bytes 3145736 | tf_op jit(solution)/shard_map/ppermute | solution.py:103
  658.1 133.4 %all-gather.8.cloned.1.call-start = ((), (), s32[]{:S(2)}) async-start(), calls=%async_computation.27 | async-start | bytes 5242880 | tf_op jit(solution)/shard_map/all_gather | solution.py:974
  674.2 30.2 %all-to-all-start.15 = ((bf16[8,64,2048]{2,1,0:T(8,128)(2,1)}), bf16[8,64,2048]{2,1,0:T(8,128)(2,1)S(1)}, u32[]{:S(2)}, u32[]{:S(2)}) async-start(bf16[8,64,2048]{2,1,0:T(8,128)(2,1)} %bitcast.101), calls=%async_computation.16 | async-start | bytes 4194304 | tf_op jit(solution)/shard_map/all_to_all | solution.py:806
  705.8 56.4 %all-to-all-start.16 = ((bf16[8,64,2048]{2,1,0:T(8,128)(2,1)}), bf16[8,64,2048]{2,1,0:T(8,128)(2,1)}, u32[]{:S(2)}, u32[]{:S(2)}) async-start(bf16[8,64,2048]{2,1,0:T(8,128)(2,1)} %bitcast.103), calls=%async_computation.17 | async-start | bytes 4194304 | tf_op jit(solution)/shard_map/all_to_all | solution.py:806
  713.6 48.5 %collective-permute-start.25 = (bf16[256,2048]{1,0:T(8,128)(2,1)}, bf16[256,2048]{1,0:T(8,128)(2,1)S(1)}, u32[]{:S(2)}, u32[]{:S(2)}) collective-permute-start(bf16[256,2048]{1,0:T(8,128)(2,1)} %line_part.12.refs_0_), channel_id=1, source_target_pairs={{0,2},{6,4},{1,3},{7,5},{8,10},{14,12},{9,11},{15,13},{16,18},{22,... | collective-permute-start | bytes 3145736 | tf_op jit(solution)/shard_map/ppermute | solution.py:90
  767.4 46.0 %all-to-all-start.17 = ((bf16[8,64,2048]{2,1,0:T(8,128)(2,1)}), bf16[8,64,2048]{2,1,0:T(8,128)(2,1)S(1)}, u32[]{:S(2)}, u32[]{:S(2)}) async-start(bf16[8,64,2048]{2,1,0:T(8,128)(2,1)} %bitcast.106), calls=%async_computation.18 | async-start | bytes 4194304 | tf_op jit(solution)/shard_map/all_to_all | solution.py:806
  771.5 103.4 %reduce-scatter.6.cloned.1.call-start = ((), (), s32[]{:S(2)}) async-start(), calls=%async_computation.28 | async-start | bytes 4718592 | tf_op jit(solution)/shard_map/reduce_scatter | solution.py:1000
  771.5 41.9 %collective-permute-start.27 = (bf16[256,2048]{1,0:T(8,128)(2,1)}, bf16[256,2048]{1,0:T(8,128)(2,1)S(1)}, u32[]{:S(2)}, u32[]{:S(2)}) collective-permute-start(bf16[256,2048]{1,0:T(8,128)(2,1)} %get-tuple-element.438), channel_id=1, source_target_pairs={{6,4},{4,2},{7,5},{5,3},{14,12},{12,10},{15,13},{13,11},{22,20},{2... | collective-permute-start | bytes 3145736 | tf_op jit(solution)/shard_map/ppermute | solution.py:96
  772.3 41.2 %collective-permute-start.26 = (bf16[256,2048]{1,0:T(8,128)(2,1)}, bf16[256,2048]{1,0:T(8,128)(2,1)}, u32[]{:S(2)}, u32[]{:S(2)}) collective-permute-start(bf16[256,2048]{1,0:T(8,128)(2,1)} %get-tuple-element.438), channel_id=1, source_target_pairs={{0,2},{2,4},{1,3},{3,5},{8,10},{10,12},{9,11},{11,13},{16,18},{18,... | collective-permute-start | bytes 3145736 | tf_op jit(solution)/shard_map/ppermute | solution.py:95
  819.8 50.3 %all-to-all-start.18 = ((bf16[8,64,2048]{2,1,0:T(8,128)(2,1)}), bf16[8,64,2048]{2,1,0:T(8,128)(2,1)S(1)}, u32[]{:S(2)}, u32[]{:S(2)}) async-start(bf16[8,64,2048]{2,1,0:T(8,128)(2,1)} %bitcast.111), calls=%async_computation.19 | async-start | bytes 4194304 | tf_op jit(solution)/shard_map/all_to_all | solution.py:806
  824.0 184.3 %reduce-scatter.8.cloned.1.call-start = ((), (), s32[]{:S(2)}) async-start(), calls=%async_computation.29 | async-start | bytes 5242880 | tf_op jit(solution)/shard_map/reduce_scatter | solution.py:1017
  824.0 45.1 %collective-permute-start.28 = (bf16[256,2048]{1,0:T(8,128)(2,1)}, bf16[256,2048]{1,0:T(8,128)(2,1)S(1)}, u32[]{:S(2)}, u32[]{:S(2)}) collective-permute-start(bf16[256,2048]{1,0:T(8,128)(2,1)} %get-tuple-element.453), channel_id=1, source_target_pairs={{0,2},{2,4},{4,6},{1,3},{3,5},{5,7},{8,10},{10,12},{12,14},{9,11},... | collective-permute-start | bytes 3145736 | tf_op jit(solution)/shard_map/ppermute | solution.py:102
  827.7 42.4 %collective-permute-start.29 = (bf16[256,2048]{1,0:T(8,128)(2,1)}, bf16[256,2048]{1,0:T(8,128)(2,1)}, u32[]{:S(2)}, u32[]{:S(2)}) collective-permute-start(bf16[256,2048]{1,0:T(8,128)(2,1)} %get-tuple-element.454), channel_id=1, source_target_pairs={{6,4},{4,2},{2,0},{7,5},{5,3},{3,1},{14,12},{12,10},{10,8},{15,13}... | collective-permute-start | bytes 3145736 | tf_op jit(solution)/shard_map/ppermute | solution.py:103
  (92 other events, 1149.7 us)
Sparse Core Ops, SparseCore 0:
  52.0 80.2 all-gather.3
  134.8 40.9 all-gather.5
  251.4 74.7 reduce-scatter.3
  674.4 96.8 all-gather.7
  813.6 61.1 reduce-scatter.5
  900.9 104.1 reduce-scatter.7

commit v3 on v2

--- a/solution.py
+++ b/solution.py
@@ -153,11 +153,15 @@
 
 
 CHEAP = pl.CostEstimate(flops=1, bytes_accessed=1, transcendentals=0)
-
-
-def run(kernel, name, grid, operands, in_specs, outs, out_specs, scalars=None, scratch=(), aliases=None):
+DEAR = pl.CostEstimate(flops=10**11, bytes_accessed=1, transcendentals=0)
+
+
+def run(kernel, name, grid, operands, in_specs, outs, out_specs, scalars=None, scratch=(), free=(), dear=False):
     prefetch = () if scalars is None else (scalars,)
-    aliases = {i + len(prefetch): o for i, o in (aliases or {}).items()}
+    operands = [
+        v if i in free else pltpu.with_memory_space_constraint(v, pltpu.HBM)
+        for i, v in enumerate(operands)
+    ]
     got = pl.pallas_call(
         kernel,
         grid_spec=pltpu.PrefetchScalarGridSpec(
@@ -168,11 +172,10 @@
             scratch_shapes=scratch,
         ),
         out_shape=[pltpu.HBM(shape, kind) for shape, kind in outs],
-        input_output_aliases=aliases,
         compiler_params=pltpu.CompilerParams(vmem_limit_bytes=52 * 1024 * 1024),
-        cost_estimate=CHEAP,
+        cost_estimate=DEAR if dear else CHEAP,
         name=name,
-    )(*prefetch, *[pltpu.with_memory_space_constraint(v, pltpu.HBM) for v in operands])
+    )(*prefetch, *operands)
     return got
 
 
@@ -185,7 +188,7 @@
     o_ref[...] = part.astype(o_ref.dtype)
 
 
-def matmul(a, b, kind, steps, by, out=BF):
+def matmul(a, b, kind, steps, by, out=BF, dear=False):
     dims = {"nn": ((1,), (0,)), "nt": ((1,), (1,)), "tn": ((0,), (0,))}[kind]
     rows = a.shape[1 - dims[0][0]]
     columns = b.shape[1 - dims[1][0]]
@@ -212,6 +215,7 @@
         [a_spec, b_spec],
         [((rows, columns), out)],
         [o_spec],
+        dear=dear,
     )[0]
 
 
@@ -239,6 +243,7 @@
         [((slots, width), BF)],
         [pl.BlockSpec((slots, 1024), lambda j, s: (0, j))],
         scalars=scalars,
+        free=(1, 2, 3, 4),
     )[0]
 
 
@@ -275,6 +280,7 @@
         [((tokens, width), BF)] * (1 if step == 0 else 2),
         [tile] * (1 if step == 0 else 2),
         scalars=scalars,
+        free=(1, 2, 3, 4),
     )
 
 
@@ -352,6 +358,33 @@
     )
 
 
+def _pack_kernel(key_ref, value_ref, small_ref, out_ref):
+    for at in range(STEPS):
+        cols = slice(at * HEAD, (at + 1) * HEAD)
+        out_ref[at, :, :HEAD] = key_ref[:, cols]
+        out_ref[at, :, HEAD : 2 * HEAD] = value_ref[:, cols]
+        out_ref[at, :, 2 * HEAD :] = small_ref[...]
+
+
+def pack(key, value, small):
+    rows = small.shape[0]
+    lanes = 2 * HEAD + small.shape[1]
+    return run(
+        _pack_kernel,
+        "pack",
+        (1,),
+        (key, value, small),
+        [full(*key.shape), full(*value.shape), full(*small.shape)],
+        [((STEPS, rows, lanes), BF)],
+        [full(STEPS, rows, lanes)],
+    )[0]
+
+
+def _lane_mean(value):
+    ones = jnp.full((HEAD, HEAD), 1.0 / HEAD, BF)
+    return jnp.dot(value.astype(BF), ones, preferred_element_type=F32)
+
+
 def _project_kernel(
     x_ref, gain_ref, w_ref, cos_ref, sin_ref, qg_ref, kg_ref, n_ref, raw_ref, q_ref, kv_ref
 ):
@@ -365,7 +398,7 @@
     for h in range(heads + 1):
         cols = slice(h * HEAD, (h + 1) * HEAD)
         value = raw_ref[:, cols]
-        factor = lax.rsqrt(jnp.mean(value * value, axis=-1, keepdims=True) + EPS)
+        factor = lax.rsqrt(_lane_mean(value * value) + EPS)
         value = value * factor * (qg_ref[...] if h < heads else kg_ref[...])
         value = (value * cosine + pltpu.roll(value, HEAD // 2, 1) * sine).astype(BF)
         if h < heads:
@@ -396,6 +429,7 @@
             ((tokens, 2 * HEAD), BF),
         ],
         [tile(width), tile(columns), tile(columns - 2 * HEAD), tile(2 * HEAD)],
+        dear=True,
     )
 
 
@@ -412,7 +446,7 @@
     for h in range(heads + 1):
         cols = slice(h * HEAD, (h + 1) * HEAD)
         value = raw_ref[:, cols]
-        factor = lax.rsqrt(jnp.mean(value * value, axis=-1, keepdims=True) + EPS)
+        factor = lax.rsqrt(_lane_mean(value * value) + EPS)
         unit = value * factor
         if h < heads:
             grad = dq_ref[:, cols].astype(F32) * (1.0 / math.sqrt(HEAD))
@@ -426,7 +460,7 @@
         else:
             dkg_ref[...] += gain_grad
             grad = grad * kg_ref[...]
-        shift = jnp.mean(grad * unit, axis=-1, keepdims=True)
+        shift = _lane_mean(grad * unit)
         rg_ref[:, cols] = (factor * (grad - unit * shift)).astype(BF)
     rg_ref[:, (heads + 1) * HEAD :] = dkv_ref[:, HEAD:].astype(BF)
     ng_ref[...] = times_transposed(rg_ref[...], w_ref[...]).astype(BF)
@@ -549,6 +583,7 @@
         [((tokens, width), BF), ((heads, tokens, HEAD), F32)],
         [tile, pl.BlockSpec((heads, rows, HEAD), lambda i, o: (0, i, 0))],
         scalars=table,
+        dear=True,
         scratch=[
             pltpu.VMEM((2 * rows, group), F32),
             pltpu.VMEM((group, HEAD), BF),
@@ -641,6 +676,7 @@
         [((tokens, width), BF)] + [((tokens, 2 * HEAD), F32)] * cores,
         [tile] + [piece] * cores,
         scalars=table,
+        dear=True,
         scratch=[
             pltpu.VMEM((2 * rows, group), F32),
             pltpu.VMEM((group, 2 * HEAD), BF),
@@ -696,6 +732,8 @@
         + [full(width, lanes), full(width, hidden), full(width, hidden)],
         [((count, width), BF)] + [((count, hidden), BF)] * 3 + [((count, 1), F32)],
         [across, thin, thin, thin, column],
+        free=(0,),
+        dear=True,
     )
 
 
@@ -770,23 +808,12 @@
         ],
         axis=1,
     )
-    packed = jnp.concatenate(
-        [
-            key_matrix.reshape(rows_dev, STEPS, HEAD).transpose(1, 0, 2),
-            value_matrix.reshape(rows_dev, STEPS, HEAD).transpose(1, 0, 2),
-            jnp.broadcast_to(small[None], (STEPS, *small.shape)),
-        ],
-        axis=2,
-    )
-    flat = [(b, (b % dps) * (devices // dps) + b // dps) for b in range(devices)]
-    w_back = lax.ppermute(w_out, ALL, flat)
+    packed = pack(key_matrix, value_matrix, small)
+    arrived = lax.all_gather(layer_input, "z", axis=0, tiled=True)
     query_own = from_dps(w_query, dp).reshape(width, own_cols)
     packed = lax.all_to_all(packed, "z", split_axis=0, concat_axis=0, tiled=True)
-    packed, w_back, own_input, order, where_block = hold(
-        packed, w_back, layer_input, order, where_block
-    )
-    arrived = lax.all_gather(own_input, "z", axis=0, tiled=True)
-    w_back = lax.all_gather(w_back, PLANE, axis=0, tiled=True)
+    packed, w_out, order, where_block = hold(packed, w_out, order, where_block)
+    w_back = lax.all_to_all(w_out, "dp", split_axis=0, concat_axis=0, tiled=True)
 
     at_slot = jnp.arange(capacity, dtype=jnp.int32)
     earlier = (jnp.arange(tokens)[:, None] > jnp.arange(tokens)[None, :]).astype(BF)
@@ -815,8 +842,9 @@
     packed = jnp.stack(cores_in_order(packed, c), axis=1).reshape(w_query.shape[0], -1)
     packed = from_dps(packed, dp).reshape(width, -1)
     w_in = cores_in_order(query_own, c)
-    *w_in, packed, ids, upstream_block = hold(*w_in, packed, ids, out_grad)
-    g0 = to_plane(dispatch(zs, own_back, [upstream_block], (0, 0, 0, 0)))
+    *w_in, packed, ids, w_back = hold(*w_in, packed, ids, w_back)
+    w_back = lax.all_to_all(w_back, "z", split_axis=0, concat_axis=0, tiled=True)
+    w_back = lax.all_gather(w_back, PLANE, axis=0, tiled=True)
     rest = packed[:, 2 * HEAD :]
     lanes = rest.shape[1]
     router_all = rest[:, :experts]
@@ -856,36 +884,39 @@
     at_block = [jnp.stack([z, order[i]]) for i in range(STEPS)]
 
     (
-        arrived, upstream_block, w_in, pick, back, slot_chosen, cosine, sine, query_at, opens, table,
-        query_gain_s, key_gain_f, at_block, own_expert, attn_gain_all, moe_gain_all, g0,
+        upstream_block, w_in, pick, back, slot_chosen, cosine, sine, query_at, opens, table,
+        query_gain_s, key_gain_f, at_block, own_expert, attn_gain_all, moe_gain_all, rest,
     ) = hold(
-        arrived, upstream_block, w_in, pick, back, slot_chosen, cosine, sine, query_at, opens, table,
-        query_gain_s, key_gain_f, at_block, own_expert, attn_gain_all, moe_gain_all, g0,
+        out_grad, w_in, pick, back, slot_chosen, cosine, sine, query_at, opens, table,
+        query_gain_s, key_gain_f, at_block, own_expert, attn_gain_all, moe_gain_all, rest,
     )
     g_up, g_down = spread_first(upstream_block)
+    g0 = to_plane(dispatch(zs, back[0], [upstream_block], (0, 0, 0, 0)))
     normed, raw, queries, key_value_rows = project(
         arrived, attn_gain_all, w_in, cosine, sine, query_gain_s, key_gain_f, tokens
     )
     pieces = [key_value_rows, *other_cores(key_value_rows)]
-    pulled0 = matmul(g0, down_w, "nt", 2, "rows", F32)
-    queries, g_up, g_down, pulled0, *pieces = hold(queries, g_up, g_down, pulled0, *pieces)
+    queries, g_up, g_down, g0, *pieces = hold(queries, g_up, g_down, g0, *pieces)
     g_up2, g_down2 = spread_second(g_up, g_down)
     g1 = to_plane(dispatch(zs, back[1], [g_up, g_down], FIRST))
     mixed, log_totals = attend(table, queries, pieces, query_at, opens, tokens)
-    mixed, g1, w_back, g_up2, g_down2 = hold(mixed, g1, w_back, g_up2, g_down2)
+    mixed, w_back, g_up2, g_down2 = hold(mixed, w_back, g_up2, g_down2)
     g_last = spread_third(g_up2, g_down2, z)
-    w_back = w_back.reshape(dps, cores, -1, width).transpose(1, 0, 2, 3).reshape(head_cols, width)
+    w_back = w_back.reshape(dps, cores, STEPS, dps // STEPS, -1, width).transpose(3, 2, 1, 0, 4, 5)
+    w_back = w_back.reshape(head_cols, width)
     attended = matmul(mixed, w_back, "nn", 4, "columns")
-    attended, g1, g_up2, g_down2, g_last = hold(attended, g1, g_up2, g_down2, g_last)
+    attended, g_last, g0, g1, g_up2, g_down2 = hold(attended, g_last, g0, g1, g_up2, g_down2)
     attended = lax.psum_scatter(attended, "z", scatter_dimension=0, tiled=True)
     g2 = to_plane(dispatch(zs, back[2], [g_up, g_down, g_up2, g_down2], SECOND))
+    pulled0 = matmul(g0, down_w, "nt", 2, "rows", F32)
+    g2, g_last, pulled0 = hold(g2, g_last, pulled0)
+    g3 = to_plane(dispatch(zs, back[3], [g_up2, g_down2, g_last], THIRD))
     pulled1 = matmul(g1, down_w, "nt", 2, "rows", F32)
-    g2, g_last, pulled1 = hold(g2, g_last, pulled1)
-    g3 = to_plane(dispatch(zs, back[3], [g_up2, g_down2, g_last], THIRD))
     pulled2 = matmul(g2, down_w, "nt", 2, "rows", F32)
-    g3, pulled2, slot_chosen = hold(g3, pulled2, slot_chosen)
+    g3, pulled1, pulled2, slot_chosen = hold(g3, pulled1, pulled2, slot_chosen)
     slot_chosen = to_plane(slot_chosen)
     slot_chosen = slot_chosen.transpose(1, 0, 2, 3).reshape(STEPS, slots, lanes)
+    slot_chosen = [slot_chosen[i] for i in range(STEPS)]
     pulled3 = matmul(g3, down_w, "nt", 2, "rows", F32)
     attended, pulled3, slot_chosen = hold(attended, pulled3, slot_chosen)
     upstream_slots = [g0, g1, g2, g3]
@@ -932,24 +963,31 @@
         ],
         axis=1,
     ).reshape(experts, capacity)
-    p3, p2, p1, p0 = [matmul(hiddens[i], down_w, "nn", 4, "columns") for i in (3, 2, 1, 0)]
-    b3, d2, p3, p2, p1, p0, centre_back, gates = hold(
-        b3, d2, p3, p2, p1, p0, centre_back, gates
-    )
+    h0, h1, h2, h3 = hiddens
+
+    def produced(value):
+        return matmul(value, down_w, "nn", 2, "columns", dear=True)
+
+    p3 = produced(h3)
+    b3, d2, p3, centre_back, gates, h0, h1, h2 = hold(
+        b3, d2, p3, centre_back, gates, h0, h1, h2
+    )
+    b2 = to_plane(d2)
     (c3,) = line_part(zs, pick[3], b3, tokens)
-    c3, d2 = hold(c3, d2)
     got = sum_first(c3)
-    b2 = to_plane(d2)
-    got, b2, d1 = hold(got, b2, d1)
+    p2 = produced(h2)
+    b2, d1, h1, p2 = hold(b2, d1, h1, p2)
+    b1 = to_plane(d1)
+    p1 = produced(h1)
+    got, b2, p1 = hold(got, b2, p1)
     c2, middle = line_part(zs, pick[2], b2, tokens, 1, (c3, got))
-    middle, c2, d1 = hold(middle, c2, d1)
     s_up, s_down = sum_second(middle)
-    b1 = to_plane(d1)
-    s_up, s_down, b1, centre_back, d0 = hold(s_up, s_down, b1, centre_back, d0)
+    b1, d0, h0 = hold(b1, d0, h0)
+    b0 = to_plane(d0)
+    p0 = produced(h0)
+    s_up, s_down, b1, p0 = hold(s_up, s_down, b1, p0)
     s_up, s_down = line_part(zs, pick[1], b1, tokens, 2, (c2, s_up, s_down))
-    s_up, s_down, d0, centre_back = hold(s_up, s_down, d0, centre_back)
     s_up, s_down = sum_third(s_up, s_down)
-    b0 = to_plane(d0)
     b0, centre_back = hold(b0, centre_back)
     centre_back = lax.all_to_all(centre_back, ALL, split_axis=0, concat_axis=0, tiled=True)
     (c0,) = line_part(zs, pick[0], b0, tokens)
@@ -982,20 +1020,21 @@
     t_got = sum_first(o3)
     o2 = to_plane(p2)
     up_weight_grad = contract_chunks(rows, up_grads)
-    o2, o3, t_got, p1, rows, up_weight_grad = hold(o2, o3, t_got, p1, rows, up_weight_grad)
+    rows, up_weight_grad, up_grads = hold(rows, up_weight_grad, up_grads)
+    gate_weight_grad = contract_chunks(rows, gate_grads)
+    o2, t_got, gate_weight_grad = hold(o2, t_got, gate_weight_grad)
     o2, middle = line_part(zs, pick[2], o2, tokens, 1, (o3, t_got))
     middle, o2, p1 = hold(middle, o2, p1)
     t_up, t_down = sum_second(middle)
     o1 = to_plane(p1)
-    gate_weight_grad = contract_chunks(rows, gate_grads)
-    resid_all, o2, gate_weight_grad = hold(resid_all, o2, gate_weight_grad)
-    mixed_grad = matmul(resid_all, w_back, "nt", 4, "rows")
+    resid_all, o2 = hold(resid_all, o2)
+    mixed_grad = matmul(resid_all, w_back, "nt", 4, "rows", dear=True)
     mixed_grad, resid_all = hold(mixed_grad, resid_all)
     out_weight_grad = matmul(mixed, resid_all, "tn", 4, "columns")
-    out_weight_grad = out_weight_grad.reshape(cores, dps, -1, width).transpose(1, 0, 2, 3)
-    out_weight_grad = out_weight_grad.reshape(head_cols, width)
-    mixed_grad, t_up, t_down, o1, o2, p0, out_weight_grad = hold(
-        mixed_grad, t_up, t_down, o1, o2, p0, out_weight_grad
+    out_weight_grad = out_weight_grad.reshape(dps // STEPS, STEPS, cores, dps, -1, width)
+    out_weight_grad = out_weight_grad.transpose(3, 2, 1, 0, 4, 5).reshape(head_cols, width)
+    out_weight_grad, mixed_grad, t_up, t_down, o1 = hold(
+        out_weight_grad, mixed_grad, t_up, t_down, o1
     )
     out_weight_grad = lax.psum_scatter(out_weight_grad, PLANE, scatter_dimension=0, tiled=True)
     t_up, t_down = line_part(zs, pick[1], o1, tokens, 2, (o2, t_up, t_down))
@@ -1005,33 +1044,21 @@
     query_grads, *sums = attend_back(
         table, queries, mixed_grad, mixed, log_totals, pieces, query_at, opens, tokens
     )
-    query_grads, t_up, t_down, o0, out_weight_grad, *sums = hold(
-        query_grads, t_up, t_down, o0, out_weight_grad, *sums
-    )
-    out_weight_grad = lax.ppermute(out_weight_grad, ALL, [(b, a) for a, b in flat]).astype(F32)
+    query_grads, t_up, t_down, o0, *sums = hold(query_grads, t_up, t_down, o0, *sums)
     sums = sum_over_cores(sums)
     normed_grad, raw_grad, query_gain_grad, key_gain_grad = project_back(
         raw, query_grads, sums, w_in, cosine, sine, query_gain_f, key_gain_f, tokens
     )
-    normed_grad, raw_grad, o0, out_weight_grad = hold(normed_grad, raw_grad, o0, out_weight_grad)
+    normed_grad, raw_grad = hold(normed_grad, raw_grad)
     normed_sum = lax.psum_scatter(normed_grad, "z", scatter_dimension=0, tiled=True)
     in_grad = matmul(normed, raw_grad, "tn", 4, "rows")
-    inputs = arrived.astype(F32)
-    input_factor = lax.rsqrt(jnp.mean(inputs * inputs, axis=-1, keepdims=True) + EPS)
-    attn_gain_grad = jnp.sum(normed_grad.astype(F32) * inputs * input_factor, axis=0)[None, :]
     query_share = sum_over_cores(by_core(in_grad[:, :head_cols], 1)).astype(BF)
     key_value_grad = in_grad[:, head_cols:].reshape(dps, STEPS, cores, rows_dev, 2 * HEAD)
     key_value_grad = sum_over_cores(
         [part[:, :, 0] for part in by_core(key_value_grad, 2)]
     ).astype(BF)
-    query_share, key_value_grad, o0, attn_gain_grad = hold(
-        query_share, key_value_grad, o0, attn_gain_grad
-    )
-    query_weight_grad = over_dps(query_share.reshape(dps, -1, own_cols), dp)
-    key_value_grad = over_dps(key_value_grad, dp).astype(BF)
-    (o0,) = line_part(zs, pick[0], o0, tokens)
-    output = resid + (o0.astype(F32) + t_up.astype(F32) + t_down.astype(F32))
-    output = output.astype(BF)
+    attn_gain_grad = jnp.sum(normed_grad.astype(F32) * normed.astype(F32), axis=0)[None, :]
+    attn_gain_grad = attn_gain_grad / attn_gain_all
 
     def to_owners(value):
         columns = value.shape[0]
@@ -1046,10 +1073,26 @@
         ],
         axis=1,
     )
-    late = jnp.sum(lax.all_to_all(late, ALL, split_axis=0, concat_axis=0, tiled=True), axis=0)
+    late = lax.all_to_all(late, ALL, split_axis=0, concat_axis=0, tiled=True)
+    late, out_weight_grad, o0, query_share, key_value_grad = hold(
+        late, out_weight_grad, o0, query_share, key_value_grad
+    )
+    query_weight_grad = over_dps(query_share.reshape(dps, -1, own_cols), dp)
+    key_value_grad = over_dps(key_value_grad, dp).astype(BF)
+    out_weight_grad = lax.all_to_all(out_weight_grad, "z", split_axis=0, concat_axis=0, tiled=True)
+    (o0,) = line_part(zs, pick[0], o0, tokens)
+    output = resid + (o0.astype(F32) + t_up.astype(F32) + t_down.astype(F32))
+    output = output.astype(BF)
+    late = jnp.sum(late, axis=0)
+    out_weight_grad, key_value_grad, output, late, query_weight_grad = hold(
+        out_weight_grad, key_value_grad, output, late, query_weight_grad
+    )
     gain_sums = late[-2 * HEAD :].reshape(2, HEAD)
     owned = late[: -2 * HEAD].reshape(experts + 2, rows_dev)
     key_value_grad = lax.all_to_all(key_value_grad, "z", split_axis=0, concat_axis=0, tiled=True)
+    key_value_grad, out_weight_grad = hold(key_value_grad, out_weight_grad)
+    out_weight_grad = lax.all_to_all(out_weight_grad, "dp", split_axis=0, concat_axis=0, tiled=True)
+    out_weight_grad = out_weight_grad.astype(F32)
     key_value_grad = key_value_grad.transpose(1, 0, 2).astype(F32)
     key_weight_grad = key_value_grad[:, :, :HEAD].reshape(rows_dev, -1)
     value_weight_grad = key_value_grad[:, :, HEAD:].reshape(rows_dev, -1)

time: 1030 us -> 960 us (0.932)
  waiting for transfers between devices: 353 us -> 306 us
  Pallas kernels: 340 us -> 328 us
    ppermute x2, waiting for transfers between devices: 55.2 us -> 20.9 us  [sum_first(): return lax.ppermute(third, 'z', [(0, 1), (3, 2)])]
    all_to_all x1, waiting for transfers between devices: 28.4 us -> 0.01 us  [body(): lax.all_to_all(packed, 'z', split_axis=0, concat_axis=0, tiled=True)]
    all_to_all x1 -> x5, starting transfers between devices: 2.59 us -> 24.2 us  [the longest x1 6.93 us: body(): late = lax.all_to_all(late, ALL, split_axis=0, concat_axis=0, tiled=True)]
    ppermute x2, waiting for transfers between devices: 22.4 us -> 1.46 us  [sum_second(): lax.ppermute(middle, 'z', [(0, 1), (1, 2)])]
    all_to_all x1 -> x5, waiting for transfers between devices: 16.3 us -> 37 us  [the longest x1 20.6 us: body(): late = lax.all_to_all(late, ALL, split_axis=0, concat_axis=0, tiled=True)]
    all_gather x1, waiting for transfers between devices: 0.01 us -> 19.3 us  [body(): w_back = lax.all_gather(w_back, PLANE, axis=0, tiled=True)]
    ppermute x2, waiting for transfers between devices: 21.4 us -> 4.18 us  [spread_first(): lax.ppermute(block, 'z', [(1, 0), (2, 1), (3, 2)])]
    ppermute x6, waiting for transfers between devices: 29.8 us -> 14.8 us  [from_dps(): got = lax.ppermute(value, 'dp', [(i, i ^ k) for i in range(dps)])]
  transfers between devices with their start and end apart: 67 -> 69, of which waited for: 29 -> 32; matrix products, arithmetic and copies ran while one was open for 10% -> 10% of each run, Pallas kernels for 27% -> 31%
where the time goes in v3:
time: 960 us; the launch traced here: 948 us
  Pallas kernels  328 us (34%)
  waiting for transfers between devices  306 us (32%)
  starting transfers between devices  172 us (18%)
  local copies, waits for them, and re-layouts  61.5 us (6%)
  other arithmetic  45.5 us (5%)
  between operations  30.7 us (3%)
    pallas_call x43, Pallas kernels, run(): pl.pallas_call(kernel, grid_spec=pltpu.PrefetchScalarGridSpec(num_scalar_...  328 us
    all_to_all x17, waiting for transfers between devices, to_plane(): return lax.all_to_all(rows, PLANE, split_axis=0, concat_axis=0, tiled=True)  126 us
    all_to_all x17, starting transfers between devices, to_plane(): return lax.all_to_all(rows, PLANE, split_axis=0, concat_axis=0, tiled=True)  67.8 us
    ppermute x2, waiting for transfers between devices, sum_first(): return lax.ppermute(third, 'z', [(0, 1), (3, 2)])  20.9 us
    ppermute x2, waiting for transfers between devices, spread_third(): return lax.ppermute(jnp.where(z == 2, up2, down2), 'z', [(2, 3), (1, 0)])  20.7 us
    all_to_all x1, waiting for transfers between devices, body(): late = lax.all_to_all(late, ALL, split_axis=0, concat_axis=0, tiled=True)  20.6 us
    all_gather x1, waiting for transfers between devices, body(): w_back = lax.all_gather(w_back, PLANE, axis=0, tiled=True)  19.3 us
  transfers between devices with their start and end apart: 69, of which 32 were waited for; matrix products, arithmetic and copies ran while one was open for 10% of the time, Pallas kernels for 31%

profile of v3, /device:TPU:0, one launch (start us, length us, event | category | flops | bytes accessed | tf_op | source)
XLA Modules:
  0.0 948.3 jit_solution(14911416277269030688)
XLA Ops:
  55.7 14.2 %collective-permute-done.6 = bf16[512,384]{1,0:T(8,128)(2,1)S(1)} collective-permute-done((bf16[512,384]{1,0:T(8,128)(2,1)S(1)}, bf16[512,384]{1,0:T(8,128)(2,1)S(1)}, u32[]{:S(2)}, u32[]{:S(2)}) %collective-permute-start.6) | collective-permute-done | bytes 393248 | tf_op jit(solution)/shard_map/ppermute | solution.py:121
  104.4 8.8 all-to-all-done.3
  123.9 13.3 %project.1 = (bf16[1024,2048]{1,0:T(8,128)(2,1)}, f32[1024,1280]{1,0:T(8,128)}, bf16[1024,1024]{1,0:T(8,128)(2,1)}, bf16[1024,256]{1,0:T(8,128)(2,1)}) custom-call(bf16[1024,2048]{1,0:T(8,128)(2,1)} %all-gather.4.cloned.1.call-done.x_ref, f32[1,2048]{1,0:T(1,128)} %bitcast.324, bf16[2048,1280]{1,0:T(8,128)(2,1)} %pad_maximum_fusion.w_ref, ...), custom_call_target="tpu_custom_call" | custom-call | flops 99999997952 | bytes 1 | tf_op jit(solution)/shard_map/project/pallas_call | solution.py:165
  154.4 19.1 %attend.1 = (bf16[1024,1024]{1,0:T(8,128)(2,1)}, f32[8,1024,128]{2,1,0:T(8,128)}) custom-call(s32[8]{0:T(128)S(1)} %pad_add_fusion.table, bf16[1024,256]{1,0:T(8,128)(2,1)} %get-tuple-element.270.refs_0_, bf16[1024,256]{1,0:T(8,128)(2,1)} %collective-permute-done.10.refs_1_, bf16[1024,1024]{1,0:T(8,128)(2,1)} %get-tuple-element.272.refs_2_, ...), custom_call_target="tpu_custom_call" | custom-call | flops 99999997952 | bytes 1 | tf_op jit(solution)/shard_map/attend/pallas_call | solution.py:165
  173.6 19.3 %all-gather.6.cloned.1.call-done = bf16[1024,2048]{1,0:T(8,128)(2,1)} async-done(((bf16[128,2048]{1,0:T(8,128)(2,1)}), bf16[1024,2048]{1,0:T(8,128)(2,1)}) %all-gather.6.cloned.1.call-update) | async-done | bytes 4194320 | tf_op jit(solution)/shard_map/all_gather | solution.py:847
  200.2 8.4 matmul_nn.5
  208.5 13.2 %collective-permute-done.13.refs_2_ = bf16[256,2048]{1,0:T(8,128)(2,1)} collective-permute-done((bf16[256,2048]{1,0:T(8,128)(2,1)}, bf16[256,2048]{1,0:T(8,128)(2,1)}, u32[]{:S(2)}, u32[]{:S(2)}) %collective-permute-start.13) | collective-permute-done | bytes 1048608 | tf_op jit(solution)/shard_map/ppermute | solution.py:81
  234.7 21.3 %all-to-all-done.5 = bf16[8,64,2048]{2,1,0:T(8,128)(2,1)S(1)} async-done(((bf16[8,64,2048]{2,1,0:T(8,128)(2,1)}), bf16[8,64,2048]{2,1,0:T(8,128)(2,1)S(1)}, u32[]{:S(2)}, u32[]{:S(2)}) %all-to-all-start.5) | async-done | bytes 2097184 | tf_op jit(solution)/shard_map/all_to_all | solution.py:833
  274.0 16.2 %all-to-all-done.6 = bf16[8,64,2048]{2,1,0:T(8,128)(2,1)S(1)} async-done(((bf16[8,64,2048]{2,1,0:T(8,128)(2,1)}), bf16[8,64,2048]{2,1,0:T(8,128)(2,1)S(1)}, u32[]{:S(2)}, u32[]{:S(2)}) %all-to-all-start.6) | async-done | bytes 2097184 | tf_op jit(solution)/shard_map/all_to_all | solution.py:833
  329.3 13.4 %collective-permute-done.14.refs_0_ = bf16[256,2048]{1,0:T(8,128)(2,1)S(1)} collective-permute-done((bf16[256,2048]{1,0:T(8,128)(2,1)S(1)}, bf16[256,2048]{1,0:T(8,128)(2,1)S(1)}, u32[]{:S(2)}, u32[]{:S(2)}) %collective-permute-start.14) | collective-permute-done | bytes 1048608 | tf_op jit(solution)/shard_map/ppermute | solution.py:68
  357.1 12.6 %expert.4 = (bf16[512,2048]{1,0:T(8,128)(2,1)}, bf16[512,768]{1,0:T(8,128)(2,1)}, bf16[512,768]{1,0:T(8,128)(2,1)}, bf16[512,768]{1,0:T(8,128)(2,1)}, f32[512,1]{1,0:T(8,128)}) custom-call(bf16[512,2048]{1,0:T(8,128)(2,1)} %bitcast.72.x_ref.refs_0_, f32[512,768]{1,0:T(8,128)} %matmul_nt.5.pulled_ref, bf16[512,128]{1,0:T(8,128)(2,1)} %bitcast.321, ...), custom_call_target="tpu_custom_call" | custom-call | flops 99999997952 | bytes 1 | tf_op jit(solution)/shard_map/expert/pallas_call | solution.py:165
  369.7 11.2 %collective-permute-done.17.refs_3_.refs_1_ = bf16[256,2048]{1,0:T(8,128)(2,1)S(1)} collective-permute-done((bf16[256,2048]{1,0:T(8,128)(2,1)}, bf16[256,2048]{1,0:T(8,128)(2,1)S(1)}, u32[]{:S(2)}, u32[]{:S(2)}) %collective-permute-start.17) | collective-permute-done | bytes 1048608 | tf_op jit(solution)/shard_map/ppermute | solution.py:76
  392.6 12.7 %expert.5 = (bf16[512,2048]{1,0:T(8,128)(2,1)}, bf16[512,768]{1,0:T(8,128)(2,1)}, bf16[512,768]{1,0:T(8,128)(2,1)}, bf16[512,768]{1,0:T(8,128)(2,1)}, f32[512,1]{1,0:T(8,128)}) custom-call(bf16[512,2048]{1,0:T(8,128)(2,1)} %bitcast.76.x_ref.refs_1_, f32[512,768]{1,0:T(8,128)} %matmul_nt.6.pulled_ref, bf16[512,128]{1,0:T(8,128)(2,1)} %bitcast.320, ...), custom_call_target="tpu_custom_call" | custom-call | flops 99999997952 | bytes 1 | tf_op jit(solution)/shard_map/expert/pallas_call | solution.py:165
  424.9 12.6 %expert.6 = (bf16[512,2048]{1,0:T(8,128)(2,1)}, bf16[512,768]{1,0:T(8,128)(2,1)}, bf16[512,768]{1,0:T(8,128)(2,1)}, bf16[512,768]{1,0:T(8,128)(2,1)}, f32[512,1]{1,0:T(8,128)}) custom-call(bf16[512,2048]{1,0:T(8,128)(2,1)} %bitcast.258, f32[512,768]{1,0:T(8,128)} %matmul_nt.7.pulled_ref, bf16[512,128]{1,0:T(8,128)(2,1)} %bitcast.319, ...), custom_call_target="tpu_custom_call" | custom-call | flops 99999997952 | bytes 1 | tf_op jit(solution)/shard_map/expert/pallas_call | solution.py:165
  437.5 14.0 %all-to-all-done.11 = bf16[8,64,2048]{2,1,0:T(8,128)(2,1)} async-done(((bf16[8,64,2048]{2,1,0:T(8,128)(2,1)}), bf16[8,64,2048]{2,1,0:T(8,128)(2,1)}, u32[]{:S(2)}, u32[]{:S(2)}) %all-to-all-start.11) | async-done | bytes 2097184 | tf_op jit(solution)/shard_map/all_to_all | solution.py:833
  451.6 12.6 %expert.7 = (bf16[512,2048]{1,0:T(8,128)(2,1)}, bf16[512,768]{1,0:T(8,128)(2,1)}, bf16[512,768]{1,0:T(8,128)(2,1)}, bf16[512,768]{1,0:T(8,128)(2,1)}, f32[512,1]{1,0:T(8,128)}) custom-call(bf16[512,2048]{1,0:T(8,128)(2,1)} %bitcast.80.x_ref.refs_3_, f32[512,768]{1,0:T(8,128)} %matmul_nt.8.pulled_ref, bf16[512,128]{1,0:T(8,128)(2,1)} %bitcast.318, ...), custom_call_target="tpu_custom_call" | custom-call | flops 99999997952 | bytes 1 | tf_op jit(solution)/shard_map/expert/pallas_call | solution.py:165
  479.6 14.8 %all-to-all-done.12 = bf16[8,64,2048]{2,1,0:T(8,128)(2,1)S(1)} async-done(((bf16[8,64,2048]{2,1,0:T(8,128)(2,1)}), bf16[8,64,2048]{2,1,0:T(8,128)(2,1)S(1)}, u32[]{:S(2)}, u32[]{:S(2)}) %all-to-all-start.12) | async-done | bytes 2097184 | tf_op jit(solution)/shard_map/all_to_all | solution.py:833
  514.0 12.9 %all-to-all-done.13 = bf16[8,64,2048]{2,1,0:T(8,128)(2,1)} async-done(((bf16[8,64,2048]{2,1,0:T(8,128)(2,1)}), bf16[8,64,2048]{2,1,0:T(8,128)(2,1)}, u32[]{:S(2)}, u32[]{:S(2)}) %all-to-all-start.13) | async-done | bytes 2097184 | tf_op jit(solution)/shard_map/all_to_all | solution.py:833
  548.1 9.0 all-to-all-done.14
  597.1 11.1 %all-to-all-done.16 = f32[32,1,64]{2,1,0:T(1,128)S(1)} async-done(((f32[32,1,64]{2,1,0:T(1,128)}), f32[32,1,64]{2,1,0:T(1,128)S(1)}, u32[]{:S(2)}, u32[]{:S(2)}) %all-to-all-start.16) | async-done | bytes 8224 | tf_op jit(solution)/shard_map/all_to_all | solution.py:992
  621.2 13.1 %contract_chunks.3 = f32[768,2048]{1,0:T(8,128)} custom-call(bf16[512,768]{1,0:T(8,128)(2,1)} %get-tuple-element.401.a_ref.refs_0_, bf16[512,768]{1,0:T(8,128)(2,1)} %get-tuple-element.402.a_ref.refs_1_, bf16[512,768]{1,0:T(8,128)(2,1)} %get-tuple-element.403.a_ref.refs_2_, bf16[512,768]{1,0:T(8,128)(2,1)} %get-tuple-element.404.a_ref.refs_3_, ...), custom_call_target="tpu_custom_call" | custom-call | flops 1 | bytes 1 | tf_op jit(solution)/shard_map/contract_chunks/pallas_call | solution.py:165
  635.3 12.5 %all-to-all-done.17 = bf16[8,64,2048]{2,1,0:T(8,128)(2,1)S(1)} async-done(((bf16[8,64,2048]{2,1,0:T(8,128)(2,1)}), bf16[8,64,2048]{2,1,0:T(8,128)(2,1)S(1)}, u32[]{:S(2)}, u32[]{:S(2)}) %all-to-all-start.17) | async-done | bytes 2097184 | tf_op jit(solution)/shard_map/all_to_all | solution.py:833
  659.4 13.0 %contract_chunks.4 = f32[2048,768]{1,0:T(8,128)} custom-call(bf16[512,2048]{1,0:T(8,128)(2,1)} %bitcast.72.x_ref.refs_0_, bf16[512,2048]{1,0:T(8,128)(2,1)} %bitcast.76.x_ref.refs_1_, bf16[512,2048]{1,0:T(8,128)(2,1)} %bitcast.259, bf16[512,2048]{1,0:T(8,128)(2,1)} %bitcast.80.x_ref.refs_3_, bf16[512,768]{1,0:T(8,128)(2,1)} %get-tuple-element.416.refs_4_, ...), custom_call_target="tpu_custom_call" | custom-call | flops 1 | bytes 1 | tf_op jit(solution)/shard_map/contract_chunks/pallas_call | solution.py:165
  672.4 13.1 %contract_chunks.5 = f32[2048,768]{1,0:T(8,128)} custom-call(bf16[512,2048]{1,0:T(8,128)(2,1)} %bitcast.72.x_ref.refs_0_, bf16[512,2048]{1,0:T(8,128)(2,1)} %bitcast.76.x_ref.refs_1_, bf16[512,2048]{1,0:T(8,128)(2,1)} %bitcast.260, bf16[512,2048]{1,0:T(8,128)(2,1)} %bitcast.80.x_ref.refs_3_, bf16[512,768]{1,0:T(8,128)(2,1)} %get-tuple-element.424.refs_4_, ...), custom_call_target="tpu_custom_call" | custom-call | flops 1 | bytes 1 | tf_op jit(solution)/shard_map/contract_chunks/pallas_call | solution.py:165
  685.4 19.0 %collective-permute-done.24.refs_1_ = bf16[256,2048]{1,0:T(8,128)(2,1)} collective-permute-done((bf16[256,2048]{1,0:T(8,128)(2,1)}, bf16[256,2048]{1,0:T(8,128)(2,1)}, u32[]{:S(2)}, u32[]{:S(2)}) %collective-permute-start.24) | collective-permute-done | bytes 1048608 | tf_op jit(solution)/shard_map/ppermute | solution.py:90
  720.8 8.6 matmul_nt.9.refs_3_
  729.5 8.5 matmul_tn.2
  760.5 40.2 %attend_back.1 = (bf16[1024,1024]{1,0:T(8,128)(2,1)}, f32[1024,256]{1,0:T(8,128)}, f32[1024,256]{1,0:T(8,128)}) custom-call(s32[8]{0:T(128)S(1)} %pad_add_fusion.table, bf16[1024,256]{1,0:T(8,128)(2,1)} %get-tuple-element.270.refs_0_, bf16[1024,256]{1,0:T(8,128)(2,1)} %collective-permute-done.10.refs_1_, bf16[1024,1024]{1,0:T(8,128)(2,1)} %get-tuple-element.272.refs_2_, ...), custom_call_target="tpu_custom_call" | custom-call | flops 99999997952 | bytes 1 | tf_op jit(solution)/shard_map/attend_back/pallas_call | solution.py:165
  806.0 14.1 %project_back.1 = (bf16[1024,2048]{1,0:T(8,128)(2,1)}, bf16[1024,1280]{1,0:T(8,128)(2,1)}, f32[1,128]{1,0:T(1,128)}, f32[1,128]{1,0:T(1,128)}) custom-call(f32[1024,1280]{1,0:T(8,128)} %get-tuple-element.408.raw_ref, bf16[1024,1024]{1,0:T(8,128)(2,1)} %get-tuple-element.454.dq_ref, f32[1024,256]{1,0:T(8,128)} %add.206.dkv_ref, ...), custom_call_target="tpu_custom_call" | custom-call | flops 1 | bytes 1 | tf_op jit(solution)/shard_map/project_back/pallas_call | solution.py:165
  820.2 9.8 %matmul_tn.3 = bf16[2048,1280]{1,0:T(8,128)(2,1)} custom-call(bf16[1024,2048]{1,0:T(8,128)(2,1)} %get-tuple-element.460.a_ref, bf16[1024,1280]{1,0:T(8,128)(2,1)} %get-tuple-element.465.b_ref), custom_call_target="tpu_custom_call" | custom-call | flops 1 | bytes 1 | tf_op jit(solution)/shard_map/matmul_tn/pallas_call | solution.py:165
  849.7 20.6 %all-to-all-done.21 = f32[32,1,2432]{2,1,0:T(1,128)S(1)} async-done(((f32[32,1,2432]{2,1,0:T(1,128)}), f32[32,1,2432]{2,1,0:T(1,128)S(1)}, u32[]{:S(2)}, u32[]{:S(2)}) %all-to-all-start.21) | async-done | bytes 311328 | tf_op jit(solution)/shard_map/all_to_all | solution.py:1076
  894.0 13.5 %collective-permute-done.33 = bf16[4,64,256]{2,1,0:T(8,128)(2,1)} collective-permute-done((bf16[4,64,256]{2,1,0:T(8,128)(2,1)}, bf16[4,64,256]{2,1,0:T(8,128)(2,1)}, u32[]{:S(2)}, u32[]{:S(2)}) %collective-permute-start.33) | collective-permute-done | bytes 131104 | tf_op jit(solution)/shard_map/ppermute | solution.py:112
  (437 shorter events, 460.9 us)
Async XLA Ops:
  23.5 100.4 %all-gather.4.cloned.1.call-start = ((), (), s32[]{:S(2)}) async-start(), calls=%async_computation.28 | async-start | bytes 5242880 | tf_op jit(solution)/shard_map/all_gather | solution.py:812
  37.5 32.5 %collective-permute-start.3 = (bf16[2048,512]{1,0:T(8,128)(2,1)}, bf16[2048,512]{1,0:T(8,128)(2,1)}, u32[]{:S(2)}, u32[]{:S(2)}) collective-permute-start(bf16[2048,512]{1,0:T(8,128)(2,1)} %bitcast.4), channel_id=1, source_target_pairs={{1,0},{0,1},{3,2},{2,3},{5,4},{4,5},{7,6},{6,7},{9,8},{8,9},{11,10... | collective-permute-start | bytes 6291464 | tf_op jit(solution)/shard_map/ppermute | solution.py:129
  81.5 31.8 %all-to-all-start.3 = ((bf16[4,32,2048]{2,1,0:T(8,128)(2,1)}), bf16[4,32,2048]{2,1,0:T(8,128)(2,1)}, u32[]{:S(2)}, u32[]{:S(2)}) async-start(bf16[4,32,2048]{2,1,0:T(8,128)(2,1)} %bitcast.54), calls=%async_computation.3 | async-start | bytes 1048576 | tf_op jit(solution)/shard_map/all_to_all | solution.py:846
  95.7 43.6 %collective-permute-start.8 = (bf16[256,2048]{1,0:T(8,128)(2,1)S(1)}, bf16[256,2048]{1,0:T(8,128)(2,1)S(1)}, u32[]{:S(2)}, u32[]{:S(2)}) collective-permute-start(bf16[256,2048]{1,0:T(8,128)(2,1)S(1)} %copy-done.10), channel_id=1, source_target_pairs={{0,2},{2,4},{4,6},{1,3},{3,5},{5,7},{8,10},{10,12},{12,14},{9,11},... | collective-permute-start | bytes 3145736 | tf_op jit(solution)/shard_map/ppermute | solution.py:68
  99.7 39.6 %collective-permute-start.9 = (bf16[256,2048]{1,0:T(8,128)(2,1)S(1)}, bf16[256,2048]{1,0:T(8,128)(2,1)S(1)}, u32[]{:S(2)}, u32[]{:S(2)}) collective-permute-start(bf16[256,2048]{1,0:T(8,128)(2,1)S(1)} %copy-done.10), channel_id=1, source_target_pairs={{2,0},{4,2},{6,4},{3,1},{5,3},{7,5},{10,8},{12,10},{14,12},{11,9},... | collective-permute-start | bytes 3145736 | tf_op jit(solution)/shard_map/ppermute | solution.py:69
  113.3 31.0 %all-to-all-start.2 = ((bf16[8,64,2048]{2,1,0:T(8,128)(2,1)}), bf16[8,64,2048]{2,1,0:T(8,128)(2,1)}, u32[]{:S(2)}, u32[]{:S(2)}) async-start(bf16[8,64,2048]{2,1,0:T(8,128)(2,1)} %bitcast.278), calls=%async_computation.2 | async-start | bytes 4194304 | tf_op jit(solution)/shard_map/all_to_all | solution.py:833
  117.6 75.2 %all-gather.6.cloned.1.call-start = ((), (), s32[]{:S(2)}) async-start(), calls=%async_computation.29 | async-start | bytes 4718592 | tf_op jit(solution)/shard_map/all_gather | solution.py:847
  150.0 58.6 %all-to-all-start.4 = ((bf16[8,64,2048]{2,1,0:T(8,128)(2,1)}), bf16[8,64,2048]{2,1,0:T(8,128)(2,1)}, u32[]{:S(2)}, u32[]{:S(2)}) async-start(bf16[8,64,2048]{2,1,0:T(8,128)(2,1)} %bitcast.284), calls=%async_computation.4 | async-start | bytes 4194304 | tf_op jit(solution)/shard_map/all_to_all | solution.py:833
  154.3 150.7 %reduce-scatter.4.cloned.1.call-start = ((), (), s32[]{:S(2)}) async-start(), calls=%async_computation.30 | async-start | bytes 5242880 | tf_op jit(solution)/shard_map/reduce_scatter | solution.py:909
  225.8 30.2 %all-to-all-start.5 = ((bf16[8,64,2048]{2,1,0:T(8,128)(2,1)}), bf16[8,64,2048]{2,1,0:T(8,128)(2,1)S(1)}, u32[]{:S(2)}, u32[]{:S(2)}) async-start(bf16[8,64,2048]{2,1,0:T(8,128)(2,1)} %bitcast.288), calls=%async_computation.6 | async-start | bytes 4194304 | tf_op jit(solution)/shard_map/all_to_all | solution.py:833
  313.7 39.0 %all-to-all-start.8 = ((bf16[8,64,2048]{2,1,0:T(8,128)(2,1)}), bf16[8,64,2048]{2,1,0:T(8,128)(2,1)}, u32[]{:S(2)}, u32[]{:S(2)}) async-start(bf16[8,64,2048]{2,1,0:T(8,128)(2,1)} %bitcast.277), calls=%async_computation.9 | async-start | bytes 4194304 | tf_op jit(solution)/shard_map/all_to_all | solution.py:833
  352.8 35.8 %all-to-all-start.9 = ((bf16[8,64,2048]{2,1,0:T(8,128)(2,1)}), bf16[8,64,2048]{2,1,0:T(8,128)(2,1)}, u32[]{:S(2)}, u32[]{:S(2)}) async-start(bf16[8,64,2048]{2,1,0:T(8,128)(2,1)} %bitcast.280), calls=%async_computation.10 | async-start | bytes 4194304 | tf_op jit(solution)/shard_map/all_to_all | solution.py:833
  388.6 30.6 %all-to-all-start.10 = ((bf16[8,64,2048]{2,1,0:T(8,128)(2,1)}), bf16[8,64,2048]{2,1,0:T(8,128)(2,1)S(1)}, u32[]{:S(2)}, u32[]{:S(2)}) async-start(bf16[8,64,2048]{2,1,0:T(8,128)(2,1)} %bitcast.282), calls=%async_computation.11 | async-start | bytes 4194304 | tf_op jit(solution)/shard_map/all_to_all | solution.py:833
  420.5 31.0 %all-to-all-start.11 = ((bf16[8,64,2048]{2,1,0:T(8,128)(2,1)}), bf16[8,64,2048]{2,1,0:T(8,128)(2,1)}, u32[]{:S(2)}, u32[]{:S(2)}) async-start(bf16[8,64,2048]{2,1,0:T(8,128)(2,1)} %bitcast.286), calls=%async_computation.12 | async-start | bytes 4194304 | tf_op jit(solution)/shard_map/all_to_all | solution.py:833
  495.8 31.2 %all-to-all-start.13 = ((bf16[8,64,2048]{2,1,0:T(8,128)(2,1)}), bf16[8,64,2048]{2,1,0:T(8,128)(2,1)}, u32[]{:S(2)}, u32[]{:S(2)}) async-start(bf16[8,64,2048]{2,1,0:T(8,128)(2,1)} %bitcast.302), calls=%async_computation.14 | async-start | bytes 4194304 | tf_op jit(solution)/shard_map/all_to_all | solution.py:833
  558.5 31.0 %all-to-all-start.15 = ((bf16[8,64,2048]{2,1,0:T(8,128)(2,1)}), bf16[8,64,2048]{2,1,0:T(8,128)(2,1)}, u32[]{:S(2)}, u32[]{:S(2)}) async-start(bf16[8,64,2048]{2,1,0:T(8,128)(2,1)} %bitcast.297), calls=%async_computation.16 | async-start | bytes 4194304 | tf_op jit(solution)/shard_map/all_to_all | solution.py:833
  574.4 35.4 %collective-permute-start.22 = (bf16[256,2048]{1,0:T(8,128)(2,1)}, bf16[256,2048]{1,0:T(8,128)(2,1)S(1)}, u32[]{:S(2)}, u32[]{:S(2)}) collective-permute-start(bf16[256,2048]{1,0:T(8,128)(2,1)} %get-tuple-element.381), channel_id=1, source_target_pairs={{0,2},{2,4},{4,6},{1,3},{3,5},{5,7},{8,10},{10,12},{12,14},{9,11},... | collective-permute-start | bytes 3145736 | tf_op jit(solution)/shard_map/ppermute | solution.py:102
  593.5 127.3 %all-gather.8.cloned.1.call-start = ((), (), s32[]{:S(2)}) async-start(), calls=%async_computation.31 | async-start | bytes 5242880 | tf_op jit(solution)/shard_map/all_gather | solution.py:1012
  649.1 55.4 %all-to-all-start.18 = ((bf16[8,64,2048]{2,1,0:T(8,128)(2,1)}), bf16[8,64,2048]{2,1,0:T(8,128)(2,1)S(1)}, u32[]{:S(2)}, u32[]{:S(2)}) async-start(bf16[8,64,2048]{2,1,0:T(8,128)(2,1)} %bitcast.300), calls=%async_computation.19 | async-start | bytes 4194304 | tf_op jit(solution)/shard_map/all_to_all | solution.py:833
  656.2 48.3 %collective-permute-start.24 = (bf16[256,2048]{1,0:T(8,128)(2,1)}, bf16[256,2048]{1,0:T(8,128)(2,1)}, u32[]{:S(2)}, u32[]{:S(2)}) collective-permute-start(bf16[256,2048]{1,0:T(8,128)(2,1)} %line_part.12.refs_0_), channel_id=1, source_target_pairs={{0,2},{6,4},{1,3},{7,5},{8,10},{14,12},{9,11},{15,13},{16,18},{22,... | collective-permute-start | bytes 3145736 | tf_op jit(solution)/shard_map/ppermute | solution.py:90
  709.7 33.1 %collective-permute-start.25 = (bf16[256,2048]{1,0:T(8,128)(2,1)}, bf16[256,2048]{1,0:T(8,128)(2,1)}, u32[]{:S(2)}, u32[]{:S(2)}) collective-permute-start(bf16[256,2048]{1,0:T(8,128)(2,1)} %get-tuple-element.437), channel_id=1, source_target_pairs={{0,2},{2,4},{1,3},{3,5},{8,10},{10,12},{9,11},{11,13},{16,18},{18,... | collective-permute-start | bytes 3145736 | tf_op jit(solution)/shard_map/ppermute | solution.py:95
  716.8 30.7 %all-to-all-start.19 = ((bf16[8,64,2048]{2,1,0:T(8,128)(2,1)}), bf16[8,64,2048]{2,1,0:T(8,128)(2,1)S(1)}, u32[]{:S(2)}, u32[]{:S(2)}) async-start(bf16[8,64,2048]{2,1,0:T(8,128)(2,1)} %bitcast.299), calls=%async_computation.20 | async-start | bytes 4194304 | tf_op jit(solution)/shard_map/all_to_all | solution.py:833
  753.1 47.5 %collective-permute-start.27 = (bf16[256,2048]{1,0:T(8,128)(2,1)}, bf16[256,2048]{1,0:T(8,128)(2,1)S(1)}, u32[]{:S(2)}, u32[]{:S(2)}) collective-permute-start(bf16[256,2048]{1,0:T(8,128)(2,1)} %get-tuple-element.449), channel_id=1, source_target_pairs={{0,2},{2,4},{4,6},{1,3},{3,5},{5,7},{8,10},{10,12},{12,14},{9,11},... | collective-permute-start | bytes 3145736 | tf_op jit(solution)/shard_map/ppermute | solution.py:102
  754.5 46.2 %collective-permute-start.28 = (bf16[256,2048]{1,0:T(8,128)(2,1)}, bf16[256,2048]{1,0:T(8,128)(2,1)}, u32[]{:S(2)}, u32[]{:S(2)}) collective-permute-start(bf16[256,2048]{1,0:T(8,128)(2,1)} %get-tuple-element.450), channel_id=1, source_target_pairs={{6,4},{4,2},{2,0},{7,5},{5,3},{3,1},{14,12},{12,10},{10,8},{15,13}... | collective-permute-start | bytes 3145736 | tf_op jit(solution)/shard_map/ppermute | solution.py:103
  755.8 44.9 %all-to-all-start.20 = ((bf16[8,64,2048]{2,1,0:T(8,128)(2,1)}), bf16[8,64,2048]{2,1,0:T(8,128)(2,1)S(1)}, u32[]{:S(2)}, u32[]{:S(2)}) async-start(bf16[8,64,2048]{2,1,0:T(8,128)(2,1)} %bitcast.296), calls=%async_computation.21 | async-start | bytes 4194304 | tf_op jit(solution)/shard_map/all_to_all | solution.py:833
  759.4 113.8 %reduce-scatter.6.cloned.1.call-start = ((), (), s32[]{:S(2)}) async-start(), calls=%async_computation.32 | async-start | bytes 4718592 | tf_op jit(solution)/shard_map/reduce_scatter | solution.py:1039
  760.0 176.1 %reduce-scatter.8.cloned.1.call-start = ((), (), s32[]{:S(2)}) async-start(), calls=%async_computation.33 | async-start | bytes 5242880 | tf_op jit(solution)/shard_map/reduce_scatter | solution.py:1053
  837.0 33.3 %collective-permute-start.30 = (bf16[2048,512]{1,0:T(8,128)(2,1)}, bf16[2048,512]{1,0:T(8,128)(2,1)}, u32[]{:S(2)}, u32[]{:S(2)}) collective-permute-start(bf16[2048,512]{1,0:T(8,128)(2,1)} %constant_dynamic-slice_fusion), channel_id=1, source_target_pairs={{0,1},{1,0},{2,3},{3,2},{4,5},{5,4},{6,7},{7,6},{8,9},{9,8},{10,11... | collective-permute-start | bytes 6291464 | tf_op jit(solution)/shard_map/ppermute | solution.py:150
  875.1 34.2 %collective-permute-start.35 = (bf16[512,512]{1,0:T(8,128)(2,1)}, bf16[512,512]{1,0:T(8,128)(2,1)}, u32[]{:S(2)}, u32[]{:S(2)}) collective-permute-start(bf16[512,512]{1,0:T(8,128)(2,1)} %get-tuple-element.488), channel_id=1, source_target_pairs={{0,8},{8,0},{16,24},{24,16},{1,9},{9,1},{17,25},{25,17},{2,10},{10... | collective-permute-start | bytes 1572872 | tf_op jit(solution)/shard_map/ppermute | solution.py:112
  877.1 32.1 %collective-permute-start.36 = (bf16[512,512]{1,0:T(8,128)(2,1)}, bf16[512,512]{1,0:T(8,128)(2,1)}, u32[]{:S(2)}, u32[]{:S(2)}) collective-permute-start(bf16[512,512]{1,0:T(8,128)(2,1)} %get-tuple-element.490), channel_id=1, source_target_pairs={{0,16},{8,24},{16,0},{24,8},{1,17},{9,25},{17,1},{25,9},{2,18},{10... | collective-permute-start | bytes 1572872 | tf_op jit(solution)/shard_map/ppermute | solution.py:112
  877.6 31.6 %collective-permute-start.37 = (bf16[512,512]{1,0:T(8,128)(2,1)S(1)}, bf16[512,512]{1,0:T(8,128)(2,1)}, u32[]{:S(2)}, u32[]{:S(2)}) collective-permute-start(bf16[512,512]{1,0:T(8,128)(2,1)S(1)} %get-tuple-element.489), channel_id=1, source_target_pairs={{0,24},{8,16},{16,8},{24,0},{1,25},{9,17},{17,9},{25,1},{2,26},{10... | collective-permute-start | bytes 1572872 | tf_op jit(solution)/shard_map/ppermute | solution.py:112
  883.2 31.0 %all-to-all-start.22 = ((bf16[4,32,2048]{2,1,0:T(8,128)(2,1)}), bf16[4,32,2048]{2,1,0:T(8,128)(2,1)}, u32[]{:S(2)}, u32[]{:S(2)}) async-start(bf16[4,32,2048]{2,1,0:T(8,128)(2,1)} %bitcast.315), calls=%async_computation.24 | async-start | bytes 1048576 | tf_op jit(solution)/shard_map/all_to_all | solution.py:1082
  (97 other events, 1431.6 us)
Sparse Core Ops, SparseCore 0:
  25.9 97.9 all-gather.3
  221.9 76.0 reduce-scatter.3
  617.7 95.5 all-gather.7
Sparse Core Ops, SparseCore 1:
  139.4 53.4 all-gather.5
  763.6 53.5 reduce-scatter.5
  820.3 92.2 reduce-scatter.7

commit v4 on v3

--- a/solution.py
+++ b/solution.py
@@ -111,6 +111,17 @@
         piece = lax.dynamic_index_in_dim(value, dp ^ k, 0, keepdims=False)
         total = total + lax.ppermute(piece, "dp", [(i, i ^ k) for i in range(dps)]).astype(F32)
     return total
+
+
+def exchange(value, axis):
+    size, me = value.shape[0], lax.axis_index(axis)
+    own = lax.dynamic_index_in_dim(value, me, 0, keepdims=False)
+    whole = lax.dynamic_update_index_in_dim(jnp.zeros_like(value), own, me, 0)
+    for k in range(1, size):
+        piece = lax.dynamic_index_in_dim(value, me ^ k, 0, keepdims=False)
+        got = lax.ppermute(piece, axis, [(i, i ^ k) for i in range(size)])
+        whole = lax.dynamic_update_index_in_dim(whole, got, me ^ k, 0)
+    return whole
 
 
 def from_dps(value, dp):
@@ -434,7 +445,8 @@
 
 
 def _project_back_kernel(
-    raw_ref, dq_ref, dkv_ref, w_ref, cos_ref, sin_ref, qg_ref, kg_ref, ng_ref, rg_ref, dqg_ref, dkg_ref
+    raw_ref, near_ref, last_ref, dkv_ref, w_ref, cos_ref, sin_ref, qg_ref, kg_ref,
+    ng_ref, rg_ref, dqg_ref, dkg_ref,
 ):
     @pl.when(pl.program_id(0) == 0)
     def _():
@@ -442,14 +454,15 @@
         dkg_ref[...] = jnp.zeros_like(dkg_ref)
 
     cosine, sine = cos_ref[...], sin_ref[...]
-    heads = dq_ref.shape[1] // HEAD
+    heads = near_ref.shape[1] // HEAD
+    at_last = pl.program_id(0) == STEPS - 1
     for h in range(heads + 1):
         cols = slice(h * HEAD, (h + 1) * HEAD)
         value = raw_ref[:, cols]
         factor = lax.rsqrt(_lane_mean(value * value) + EPS)
         unit = value * factor
         if h < heads:
-            grad = dq_ref[:, cols].astype(F32) * (1.0 / math.sqrt(HEAD))
+            grad = jnp.where(at_last, last_ref[:, cols], near_ref[:, cols]).astype(F32) * (1.0 / math.sqrt(HEAD))
         else:
             grad = dkv_ref[:, :HEAD]
         grad = grad * cosine + pltpu.roll(grad * sine, HEAD // 2, 1)
@@ -466,7 +479,7 @@
     ng_ref[...] = times_transposed(rg_ref[...], w_ref[...]).astype(BF)
 
 
-def project_back(raw, query_grads, key_value_grads, w_in, cosine, sine, query_gain, key_gain, rows):
+def project_back(raw, near, last, key_value_grads, w_in, cosine, sine, query_gain, key_gain, rows):
     tokens, columns = raw.shape
     width = w_in.shape[0]
 
@@ -477,10 +490,11 @@
         _project_back_kernel,
         "project_back",
         (tokens // rows,),
-        (raw, query_grads, key_value_grads, w_in, cosine, sine, query_gain, key_gain),
+        (raw, near, last, key_value_grads, w_in, cosine, sine, query_gain, key_gain),
         [
             tile(columns),
-            tile(columns - 2 * HEAD),
+            pl.BlockSpec((rows, columns - 2 * HEAD), lambda i: (jnp.minimum(i, STEPS - 2), 0)),
+            full(rows, columns - 2 * HEAD),
             tile(2 * HEAD),
             full(width, columns),
             tile(HEAD),
@@ -490,6 +504,7 @@
         ],
         [((tokens, width), BF), ((tokens, columns), BF), ((1, HEAD), F32), ((1, HEAD), F32)],
         [tile(width), tile(columns), full(1, HEAD), full(1, HEAD)],
+        dear=True,
     )
 
 
@@ -601,7 +616,7 @@
     return jnp.concatenate([value, extra], axis=1)
 
 
-def _attend_back_kernel(table, *refs, cores, chunk, rows):
+def _attend_back_kernel(table, *refs, cores, chunk, rows, first, count):
     pieces, refs = refs[:cores], refs[cores:]
     q_ref, do_ref, o_ref, l_ref, at_ref, opens_ref, dq_ref = refs[:7]
     sums, refs = refs[7 : 7 + cores], refs[7 + cores :]
@@ -616,8 +631,8 @@
         dk_ref[...] = jnp.zeros_like(dk_ref)
         dv_ref[...] = jnp.zeros_like(dv_ref)
 
-    number = pl.program_id(0)
-    for n in range(STEPS):
+    number = first + pl.program_id(0)
+    for n in range(first, first + count):
 
         @pl.when(number == n)
         def _(n=n):
@@ -648,7 +663,7 @@
 
             lax.fori_loop(0, q_ref.shape[1] // (2 * HEAD), pair_of_heads, 0)
 
-    @pl.when(number == STEPS - 1)
+    @pl.when(number == first + count - 1)
     def _():
         for k, piece in enumerate(sums):
             for i in range(STEPS):
@@ -657,24 +672,24 @@
                 piece[i * rows : (i + 1) * rows, HEAD:] = dv_ref[place, :]
 
 
-def attend_back(table, queries, grads, mixed, log_totals, pieces, query_at, opens, rows):
+def attend_back(table, queries, grads, mixed, log_totals, pieces, query_at, opens, rows, first, count):
     tokens, width = queries.shape
     heads, cores = width // HEAD, len(pieces)
     group = cores * tokens
     chunk = group // STEPS
     piece = full(tokens, 2 * HEAD)
-    column = pl.BlockSpec((rows, 1), lambda i, o: (i, 0))
-    tile = pl.BlockSpec((rows, width), lambda i, o: (i, 0))
+    column = pl.BlockSpec((rows, 1), lambda i, o: (i + first, 0))
+    tile = pl.BlockSpec((rows, width), lambda i, o: (i + first, 0))
     return run(
-        partial(_attend_back_kernel, cores=cores, chunk=chunk, rows=rows),
+        partial(_attend_back_kernel, cores=cores, chunk=chunk, rows=rows, first=first, count=count),
         "attend_back",
-        (STEPS,),
+        (count,),
         (*pieces, queries, grads, mixed, log_totals, query_at, opens),
         [piece] * cores
-        + [tile, tile, tile, pl.BlockSpec((heads, rows, HEAD), lambda i, o: (0, i, 0))]
+        + [tile, tile, tile, pl.BlockSpec((heads, rows, HEAD), lambda i, o: (0, i + first, 0))]
         + [column, column],
-        [((tokens, width), BF)] + [((tokens, 2 * HEAD), F32)] * cores,
-        [tile] + [piece] * cores,
+        [((count * rows, width), BF)] + [((tokens, 2 * HEAD), F32)] * cores,
+        [pl.BlockSpec((rows, width), lambda i, o: (i, 0))] + [piece] * cores,
         scalars=table,
         dear=True,
         scratch=[
@@ -900,7 +915,7 @@
     g_up2, g_down2 = spread_second(g_up, g_down)
     g1 = to_plane(dispatch(zs, back[1], [g_up, g_down], FIRST))
     mixed, log_totals = attend(table, queries, pieces, query_at, opens, tokens)
-    mixed, w_back, g_up2, g_down2 = hold(mixed, w_back, g_up2, g_down2)
+    mixed, g_up2, g_down2 = hold(mixed, g_up2, g_down2)
     g_last = spread_third(g_up2, g_down2, z)
     w_back = w_back.reshape(dps, cores, STEPS, dps // STEPS, -1, width).transpose(3, 2, 1, 0, 4, 5)
     w_back = w_back.reshape(head_cols, width)
@@ -974,6 +989,7 @@
     )
     b2 = to_plane(d2)
     (c3,) = line_part(zs, pick[3], b3, tokens)
+    c3, h2 = hold(c3, h2)
     got = sum_first(c3)
     p2 = produced(h2)
     b2, d1, h1, p2 = hold(b2, d1, h1, p2)
@@ -1016,42 +1032,48 @@
     o3, p2, rows, down_weight_grad, router_grad = hold(
         o3, p2, rows, down_weight_grad, router_grad
     )
+    o2 = to_plane(p2)
     (o3,) = line_part(zs, pick[3], o3, tokens)
+    up_weight_grad = contract_chunks(rows, up_grads)
+    o2, p1, rows, up_weight_grad = hold(o2, p1, rows, up_weight_grad)
+    o1 = to_plane(p1)
+    gate_weight_grad = contract_chunks(rows, gate_grads)
+    resid_all, o3, o2, gate_weight_grad = hold(resid_all, o3, o2, gate_weight_grad)
     t_got = sum_first(o3)
-    o2 = to_plane(p2)
-    up_weight_grad = contract_chunks(rows, up_grads)
-    rows, up_weight_grad, up_grads = hold(rows, up_weight_grad, up_grads)
-    gate_weight_grad = contract_chunks(rows, gate_grads)
-    o2, t_got, gate_weight_grad = hold(o2, t_got, gate_weight_grad)
-    o2, middle = line_part(zs, pick[2], o2, tokens, 1, (o3, t_got))
-    middle, o2, p1 = hold(middle, o2, p1)
-    t_up, t_down = sum_second(middle)
-    o1 = to_plane(p1)
-    resid_all, o2 = hold(resid_all, o2)
     mixed_grad = matmul(resid_all, w_back, "nt", 4, "rows", dear=True)
     mixed_grad, resid_all = hold(mixed_grad, resid_all)
     out_weight_grad = matmul(mixed, resid_all, "tn", 4, "columns")
     out_weight_grad = out_weight_grad.reshape(dps // STEPS, STEPS, cores, dps, -1, width)
     out_weight_grad = out_weight_grad.transpose(3, 2, 1, 0, 4, 5).reshape(head_cols, width)
-    out_weight_grad, mixed_grad, t_up, t_down, o1 = hold(
-        out_weight_grad, mixed_grad, t_up, t_down, o1
-    )
+    out_weight_grad, mixed_grad, t_got, o2, o3 = hold(out_weight_grad, mixed_grad, t_got, o2, o3)
     out_weight_grad = lax.psum_scatter(out_weight_grad, PLANE, scatter_dimension=0, tiled=True)
+    o2, middle = line_part(zs, pick[2], o2, tokens, 1, (o3, t_got))
+    middle, o2, mixed_grad = hold(middle, o2, mixed_grad)
+    t_up, t_down = sum_second(middle)
+    back = partial(attend_back, table, queries, mixed_grad, mixed, log_totals, pieces, query_at)
+    near_grads, *near_sums = back(opens, tokens, 0, STEPS - 1)
+    near_grads, t_up, t_down, o1, o2, mixed_grad = hold(
+        near_grads, t_up, t_down, o1, o2, mixed_grad
+    )
     t_up, t_down = line_part(zs, pick[1], o1, tokens, 2, (o2, t_up, t_down))
-    t_up, t_down, p0 = hold(t_up, t_down, p0)
+    t_up, t_down, mixed_grad = hold(t_up, t_down, mixed_grad)
     t_up, t_down = sum_third(t_up, t_down)
+    last_grads, *last_sums = attend_back(
+        table, queries, mixed_grad, mixed, log_totals, pieces, query_at, opens, tokens, STEPS - 1, 1
+    )
+    last_grads, out_weight_grad, *last_sums = hold(last_grads, out_weight_grad, *last_sums)
+    own_sums, *other_sums = [a + b for a, b in zip(near_sums, last_sums)]
+    sums = sum_over_cores([own_sums, *[v.astype(BF) for v in other_sums]])
+    sums, t_up, t_down = hold(sums, t_up, t_down)
+    normed_grad, raw_grad, query_gain_grad, key_gain_grad = project_back(
+        raw, near_grads, last_grads, sums, w_in, cosine, sine, query_gain_f, key_gain_f, tokens
+    )
+    normed_grad, raw_grad, out_weight_grad, p0 = hold(normed_grad, raw_grad, out_weight_grad, p0)
+    normed_sum = lax.psum_scatter(normed_grad, "z", scatter_dimension=0, tiled=True)
     o0 = to_plane(p0)
-    query_grads, *sums = attend_back(
-        table, queries, mixed_grad, mixed, log_totals, pieces, query_at, opens, tokens
-    )
-    query_grads, t_up, t_down, o0, *sums = hold(query_grads, t_up, t_down, o0, *sums)
-    sums = sum_over_cores(sums)
-    normed_grad, raw_grad, query_gain_grad, key_gain_grad = project_back(
-        raw, query_grads, sums, w_in, cosine, sine, query_gain_f, key_gain_f, tokens
-    )
-    normed_grad, raw_grad = hold(normed_grad, raw_grad)
-    normed_sum = lax.psum_scatter(normed_grad, "z", scatter_dimension=0, tiled=True)
     in_grad = matmul(normed, raw_grad, "tn", 4, "rows")
+    in_grad, o0 = hold(in_grad, o0)
+    out_weight_grad = exchange(out_weight_grad.reshape(STEPS, -1, width), "z")
     query_share = sum_over_cores(by_core(in_grad[:, :head_cols], 1)).astype(BF)
     key_value_grad = in_grad[:, head_cols:].reshape(dps, STEPS, cores, rows_dev, 2 * HEAD)
     key_value_grad = sum_over_cores(
@@ -1073,26 +1095,21 @@
         ],
         axis=1,
     )
+    query_share, key_value_grad, late, out_weight_grad, o0 = hold(
+        query_share, key_value_grad, late, out_weight_grad, o0
+    )
     late = lax.all_to_all(late, ALL, split_axis=0, concat_axis=0, tiled=True)
-    late, out_weight_grad, o0, query_share, key_value_grad = hold(
-        late, out_weight_grad, o0, query_share, key_value_grad
-    )
     query_weight_grad = over_dps(query_share.reshape(dps, -1, own_cols), dp)
     key_value_grad = over_dps(key_value_grad, dp).astype(BF)
-    out_weight_grad = lax.all_to_all(out_weight_grad, "z", split_axis=0, concat_axis=0, tiled=True)
+    out_weight_grad = exchange(out_weight_grad.reshape(dps, -1, width), "dp")
+    out_weight_grad = out_weight_grad.reshape(-1, width).astype(F32)
     (o0,) = line_part(zs, pick[0], o0, tokens)
     output = resid + (o0.astype(F32) + t_up.astype(F32) + t_down.astype(F32))
     output = output.astype(BF)
     late = jnp.sum(late, axis=0)
-    out_weight_grad, key_value_grad, output, late, query_weight_grad = hold(
-        out_weight_grad, key_value_grad, output, late, query_weight_grad
-    )
     gain_sums = late[-2 * HEAD :].reshape(2, HEAD)
     owned = late[: -2 * HEAD].reshape(experts + 2, rows_dev)
-    key_value_grad = lax.all_to_all(key_value_grad, "z", split_axis=0, concat_axis=0, tiled=True)
-    key_value_grad, out_weight_grad = hold(key_value_grad, out_weight_grad)
-    out_weight_grad = lax.all_to_all(out_weight_grad, "dp", split_axis=0, concat_axis=0, tiled=True)
-    out_weight_grad = out_weight_grad.astype(F32)
+    key_value_grad = exchange(key_value_grad, "z")
     key_value_grad = key_value_grad.transpose(1, 0, 2).astype(F32)
     key_weight_grad = key_value_grad[:, :, :HEAD].reshape(rows_dev, -1)
     value_weight_grad = key_value_grad[:, :, HEAD:].reshape(rows_dev, -1)

time: 960 us -> 923 us (0.961)
  waiting for transfers between devices: 306 us -> 246 us
  local copies, waits for them, and re-layouts: 61.5 us -> 73 us
    all_to_all x1, waiting for transfers between devices: 20.6 us -> 0.01 us  [body(): late = lax.all_to_all(late, ALL, split_axis=0, concat_axis=0, tiled=True)]
    ppermute x2, waiting for transfers between devices: 20.9 us -> 0.88 us  [sum_first(): return lax.ppermute(third, 'z', [(0, 1), (3, 2)])]
    ppermute x0 -> x9, starting transfers between devices: none -> 16.4 us  [exchange(): got = lax.ppermute(piece, axis, [(i, i ^ k) for i in range(size)])]
    all_to_all x17, waiting for transfers between devices: 126 us -> 140 us  [to_plane(): return lax.all_to_all(rows, PLANE, split_axis=0, concat_axis=0, tiled=True)]
    ppermute x2, waiting for transfers between devices: 20.7 us -> 7.97 us  [spread_third(): return lax.ppermute(jnp.where(z == 2, up2, down2), 'z', [(2, 3), (1, 0)])]
    all_to_all x3 -> x0, starting transfers between devices: 12.3 us -> none  [the longest x1 4.44 us: body(): lax.all_to_all(key_value_grad, 'z', split_axis=0, concat_axis=0, tiled=True)]
    all_to_all x3 -> x0, waiting for transfers between devices: 11.8 us -> none  [the longest x1 5.2 us: body(): lax.all_to_all(out_weight_grad, 'dp', split_axis=0, concat_axis=0, tiled=...]
    pallas_call x43 -> x44, Pallas kernels: 328 us -> 333 us  [run(): pl.pallas_call(kernel, grid_spec=pltpu.PrefetchScalarGridSpec(num_scalar_...]
  transfers between devices with their start and end apart: 69 -> 75, of which waited for: 32 -> 31; matrix products, arithmetic and copies ran while one was open for 10% -> 12% of each run, Pallas kernels for 31% -> 31%
where the time goes in v4:
time: 923 us; the launch traced here: 911 us
  Pallas kernels  333 us (36%)
  waiting for transfers between devices  246 us (27%)
  starting transfers between devices  177 us (19%)
  local copies, waits for them, and re-layouts  73 us (8%)
  other arithmetic  46.4 us (5%)
  between operations  30.9 us (3%)
    pallas_call x44, Pallas kernels, run(): pl.pallas_call(kernel, grid_spec=pltpu.PrefetchScalarGridSpec(num_scalar_...  333 us
    all_to_all x17, waiting for transfers between devices, to_plane(): return lax.all_to_all(rows, PLANE, split_axis=0, concat_axis=0, tiled=True)  140 us
    all_to_all x17, starting transfers between devices, to_plane(): return lax.all_to_all(rows, PLANE, split_axis=0, concat_axis=0, tiled=True)  68.2 us
  transfers between devices with their start and end apart: 75, of which 31 were waited for; matrix products, arithmetic and copies ran while one was open for 12% of the time, Pallas kernels for 31%

profile of v4, /device:TPU:0, one launch (start us, length us, event | category | flops | bytes accessed | tf_op | source)
XLA Modules:
  0.0 910.7 jit_solution(2535196910224190956)
XLA Ops:
  55.8 14.2 %collective-permute-done.6 = bf16[512,384]{1,0:T(8,128)(2,1)S(1)} collective-permute-done((bf16[512,384]{1,0:T(8,128)(2,1)S(1)}, bf16[512,384]{1,0:T(8,128)(2,1)S(1)}, u32[]{:S(2)}, u32[]{:S(2)}) %collective-permute-start.6) | collective-permute-done | bytes 393248 | tf_op jit(solution)/shard_map/ppermute | solution.py:132
  104.5 8.8 all-to-all-done.3
  123.8 13.3 %project.1 = (bf16[1024,2048]{1,0:T(8,128)(2,1)}, f32[1024,1280]{1,0:T(8,128)}, bf16[1024,1024]{1,0:T(8,128)(2,1)}, bf16[1024,256]{1,0:T(8,128)(2,1)}) custom-call(bf16[1024,2048]{1,0:T(8,128)(2,1)} %all-gather.4.cloned.1.call-done.x_ref, f32[1,2048]{1,0:T(1,128)} %bitcast.349, bf16[2048,1280]{1,0:T(8,128)(2,1)} %pad_maximum_fusion.w_ref, ...), custom_call_target="tpu_custom_call" | custom-call | flops 99999997952 | bytes 1 | tf_op jit(solution)/shard_map/project/pallas_call | solution.py:176
  154.5 19.1 %attend.1 = (bf16[1024,1024]{1,0:T(8,128)(2,1)}, f32[8,1024,128]{2,1,0:T(8,128)}) custom-call(s32[8]{0:T(128)S(1)} %pad_add_fusion.table, bf16[1024,256]{1,0:T(8,128)(2,1)} %get-tuple-element.279.refs_0_, bf16[1024,256]{1,0:T(8,128)(2,1)} %collective-permute-done.10.refs_1_, bf16[1024,1024]{1,0:T(8,128)(2,1)} %get-tuple-element.281.refs_2_, ...), custom_call_target="tpu_custom_call" | custom-call | flops 99999997952 | bytes 1 | tf_op jit(solution)/shard_map/attend/pallas_call | solution.py:176
  176.3 16.6 %all-gather.6.cloned.1.call-done = bf16[1024,2048]{1,0:T(8,128)(2,1)} async-done(((bf16[128,2048]{1,0:T(8,128)(2,1)}), bf16[1024,2048]{1,0:T(8,128)(2,1)}) %all-gather.6.cloned.1.call-update) | async-done | bytes 4194320 | tf_op jit(solution)/shard_map/all_gather | solution.py:862
  197.7 8.4 matmul_nn.5
  219.8 21.4 %all-to-all-done.5 = bf16[8,64,2048]{2,1,0:T(8,128)(2,1)} async-done(((bf16[8,64,2048]{2,1,0:T(8,128)(2,1)}), bf16[8,64,2048]{2,1,0:T(8,128)(2,1)}, u32[]{:S(2)}, u32[]{:S(2)}) %all-to-all-start.5) | async-done | bytes 2097184 | tf_op jit(solution)/shard_map/all_to_all | solution.py:848
  258.9 16.2 %all-to-all-done.6 = bf16[8,64,2048]{2,1,0:T(8,128)(2,1)S(1)} async-done(((bf16[8,64,2048]{2,1,0:T(8,128)(2,1)}), bf16[8,64,2048]{2,1,0:T(8,128)(2,1)S(1)}, u32[]{:S(2)}, u32[]{:S(2)}) %all-to-all-start.6) | async-done | bytes 2097184 | tf_op jit(solution)/shard_map/all_to_all | solution.py:848
  317.5 13.2 %collective-permute-done.14.refs_0_ = bf16[256,2048]{1,0:T(8,128)(2,1)S(1)} collective-permute-done((bf16[256,2048]{1,0:T(8,128)(2,1)S(1)}, bf16[256,2048]{1,0:T(8,128)(2,1)S(1)}, u32[]{:S(2)}, u32[]{:S(2)}) %collective-permute-start.14) | collective-permute-done | bytes 1048608 | tf_op jit(solution)/shard_map/ppermute | solution.py:68
  345.1 12.6 %expert.4 = (bf16[512,2048]{1,0:T(8,128)(2,1)}, bf16[512,768]{1,0:T(8,128)(2,1)}, bf16[512,768]{1,0:T(8,128)(2,1)}, bf16[512,768]{1,0:T(8,128)(2,1)}, f32[512,1]{1,0:T(8,128)}) custom-call(bf16[512,2048]{1,0:T(8,128)(2,1)} %bitcast.72.x_ref.refs_0_, f32[512,768]{1,0:T(8,128)} %matmul_nt.5.pulled_ref, bf16[512,128]{1,0:T(8,128)(2,1)} %bitcast.346, ...), custom_call_target="tpu_custom_call" | custom-call | flops 99999997952 | bytes 1 | tf_op jit(solution)/shard_map/expert/pallas_call | solution.py:176
  357.7 9.3 %collective-permute-done.17.refs_3_.refs_1_ = bf16[256,2048]{1,0:T(8,128)(2,1)S(1)} collective-permute-done((bf16[256,2048]{1,0:T(8,128)(2,1)}, bf16[256,2048]{1,0:T(8,128)(2,1)S(1)}, u32[]{:S(2)}, u32[]{:S(2)}) %collective-permute-start.17) | collective-permute-done | bytes 1048608 | tf_op jit(solution)/shard_map/ppermute | solution.py:76
  378.5 12.7 %expert.5 = (bf16[512,2048]{1,0:T(8,128)(2,1)}, bf16[512,768]{1,0:T(8,128)(2,1)}, bf16[512,768]{1,0:T(8,128)(2,1)}, bf16[512,768]{1,0:T(8,128)(2,1)}, f32[512,1]{1,0:T(8,128)}) custom-call(bf16[512,2048]{1,0:T(8,128)(2,1)} %bitcast.76.x_ref.refs_1_, f32[512,768]{1,0:T(8,128)} %matmul_nt.6.pulled_ref, bf16[512,128]{1,0:T(8,128)(2,1)} %bitcast.345, ...), custom_call_target="tpu_custom_call" | custom-call | flops 99999997952 | bytes 1 | tf_op jit(solution)/shard_map/expert/pallas_call | solution.py:176
  391.2 8.0 collective-permute-done.18.refs_2_
  410.8 12.6 %expert.6 = (bf16[512,2048]{1,0:T(8,128)(2,1)}, bf16[512,768]{1,0:T(8,128)(2,1)}, bf16[512,768]{1,0:T(8,128)(2,1)}, bf16[512,768]{1,0:T(8,128)(2,1)}, f32[512,1]{1,0:T(8,128)}) custom-call(bf16[512,2048]{1,0:T(8,128)(2,1)} %bitcast.283, f32[512,768]{1,0:T(8,128)} %matmul_nt.7.pulled_ref, bf16[512,128]{1,0:T(8,128)(2,1)} %bitcast.344, ...), custom_call_target="tpu_custom_call" | custom-call | flops 99999997952 | bytes 1 | tf_op jit(solution)/shard_map/expert/pallas_call | solution.py:176
  423.5 14.0 %all-to-all-done.11 = bf16[8,64,2048]{2,1,0:T(8,128)(2,1)} async-done(((bf16[8,64,2048]{2,1,0:T(8,128)(2,1)}), bf16[8,64,2048]{2,1,0:T(8,128)(2,1)}, u32[]{:S(2)}, u32[]{:S(2)}) %all-to-all-start.11) | async-done | bytes 2097184 | tf_op jit(solution)/shard_map/all_to_all | solution.py:848
  437.5 12.6 %expert.7 = (bf16[512,2048]{1,0:T(8,128)(2,1)}, bf16[512,768]{1,0:T(8,128)(2,1)}, bf16[512,768]{1,0:T(8,128)(2,1)}, bf16[512,768]{1,0:T(8,128)(2,1)}, f32[512,1]{1,0:T(8,128)}) custom-call(bf16[512,2048]{1,0:T(8,128)(2,1)} %bitcast.80.x_ref.refs_3_, f32[512,768]{1,0:T(8,128)} %matmul_nt.8.pulled_ref, bf16[512,128]{1,0:T(8,128)(2,1)} %bitcast.343, ...), custom_call_target="tpu_custom_call" | custom-call | flops 99999997952 | bytes 1 | tf_op jit(solution)/shard_map/expert/pallas_call | solution.py:176
  465.9 14.8 %all-to-all-done.12 = bf16[8,64,2048]{2,1,0:T(8,128)(2,1)S(1)} async-done(((bf16[8,64,2048]{2,1,0:T(8,128)(2,1)}), bf16[8,64,2048]{2,1,0:T(8,128)(2,1)S(1)}, u32[]{:S(2)}, u32[]{:S(2)}) %all-to-all-start.12) | async-done | bytes 2097184 | tf_op jit(solution)/shard_map/all_to_all | solution.py:848
  500.3 15.4 %all-to-all-done.13 = bf16[8,64,2048]{2,1,0:T(8,128)(2,1)S(1)} async-done(((bf16[8,64,2048]{2,1,0:T(8,128)(2,1)}), bf16[8,64,2048]{2,1,0:T(8,128)(2,1)S(1)}, u32[]{:S(2)}, u32[]{:S(2)}) %all-to-all-start.13) | async-done | bytes 2097184 | tf_op jit(solution)/shard_map/all_to_all | solution.py:848
  536.5 10.7 %all-to-all-done.14 = bf16[8,64,2048]{2,1,0:T(8,128)(2,1)S(1)} async-done(((bf16[8,64,2048]{2,1,0:T(8,128)(2,1)}), bf16[8,64,2048]{2,1,0:T(8,128)(2,1)S(1)}, u32[]{:S(2)}, u32[]{:S(2)}) %all-to-all-start.14) | async-done | bytes 2097184 | tf_op jit(solution)/shard_map/all_to_all | solution.py:848
  570.2 9.3 %all-to-all-done.15 = bf16[8,64,2048]{2,1,0:T(8,128)(2,1)} async-done(((bf16[8,64,2048]{2,1,0:T(8,128)(2,1)}), bf16[8,64,2048]{2,1,0:T(8,128)(2,1)}, u32[]{:S(2)}, u32[]{:S(2)}) %all-to-all-start.15) | async-done | bytes 2097184 | tf_op jit(solution)/shard_map/all_to_all | solution.py:848
  587.1 11.1 %all-to-all-done.16 = f32[32,1,64]{2,1,0:T(1,128)S(1)} async-done(((f32[32,1,64]{2,1,0:T(1,128)}), f32[32,1,64]{2,1,0:T(1,128)S(1)}, u32[]{:S(2)}, u32[]{:S(2)}) %all-to-all-start.16) | async-done | bytes 8224 | tf_op jit(solution)/shard_map/all_to_all | solution.py:1008
  611.2 13.1 %contract_chunks.3 = f32[768,2048]{1,0:T(8,128)} custom-call(bf16[512,768]{1,0:T(8,128)(2,1)} %get-tuple-element.414.a_ref.refs_0_, bf16[512,768]{1,0:T(8,128)(2,1)} %get-tuple-element.415.a_ref.refs_1_, bf16[512,768]{1,0:T(8,128)(2,1)} %get-tuple-element.416.a_ref.refs_2_, bf16[512,768]{1,0:T(8,128)(2,1)} %get-tuple-element.417.a_ref.refs_3_, ...), custom_call_target="tpu_custom_call" | custom-call | flops 1 | bytes 1 | tf_op jit(solution)/shard_map/contract_chunks/pallas_call | solution.py:176
  625.3 12.4 %all-to-all-done.17 = bf16[8,64,2048]{2,1,0:T(8,128)(2,1)S(1)} async-done(((bf16[8,64,2048]{2,1,0:T(8,128)(2,1)}), bf16[8,64,2048]{2,1,0:T(8,128)(2,1)S(1)}, u32[]{:S(2)}, u32[]{:S(2)}) %all-to-all-start.17) | async-done | bytes 2097184 | tf_op jit(solution)/shard_map/all_to_all | solution.py:848
  646.2 13.1 %contract_chunks.4 = f32[2048,768]{1,0:T(8,128)} custom-call(bf16[512,2048]{1,0:T(8,128)(2,1)} %bitcast.72.x_ref.refs_0_, bf16[512,2048]{1,0:T(8,128)(2,1)} %bitcast.76.x_ref.refs_1_, bf16[512,2048]{1,0:T(8,128)(2,1)} %bitcast.284, bf16[512,2048]{1,0:T(8,128)(2,1)} %bitcast.80.x_ref.refs_3_, bf16[512,768]{1,0:T(8,128)(2,1)} %get-tuple-element.426.refs_4_, ...), custom_call_target="tpu_custom_call" | custom-call | flops 1 | bytes 1 | tf_op jit(solution)/shard_map/contract_chunks/pallas_call | solution.py:176
  659.3 10.0 %all-to-all-done.18 = bf16[8,64,2048]{2,1,0:T(8,128)(2,1)S(1)} async-done(((bf16[8,64,2048]{2,1,0:T(8,128)(2,1)}), bf16[8,64,2048]{2,1,0:T(8,128)(2,1)S(1)}, u32[]{:S(2)}, u32[]{:S(2)}) %all-to-all-start.18) | async-done | bytes 2097184 | tf_op jit(solution)/shard_map/all_to_all | solution.py:848
  675.2 13.1 %contract_chunks.5 = f32[2048,768]{1,0:T(8,128)} custom-call(bf16[512,2048]{1,0:T(8,128)(2,1)} %bitcast.72.x_ref.refs_0_, bf16[512,2048]{1,0:T(8,128)(2,1)} %bitcast.76.x_ref.refs_1_, bf16[512,2048]{1,0:T(8,128)(2,1)} %bitcast.285, bf16[512,2048]{1,0:T(8,128)(2,1)} %bitcast.80.x_ref.refs_3_, bf16[512,768]{1,0:T(8,128)(2,1)} %get-tuple-element.435.refs_4_, ...), custom_call_target="tpu_custom_call" | custom-call | flops 1 | bytes 1 | tf_op jit(solution)/shard_map/contract_chunks/pallas_call | solution.py:176
  690.5 8.7 matmul_nt.9.refs_3_
  699.2 8.5 matmul_tn.2
  723.4 27.3 %attend_back.2 = (bf16[768,1024]{1,0:T(8,128)(2,1)}, f32[1024,256]{1,0:T(8,128)}, f32[1024,256]{1,0:T(8,128)}) custom-call(s32[8]{0:T(128)S(1)} %pad_add_fusion.table, bf16[1024,256]{1,0:T(8,128)(2,1)} %get-tuple-element.279.refs_0_, bf16[1024,256]{1,0:T(8,128)(2,1)} %collective-permute-done.10.refs_1_, bf16[1024,1024]{1,0:T(8,128)(2,1)} %get-tuple-element.281.refs_2_, ...), custom_call_target="tpu_custom_call" | custom-call | flops 99999997952 | bytes 1 | tf_op jit(solution)/shard_map/attend_back/pallas_call | solution.py:176
  761.6 17.3 %attend_back.3 = (bf16[256,1024]{1,0:T(8,128)(2,1)}, f32[1024,256]{1,0:T(8,128)}, f32[1024,256]{1,0:T(8,128)}) custom-call(s32[8]{0:T(128)S(1)} %pad_add_fusion.table, bf16[1024,256]{1,0:T(8,128)(2,1)} %get-tuple-element.279.refs_0_, bf16[1024,256]{1,0:T(8,128)(2,1)} %collective-permute-done.10.refs_1_, bf16[1024,1024]{1,0:T(8,128)(2,1)} %get-tuple-element.281.refs_2_, ...), custom_call_target="tpu_custom_call" | custom-call | flops 99999997952 | bytes 1 | tf_op jit(solution)/shard_map/attend_back/pallas_call | solution.py:176
  786.6 14.3 %project_back.1 = (bf16[1024,2048]{1,0:T(8,128)(2,1)}, bf16[1024,1280]{1,0:T(8,128)(2,1)}, f32[1,128]{1,0:T(1,128)}, f32[1,128]{1,0:T(1,128)}) custom-call(f32[1024,1280]{1,0:T(8,128)} %get-tuple-element.310.raw_ref, bf16[768,1024]{1,0:T(8,128)(2,1)} %get-tuple-element.456.near_ref, bf16[256,1024]{1,0:T(8,128)(2,1)} %get-tuple-element.469.last_ref, ...), custom_call_target="tpu_custom_call" | custom-call | flops 99999997952 | bytes 1 | tf_op jit(solution)/shard_map/project_back/pallas_call | solution.py:176
  816.4 10.1 %matmul_tn.3 = bf16[2048,1280]{1,0:T(8,128)(2,1)} custom-call(bf16[1024,2048]{1,0:T(8,128)(2,1)} %get-tuple-element.309.a_ref, bf16[1024,1280]{1,0:T(8,128)(2,1)} %get-tuple-element.481.b_ref), custom_call_target="tpu_custom_call" | custom-call | flops 1 | bytes 1 | tf_op jit(solution)/shard_map/matmul_tn/pallas_call | solution.py:176
  (473 shorter events, 457.6 us)
Async XLA Ops:
  23.5 100.3 %all-gather.4.cloned.1.call-start = ((), (), s32[]{:S(2)}) async-start(), calls=%async_computation.25 | async-start | bytes 5242880 | tf_op jit(solution)/shard_map/all_gather | solution.py:827
  37.5 32.6 %collective-permute-start.3 = (bf16[2048,512]{1,0:T(8,128)(2,1)}, bf16[2048,512]{1,0:T(8,128)(2,1)}, u32[]{:S(2)}, u32[]{:S(2)}) collective-permute-start(bf16[2048,512]{1,0:T(8,128)(2,1)} %bitcast.4), channel_id=1, source_target_pairs={{1,0},{0,1},{3,2},{2,3},{5,4},{4,5},{7,6},{6,7},{9,8},{8,9},{11,10... | collective-permute-start | bytes 6291464 | tf_op jit(solution)/shard_map/ppermute | solution.py:140
  81.6 31.8 %all-to-all-start.3 = ((bf16[4,32,2048]{2,1,0:T(8,128)(2,1)}), bf16[4,32,2048]{2,1,0:T(8,128)(2,1)}, u32[]{:S(2)}, u32[]{:S(2)}) async-start(bf16[4,32,2048]{2,1,0:T(8,128)(2,1)} %bitcast.54), calls=%async_computation.3 | async-start | bytes 1048576 | tf_op jit(solution)/shard_map/all_to_all | solution.py:861
  95.8 43.5 %collective-permute-start.8 = (bf16[256,2048]{1,0:T(8,128)(2,1)S(1)}, bf16[256,2048]{1,0:T(8,128)(2,1)S(1)}, u32[]{:S(2)}, u32[]{:S(2)}) collective-permute-start(bf16[256,2048]{1,0:T(8,128)(2,1)S(1)} %copy-done.10), channel_id=1, source_target_pairs={{0,2},{2,4},{4,6},{1,3},{3,5},{5,7},{8,10},{10,12},{12,14},{9,11},... | collective-permute-start | bytes 3145736 | tf_op jit(solution)/shard_map/ppermute | solution.py:68
  99.8 39.5 %collective-permute-start.9 = (bf16[256,2048]{1,0:T(8,128)(2,1)S(1)}, bf16[256,2048]{1,0:T(8,128)(2,1)S(1)}, u32[]{:S(2)}, u32[]{:S(2)}) collective-permute-start(bf16[256,2048]{1,0:T(8,128)(2,1)S(1)} %copy-done.10), channel_id=1, source_target_pairs={{2,0},{4,2},{6,4},{3,1},{5,3},{7,5},{10,8},{12,10},{14,12},{11,9},... | collective-permute-start | bytes 3145736 | tf_op jit(solution)/shard_map/ppermute | solution.py:69
  113.3 31.0 %all-to-all-start.2 = ((bf16[8,64,2048]{2,1,0:T(8,128)(2,1)}), bf16[8,64,2048]{2,1,0:T(8,128)(2,1)}, u32[]{:S(2)}, u32[]{:S(2)}) async-start(bf16[8,64,2048]{2,1,0:T(8,128)(2,1)} %bitcast.302), calls=%async_computation.2 | async-start | bytes 4194304 | tf_op jit(solution)/shard_map/all_to_all | solution.py:848
  117.7 75.2 %all-gather.6.cloned.1.call-start = ((), (), s32[]{:S(2)}) async-start(), calls=%async_computation.26 | async-start | bytes 4718592 | tf_op jit(solution)/shard_map/all_gather | solution.py:862
  150.0 56.0 %all-to-all-start.4 = ((bf16[8,64,2048]{2,1,0:T(8,128)(2,1)}), bf16[8,64,2048]{2,1,0:T(8,128)(2,1)}, u32[]{:S(2)}, u32[]{:S(2)}) async-start(bf16[8,64,2048]{2,1,0:T(8,128)(2,1)} %bitcast.306), calls=%async_computation.4 | async-start | bytes 4194304 | tf_op jit(solution)/shard_map/all_to_all | solution.py:848
  154.4 135.6 %reduce-scatter.4.cloned.1.call-start = ((), (), s32[]{:S(2)}) async-start(), calls=%async_computation.27 | async-start | bytes 5242880 | tf_op jit(solution)/shard_map/reduce_scatter | solution.py:924
  174.9 31.2 %collective-permute-start.13 = (bf16[256,2048]{1,0:T(8,128)(2,1)}, bf16[256,2048]{1,0:T(8,128)(2,1)}, u32[]{:S(2)}, u32[]{:S(2)}) collective-permute-start(bf16[256,2048]{1,0:T(8,128)(2,1)} %broadcast_select_fusion.3), channel_id=1, source_target_pairs={{4,6},{2,0},{5,7},{3,1},{12,14},{10,8},{13,15},{11,9},{20,22},{18,... | collective-permute-start | bytes 3145736 | tf_op jit(solution)/shard_map/ppermute | solution.py:81
  210.1 31.1 %all-to-all-start.5 = ((bf16[8,64,2048]{2,1,0:T(8,128)(2,1)}), bf16[8,64,2048]{2,1,0:T(8,128)(2,1)}, u32[]{:S(2)}, u32[]{:S(2)}) async-start(bf16[8,64,2048]{2,1,0:T(8,128)(2,1)} %bitcast.311), calls=%async_computation.6 | async-start | bytes 4194304 | tf_op jit(solution)/shard_map/all_to_all | solution.py:848
  245.0 30.2 %all-to-all-start.6 = ((bf16[8,64,2048]{2,1,0:T(8,128)(2,1)}), bf16[8,64,2048]{2,1,0:T(8,128)(2,1)S(1)}, u32[]{:S(2)}, u32[]{:S(2)}) async-start(bf16[8,64,2048]{2,1,0:T(8,128)(2,1)} %bitcast.310), calls=%async_computation.7 | async-start | bytes 4194304 | tf_op jit(solution)/shard_map/all_to_all | solution.py:848
  298.7 42.0 %all-to-all-start.8 = ((bf16[8,64,2048]{2,1,0:T(8,128)(2,1)}), bf16[8,64,2048]{2,1,0:T(8,128)(2,1)}, u32[]{:S(2)}, u32[]{:S(2)}) async-start(bf16[8,64,2048]{2,1,0:T(8,128)(2,1)} %bitcast.300), calls=%async_computation.9 | async-start | bytes 4194304 | tf_op jit(solution)/shard_map/all_to_all | solution.py:848
  340.7 34.0 %all-to-all-start.9 = ((bf16[8,64,2048]{2,1,0:T(8,128)(2,1)}), bf16[8,64,2048]{2,1,0:T(8,128)(2,1)}, u32[]{:S(2)}, u32[]{:S(2)}) async-start(bf16[8,64,2048]{2,1,0:T(8,128)(2,1)} %bitcast.304), calls=%async_computation.10 | async-start | bytes 4194304 | tf_op jit(solution)/shard_map/all_to_all | solution.py:848
  374.7 30.4 %all-to-all-start.10 = ((bf16[8,64,2048]{2,1,0:T(8,128)(2,1)}), bf16[8,64,2048]{2,1,0:T(8,128)(2,1)S(1)}, u32[]{:S(2)}, u32[]{:S(2)}) async-start(bf16[8,64,2048]{2,1,0:T(8,128)(2,1)} %bitcast.305), calls=%async_computation.11 | async-start | bytes 4194304 | tf_op jit(solution)/shard_map/all_to_all | solution.py:848
  406.5 31.0 %all-to-all-start.11 = ((bf16[8,64,2048]{2,1,0:T(8,128)(2,1)}), bf16[8,64,2048]{2,1,0:T(8,128)(2,1)}, u32[]{:S(2)}, u32[]{:S(2)}) async-start(bf16[8,64,2048]{2,1,0:T(8,128)(2,1)} %bitcast.309), calls=%async_computation.12 | async-start | bytes 4194304 | tf_op jit(solution)/shard_map/all_to_all | solution.py:848
  450.1 30.6 %all-to-all-start.12 = ((bf16[8,64,2048]{2,1,0:T(8,128)(2,1)}), bf16[8,64,2048]{2,1,0:T(8,128)(2,1)S(1)}, u32[]{:S(2)}, u32[]{:S(2)}) async-start(bf16[8,64,2048]{2,1,0:T(8,128)(2,1)} %bitcast.326), calls=%async_computation.13 | async-start | bytes 4194304 | tf_op jit(solution)/shard_map/all_to_all | solution.py:848
  493.8 31.4 %collective-permute-start.19 = (bf16[256,2048]{1,0:T(8,128)(2,1)S(1)}, bf16[256,2048]{1,0:T(8,128)(2,1)}, u32[]{:S(2)}, u32[]{:S(2)}) collective-permute-start(bf16[256,2048]{1,0:T(8,128)(2,1)S(1)} %copy-done.5), channel_id=1, source_target_pairs={{0,2},{6,4},{1,3},{7,5},{8,10},{14,12},{9,11},{15,13},{16,18},{22,... | collective-permute-start | bytes 3145736 | tf_op jit(solution)/shard_map/ppermute | solution.py:90
  548.5 31.0 %all-to-all-start.15 = ((bf16[8,64,2048]{2,1,0:T(8,128)(2,1)}), bf16[8,64,2048]{2,1,0:T(8,128)(2,1)}, u32[]{:S(2)}, u32[]{:S(2)}) async-start(bf16[8,64,2048]{2,1,0:T(8,128)(2,1)} %bitcast.320), calls=%async_computation.16 | async-start | bytes 4194304 | tf_op jit(solution)/shard_map/all_to_all | solution.py:848
  563.3 36.5 %collective-permute-start.22 = (bf16[256,2048]{1,0:T(8,128)(2,1)}, bf16[256,2048]{1,0:T(8,128)(2,1)S(1)}, u32[]{:S(2)}, u32[]{:S(2)}) collective-permute-start(bf16[256,2048]{1,0:T(8,128)(2,1)} %get-tuple-element.394), channel_id=1, source_target_pairs={{0,2},{2,4},{4,6},{1,3},{3,5},{5,7},{8,10},{10,12},{12,14},{9,11},... | collective-permute-start | bytes 3145736 | tf_op jit(solution)/shard_map/ppermute | solution.py:102
  568.9 30.9 %collective-permute-start.23 = (bf16[256,2048]{1,0:T(8,128)(2,1)}, bf16[256,2048]{1,0:T(8,128)(2,1)S(1)}, u32[]{:S(2)}, u32[]{:S(2)}) collective-permute-start(bf16[256,2048]{1,0:T(8,128)(2,1)} %get-tuple-element.395), channel_id=1, source_target_pairs={{6,4},{4,2},{2,0},{7,5},{5,3},{3,1},{14,12},{12,10},{10,8},{15,13}... | collective-permute-start | bytes 3145736 | tf_op jit(solution)/shard_map/ppermute | solution.py:103
  583.5 104.7 %all-gather.8.cloned.1.call-start = ((), (), s32[]{:S(2)}) async-start(), calls=%async_computation.28 | async-start | bytes 5242880 | tf_op jit(solution)/shard_map/all_gather | solution.py:1028
  607.5 30.2 %all-to-all-start.17 = ((bf16[8,64,2048]{2,1,0:T(8,128)(2,1)}), bf16[8,64,2048]{2,1,0:T(8,128)(2,1)S(1)}, u32[]{:S(2)}, u32[]{:S(2)}) async-start(bf16[8,64,2048]{2,1,0:T(8,128)(2,1)} %bitcast.322), calls=%async_computation.18 | async-start | bytes 4194304 | tf_op jit(solution)/shard_map/all_to_all | solution.py:848
  670.6 80.2 %all-to-all-start.19 = ((bf16[8,64,2048]{2,1,0:T(8,128)(2,1)}), bf16[8,64,2048]{2,1,0:T(8,128)(2,1)}, u32[]{:S(2)}, u32[]{:S(2)}) async-start(bf16[8,64,2048]{2,1,0:T(8,128)(2,1)} %bitcast.321), calls=%async_computation.20 | async-start | bytes 4194304 | tf_op jit(solution)/shard_map/all_to_all | solution.py:848
  674.9 104.0 %reduce-scatter.6.cloned.1.call-start = ((), (), s32[]{:S(2)}) async-start(), calls=%async_computation.29 | async-start | bytes 4718592 | tf_op jit(solution)/shard_map/reduce_scatter | solution.py:1049
  718.2 32.5 %collective-permute-start.25 = (bf16[256,2048]{1,0:T(8,128)(2,1)}, bf16[256,2048]{1,0:T(8,128)(2,1)S(1)}, u32[]{:S(2)}, u32[]{:S(2)}) collective-permute-start(bf16[256,2048]{1,0:T(8,128)(2,1)} %get-tuple-element.453), channel_id=1, source_target_pairs={{0,2},{2,4},{1,3},{3,5},{8,10},{10,12},{9,11},{11,13},{16,18},{18,... | collective-permute-start | bytes 3145736 | tf_op jit(solution)/shard_map/ppermute | solution.py:95
  801.0 30.4 %all-to-all-start.20 = ((bf16[8,64,2048]{2,1,0:T(8,128)(2,1)}), bf16[8,64,2048]{2,1,0:T(8,128)(2,1)S(1)}, u32[]{:S(2)}, u32[]{:S(2)}) async-start(bf16[8,64,2048]{2,1,0:T(8,128)(2,1)} %bitcast.319), calls=%async_computation.22 | async-start | bytes 4194304 | tf_op jit(solution)/shard_map/all_to_all | solution.py:848
  804.7 93.8 %reduce-scatter.8.cloned.1.call-start = ((), (), s32[]{:S(2)}) async-start(), calls=%async_computation.30 | async-start | bytes 5242880 | tf_op jit(solution)/shard_map/reduce_scatter | solution.py:1072
  808.1 30.6 %collective-permute-start.33 = (bf16[32,2048]{1,0:T(8,128)(2,1)}, bf16[32,2048]{1,0:T(8,128)(2,1)}, u32[]{:S(2)}, u32[]{:S(2)}) collective-permute-start(bf16[32,2048]{1,0:T(8,128)(2,1)} %get-tuple-element.517), channel_id=1, source_target_pairs={{0,4},{2,6},{4,0},{6,2},{1,5},{3,7},{5,1},{7,3},{8,12},{10,14},{12... | collective-permute-start | bytes 393224 | tf_op jit(solution)/shard_map/ppermute | solution.py:122
  808.7 31.5 %collective-permute-start.34 = (bf16[32,2048]{1,0:T(8,128)(2,1)}, bf16[32,2048]{1,0:T(8,128)(2,1)S(1)}, u32[]{:S(2)}, u32[]{:S(2)}) collective-permute-start(bf16[32,2048]{1,0:T(8,128)(2,1)} %get-tuple-element.516), channel_id=1, source_target_pairs={{0,6},{2,4},{4,2},{6,0},{1,7},{3,5},{5,3},{7,1},{8,14},{10,12},{12... | collective-permute-start | bytes 393224 | tf_op jit(solution)/shard_map/ppermute | solution.py:122
  845.0 31.7 %collective-permute-start.46 = (bf16[32,2048]{1,0:T(8,128)(2,1)}, bf16[32,2048]{1,0:T(8,128)(2,1)}, u32[]{:S(2)}, u32[]{:S(2)}) collective-permute-start(bf16[32,2048]{1,0:T(8,128)(2,1)} %get-tuple-element.509), channel_id=1, source_target_pairs={{0,24},{8,16},{16,8},{24,0},{1,25},{9,17},{17,9},{25,1},{2,26},{10... | collective-permute-start | bytes 393224 | tf_op jit(solution)/shard_map/ppermute | solution.py:122
  853.8 42.8 %all-to-all-start.21 = ((f32[32,1,2432]{2,1,0:T(1,128)}), f32[32,1,2432]{2,1,0:T(1,128)S(1)}, u32[]{:S(2)}, u32[]{:S(2)}) async-start(f32[32,1,2432]{2,1,0:T(1,128)} %copy.182), calls=%async_computation.24 | async-start | bytes 622592 | tf_op jit(solution)/shard_map/all_to_all | solution.py:1101
  (105 other events, 1464.1 us)
Sparse Core Ops, SparseCore 0:
  25.9 97.8 all-gather.3
  206.2 77.2 reduce-scatter.3
  607.7 77.1 all-gather.7
  811.3 85.0 reduce-scatter.7
Sparse Core Ops, SparseCore 1:
  139.4 53.5 all-gather.5
  723.5 51.5 reduce-scatter.5

commit v5 on v4

--- a/solution.py
+++ b/solution.py
@@ -388,6 +388,33 @@
         [full(*key.shape), full(*value.shape), full(*small.shape)],
         [((STEPS, rows, lanes), BF)],
         [full(STEPS, rows, lanes)],
+    )[0]
+
+
+def _gain_kernel(grad_ref, value_ref, gain_ref, out_ref):
+    @pl.when(pl.program_id(0) == 0)
+    def _():
+        out_ref[...] = jnp.zeros_like(out_ref)
+
+    product = grad_ref[...].astype(F32) * value_ref[...].astype(F32)
+    out_ref[...] += jnp.sum(product, axis=0, keepdims=True)
+
+    @pl.when(pl.program_id(0) == pl.num_programs(0) - 1)
+    def _():
+        out_ref[...] = out_ref[...] / gain_ref[...]
+
+
+def gain_sum(grad, value, gain):
+    tokens, width = grad.shape
+    tile = pl.BlockSpec((tokens // STEPS, width), lambda i: (i, 0))
+    return run(
+        _gain_kernel,
+        "gain_sum",
+        (STEPS,),
+        (grad, value, gain),
+        [tile, tile, full(1, width)],
+        [((1, width), F32)],
+        [full(1, width)],
     )[0]
 
 
@@ -826,7 +853,7 @@
     packed = pack(key_matrix, value_matrix, small)
     arrived = lax.all_gather(layer_input, "z", axis=0, tiled=True)
     query_own = from_dps(w_query, dp).reshape(width, own_cols)
-    packed = lax.all_to_all(packed, "z", split_axis=0, concat_axis=0, tiled=True)
+    packed = exchange(packed, "z")
     packed, w_out, order, where_block = hold(packed, w_out, order, where_block)
     w_back = lax.all_to_all(w_out, "dp", split_axis=0, concat_axis=0, tiled=True)
 
@@ -911,7 +938,7 @@
         arrived, attn_gain_all, w_in, cosine, sine, query_gain_s, key_gain_f, tokens
     )
     pieces = [key_value_rows, *other_cores(key_value_rows)]
-    queries, g_up, g_down, g0, *pieces = hold(queries, g_up, g_down, g0, *pieces)
+    queries, g_up, g_down, *pieces = hold(queries, g_up, g_down, *pieces)
     g_up2, g_down2 = spread_second(g_up, g_down)
     g1 = to_plane(dispatch(zs, back[1], [g_up, g_down], FIRST))
     mixed, log_totals = attend(table, queries, pieces, query_at, opens, tokens)
@@ -1079,8 +1106,7 @@
     key_value_grad = sum_over_cores(
         [part[:, :, 0] for part in by_core(key_value_grad, 2)]
     ).astype(BF)
-    attn_gain_grad = jnp.sum(normed_grad.astype(F32) * normed.astype(F32), axis=0)[None, :]
-    attn_gain_grad = attn_gain_grad / attn_gain_all
+    attn_gain_grad = gain_sum(normed_grad, normed, attn_gain_all)
 
     def to_owners(value):
         columns = value.shape[0]

time: 923 us -> 918 us (level)
  waiting for transfers between devices: 246 us -> 235 us
    ppermute x9 -> x12, starting transfers between devices: 16.4 us -> 22.2 us  [exchange(): got = lax.ppermute(piece, axis, [(i, i ^ k) for i in range(size)])]
    pallas_call x44 -> x45, Pallas kernels: 333 us -> 338 us  [run(): pl.pallas_call(kernel, grid_spec=pltpu.PrefetchScalarGridSpec(num_scalar_...]
    unnamed x131 -> x133, local copies, waits for them, and re-layouts: 18.1 us -> 19 us
  transfers between devices with their start and end apart: 75 -> 77, of which waited for: 31 -> 31; matrix products, arithmetic and copies ran while one was open for 12% -> 12% of each run, Pallas kernels for 31% -> 32%
where the time goes in v5:
time: 918 us; the launch traced here: 904 us
  Pallas kernels  338 us (37%)
  waiting for transfers between devices  235 us (26%)
  starting transfers between devices  176 us (19%)
  local copies, waits for them, and re-layouts  78.3 us (9%)
  other arithmetic  41.8 us (5%)
  between operations  30.9 us (3%)
    pallas_call x45, Pallas kernels, run(): pl.pallas_call(kernel, grid_spec=pltpu.PrefetchScalarGridSpec(num_scalar_...  338 us
    all_to_all x17, waiting for transfers between devices, to_plane(): return lax.all_to_all(rows, PLANE, split_axis=0, concat_axis=0, tiled=True)  140 us
    all_to_all x17, starting transfers between devices, to_plane(): return lax.all_to_all(rows, PLANE, split_axis=0, concat_axis=0, tiled=True)  70 us
    ppermute x12, starting transfers between devices, exchange(): got = lax.ppermute(piece, axis, [(i, i ^ k) for i in range(size)])  22.2 us
    unnamed x133, local copies, waits for them, and re-layouts  19 us
  transfers between devices with their start and end apart: 77, of which 31 were waited for; matrix products, arithmetic and copies ran while one was open for 12% of the time, Pallas kernels for 32%

profile of v5, /device:TPU:0, one launch (start us, length us, event | category | flops | bytes accessed | tf_op | source)
XLA Modules:
  0.0 904.0 jit_solution(13270045851806864255)
XLA Ops:
  63.1 13.0 %collective-permute-done.9 = bf16[512,384]{1,0:T(8,128)(2,1)S(1)} collective-permute-done((bf16[512,384]{1,0:T(8,128)(2,1)S(1)}, bf16[512,384]{1,0:T(8,128)(2,1)S(1)}, u32[]{:S(2)}, u32[]{:S(2)}) %collective-permute-start.9) | collective-permute-done | bytes 393248 | tf_op jit(solution)/shard_map/ppermute | solution.py:132
  121.8 13.3 %project.1 = (bf16[1024,2048]{1,0:T(8,128)(2,1)}, f32[1024,1280]{1,0:T(8,128)}, bf16[1024,1024]{1,0:T(8,128)(2,1)}, bf16[1024,256]{1,0:T(8,128)(2,1)}) custom-call(bf16[1024,2048]{1,0:T(8,128)(2,1)} %all-gather.4.cloned.1.call-done.x_ref, f32[1,2048]{1,0:T(1,128)} %bitcast.370, bf16[2048,1280]{1,0:T(8,128)(2,1)} %pad_maximum_fusion.w_ref, ...), custom_call_target="tpu_custom_call" | custom-call | flops 99999997952 | bytes 1 | tf_op jit(solution)/shard_map/project/pallas_call | solution.py:176
  153.0 19.1 %attend.1 = (bf16[1024,1024]{1,0:T(8,128)(2,1)}, f32[8,1024,128]{2,1,0:T(8,128)}) custom-call(s32[8]{0:T(128)S(1)} %pad_add_fusion.table, bf16[1024,256]{1,0:T(8,128)(2,1)} %get-tuple-element.277.refs_0_, bf16[1024,256]{1,0:T(8,128)(2,1)} %collective-permute-done.13.refs_1_, bf16[1024,1024]{1,0:T(8,128)(2,1)} %get-tuple-element.279.refs_2_, ...), custom_call_target="tpu_custom_call" | custom-call | flops 99999997952 | bytes 1 | tf_op jit(solution)/shard_map/attend/pallas_call | solution.py:176
  174.9 11.0 %all-gather.6.cloned.1.call-done = bf16[1024,2048]{1,0:T(8,128)(2,1)} async-done(((bf16[128,2048]{1,0:T(8,128)(2,1)}), bf16[1024,2048]{1,0:T(8,128)(2,1)}) %all-gather.6.cloned.1.call-update) | async-done | bytes 4194320 | tf_op jit(solution)/shard_map/all_gather | solution.py:889
  190.6 8.4 matmul_nn.5
  216.6 21.5 %all-to-all-done.4 = bf16[8,64,2048]{2,1,0:T(8,128)(2,1)} async-done(((bf16[8,64,2048]{2,1,0:T(8,128)(2,1)}), bf16[8,64,2048]{2,1,0:T(8,128)(2,1)}, u32[]{:S(2)}, u32[]{:S(2)}) %all-to-all-start.4) | async-done | bytes 2097184 | tf_op jit(solution)/shard_map/all_to_all | solution.py:875
  255.9 16.2 %all-to-all-done.5 = bf16[8,64,2048]{2,1,0:T(8,128)(2,1)S(1)} async-done(((bf16[8,64,2048]{2,1,0:T(8,128)(2,1)}), bf16[8,64,2048]{2,1,0:T(8,128)(2,1)S(1)}, u32[]{:S(2)}, u32[]{:S(2)}) %all-to-all-start.5) | async-done | bytes 2097184 | tf_op jit(solution)/shard_map/all_to_all | solution.py:875
  311.2 13.5 %collective-permute-done.17.refs_0_ = bf16[256,2048]{1,0:T(8,128)(2,1)S(1)} collective-permute-done((bf16[256,2048]{1,0:T(8,128)(2,1)S(1)}, bf16[256,2048]{1,0:T(8,128)(2,1)S(1)}, u32[]{:S(2)}, u32[]{:S(2)}) %collective-permute-start.17) | collective-permute-done | bytes 1048608 | tf_op jit(solution)/shard_map/ppermute | solution.py:68
  339.1 12.6 %expert.4 = (bf16[512,2048]{1,0:T(8,128)(2,1)}, bf16[512,768]{1,0:T(8,128)(2,1)}, bf16[512,768]{1,0:T(8,128)(2,1)}, bf16[512,768]{1,0:T(8,128)(2,1)}, f32[512,1]{1,0:T(8,128)}) custom-call(bf16[512,2048]{1,0:T(8,128)(2,1)} %bitcast.79.x_ref.refs_0_, f32[512,768]{1,0:T(8,128)} %matmul_nt.5.pulled_ref, bf16[512,128]{1,0:T(8,128)(2,1)} %bitcast.359, ...), custom_call_target="tpu_custom_call" | custom-call | flops 99999997952 | bytes 1 | tf_op jit(solution)/shard_map/expert/pallas_call | solution.py:176
  351.7 9.1 %collective-permute-done.20.refs_3_.refs_1_ = bf16[256,2048]{1,0:T(8,128)(2,1)S(1)} collective-permute-done((bf16[256,2048]{1,0:T(8,128)(2,1)}, bf16[256,2048]{1,0:T(8,128)(2,1)S(1)}, u32[]{:S(2)}, u32[]{:S(2)}) %collective-permute-start.20) | collective-permute-done | bytes 1048608 | tf_op jit(solution)/shard_map/ppermute | solution.py:76
  372.3 12.7 %expert.5 = (bf16[512,2048]{1,0:T(8,128)(2,1)}, bf16[512,768]{1,0:T(8,128)(2,1)}, bf16[512,768]{1,0:T(8,128)(2,1)}, bf16[512,768]{1,0:T(8,128)(2,1)}, f32[512,1]{1,0:T(8,128)}) custom-call(bf16[512,2048]{1,0:T(8,128)(2,1)} %bitcast.83.x_ref.refs_1_, f32[512,768]{1,0:T(8,128)} %matmul_nt.6.pulled_ref, bf16[512,128]{1,0:T(8,128)(2,1)} %bitcast.358, ...), custom_call_target="tpu_custom_call" | custom-call | flops 99999997952 | bytes 1 | tf_op jit(solution)/shard_map/expert/pallas_call | solution.py:176
  385.0 7.9 collective-permute-done.21.refs_2_
  404.6 12.6 %expert.6 = (bf16[512,2048]{1,0:T(8,128)(2,1)}, bf16[512,768]{1,0:T(8,128)(2,1)}, bf16[512,768]{1,0:T(8,128)(2,1)}, bf16[512,768]{1,0:T(8,128)(2,1)}, f32[512,1]{1,0:T(8,128)}) custom-call(bf16[512,2048]{1,0:T(8,128)(2,1)} %bitcast.296, f32[512,768]{1,0:T(8,128)} %matmul_nt.7.pulled_ref, bf16[512,128]{1,0:T(8,128)(2,1)} %bitcast.357, ...), custom_call_target="tpu_custom_call" | custom-call | flops 99999997952 | bytes 1 | tf_op jit(solution)/shard_map/expert/pallas_call | solution.py:176
  417.3 14.0 %all-to-all-done.10 = bf16[8,64,2048]{2,1,0:T(8,128)(2,1)} async-done(((bf16[8,64,2048]{2,1,0:T(8,128)(2,1)}), bf16[8,64,2048]{2,1,0:T(8,128)(2,1)}, u32[]{:S(2)}, u32[]{:S(2)}) %all-to-all-start.10) | async-done | bytes 2097184 | tf_op jit(solution)/shard_map/all_to_all | solution.py:875
  431.3 12.6 %expert.7 = (bf16[512,2048]{1,0:T(8,128)(2,1)}, bf16[512,768]{1,0:T(8,128)(2,1)}, bf16[512,768]{1,0:T(8,128)(2,1)}, bf16[512,768]{1,0:T(8,128)(2,1)}, f32[512,1]{1,0:T(8,128)}) custom-call(bf16[512,2048]{1,0:T(8,128)(2,1)} %bitcast.87.x_ref.refs_3_, f32[512,768]{1,0:T(8,128)} %matmul_nt.8.pulled_ref, bf16[512,128]{1,0:T(8,128)(2,1)} %bitcast.356, ...), custom_call_target="tpu_custom_call" | custom-call | flops 99999997952 | bytes 1 | tf_op jit(solution)/shard_map/expert/pallas_call | solution.py:176
  459.7 14.8 %all-to-all-done.11 = bf16[8,64,2048]{2,1,0:T(8,128)(2,1)S(1)} async-done(((bf16[8,64,2048]{2,1,0:T(8,128)(2,1)}), bf16[8,64,2048]{2,1,0:T(8,128)(2,1)S(1)}, u32[]{:S(2)}, u32[]{:S(2)}) %all-to-all-start.11) | async-done | bytes 2097184 | tf_op jit(solution)/shard_map/all_to_all | solution.py:875
  487.6 6.5 collective-permute-start.22
  494.1 15.4 %all-to-all-done.12 = bf16[8,64,2048]{2,1,0:T(8,128)(2,1)S(1)} async-done(((bf16[8,64,2048]{2,1,0:T(8,128)(2,1)}), bf16[8,64,2048]{2,1,0:T(8,128)(2,1)S(1)}, u32[]{:S(2)}, u32[]{:S(2)}) %all-to-all-start.12) | async-done | bytes 2097184 | tf_op jit(solution)/shard_map/all_to_all | solution.py:875
  530.2 10.8 %all-to-all-done.13 = bf16[8,64,2048]{2,1,0:T(8,128)(2,1)S(1)} async-done(((bf16[8,64,2048]{2,1,0:T(8,128)(2,1)}), bf16[8,64,2048]{2,1,0:T(8,128)(2,1)S(1)}, u32[]{:S(2)}, u32[]{:S(2)}) %all-to-all-start.13) | async-done | bytes 2097184 | tf_op jit(solution)/shard_map/all_to_all | solution.py:875
  564.0 9.3 %all-to-all-done.14 = bf16[8,64,2048]{2,1,0:T(8,128)(2,1)} async-done(((bf16[8,64,2048]{2,1,0:T(8,128)(2,1)}), bf16[8,64,2048]{2,1,0:T(8,128)(2,1)}, u32[]{:S(2)}, u32[]{:S(2)}) %all-to-all-start.14) | async-done | bytes 2097184 | tf_op jit(solution)/shard_map/all_to_all | solution.py:875
  580.9 11.1 %all-to-all-done.15 = f32[32,1,64]{2,1,0:T(1,128)S(1)} async-done(((f32[32,1,64]{2,1,0:T(1,128)}), f32[32,1,64]{2,1,0:T(1,128)S(1)}, u32[]{:S(2)}, u32[]{:S(2)}) %all-to-all-start.15) | async-done | bytes 8224 | tf_op jit(solution)/shard_map/all_to_all | solution.py:1035
  605.1 13.1 %contract_chunks.3 = f32[768,2048]{1,0:T(8,128)} custom-call(bf16[512,768]{1,0:T(8,128)(2,1)} %get-tuple-element.412.a_ref.refs_0_, bf16[512,768]{1,0:T(8,128)(2,1)} %get-tuple-element.413.a_ref.refs_1_, bf16[512,768]{1,0:T(8,128)(2,1)} %get-tuple-element.414.a_ref.refs_2_, bf16[512,768]{1,0:T(8,128)(2,1)} %get-tuple-element.415.a_ref.refs_3_, ...), custom_call_target="tpu_custom_call" | custom-call | flops 1 | bytes 1 | tf_op jit(solution)/shard_map/contract_chunks/pallas_call | solution.py:176
  619.1 12.5 %all-to-all-done.16 = bf16[8,64,2048]{2,1,0:T(8,128)(2,1)S(1)} async-done(((bf16[8,64,2048]{2,1,0:T(8,128)(2,1)}), bf16[8,64,2048]{2,1,0:T(8,128)(2,1)S(1)}, u32[]{:S(2)}, u32[]{:S(2)}) %all-to-all-start.16) | async-done | bytes 2097184 | tf_op jit(solution)/shard_map/all_to_all | solution.py:875
  640.1 13.1 %contract_chunks.4 = f32[2048,768]{1,0:T(8,128)} custom-call(bf16[512,2048]{1,0:T(8,128)(2,1)} %bitcast.79.x_ref.refs_0_, bf16[512,2048]{1,0:T(8,128)(2,1)} %bitcast.83.x_ref.refs_1_, bf16[512,2048]{1,0:T(8,128)(2,1)} %bitcast.297, bf16[512,2048]{1,0:T(8,128)(2,1)} %bitcast.87.x_ref.refs_3_, bf16[512,768]{1,0:T(8,128)(2,1)} %get-tuple-element.424.refs_4_, ...), custom_call_target="tpu_custom_call" | custom-call | flops 1 | bytes 1 | tf_op jit(solution)/shard_map/contract_chunks/pallas_call | solution.py:176
  653.1 10.0 %all-to-all-done.17 = bf16[8,64,2048]{2,1,0:T(8,128)(2,1)S(1)} async-done(((bf16[8,64,2048]{2,1,0:T(8,128)(2,1)}), bf16[8,64,2048]{2,1,0:T(8,128)(2,1)S(1)}, u32[]{:S(2)}, u32[]{:S(2)}) %all-to-all-start.17) | async-done | bytes 2097184 | tf_op jit(solution)/shard_map/all_to_all | solution.py:875
  669.0 13.1 %contract_chunks.5 = f32[2048,768]{1,0:T(8,128)} custom-call(bf16[512,2048]{1,0:T(8,128)(2,1)} %bitcast.79.x_ref.refs_0_, bf16[512,2048]{1,0:T(8,128)(2,1)} %bitcast.83.x_ref.refs_1_, bf16[512,2048]{1,0:T(8,128)(2,1)} %bitcast.298, bf16[512,2048]{1,0:T(8,128)(2,1)} %bitcast.87.x_ref.refs_3_, bf16[512,768]{1,0:T(8,128)(2,1)} %get-tuple-element.433.refs_4_, ...), custom_call_target="tpu_custom_call" | custom-call | flops 1 | bytes 1 | tf_op jit(solution)/shard_map/contract_chunks/pallas_call | solution.py:176
  684.4 8.6 matmul_nt.9.refs_3_
  693.0 8.5 matmul_tn.2
  717.3 27.3 %attend_back.2 = (bf16[768,1024]{1,0:T(8,128)(2,1)}, f32[1024,256]{1,0:T(8,128)}, f32[1024,256]{1,0:T(8,128)}) custom-call(s32[8]{0:T(128)S(1)} %pad_add_fusion.table, bf16[1024,256]{1,0:T(8,128)(2,1)} %get-tuple-element.277.refs_0_, bf16[1024,256]{1,0:T(8,128)(2,1)} %collective-permute-done.13.refs_1_, bf16[1024,1024]{1,0:T(8,128)(2,1)} %get-tuple-element.279.refs_2_, ...), custom_call_target="tpu_custom_call" | custom-call | flops 99999997952 | bytes 1 | tf_op jit(solution)/shard_map/attend_back/pallas_call | solution.py:176
  755.5 17.3 %attend_back.3 = (bf16[256,1024]{1,0:T(8,128)(2,1)}, f32[1024,256]{1,0:T(8,128)}, f32[1024,256]{1,0:T(8,128)}) custom-call(s32[8]{0:T(128)S(1)} %pad_add_fusion.table, bf16[1024,256]{1,0:T(8,128)(2,1)} %get-tuple-element.277.refs_0_, bf16[1024,256]{1,0:T(8,128)(2,1)} %collective-permute-done.13.refs_1_, bf16[1024,1024]{1,0:T(8,128)(2,1)} %get-tuple-element.279.refs_2_, ...), custom_call_target="tpu_custom_call" | custom-call | flops 99999997952 | bytes 1 | tf_op jit(solution)/shard_map/attend_back/pallas_call | solution.py:176
  780.5 14.3 %project_back.1 = (bf16[1024,2048]{1,0:T(8,128)(2,1)}, bf16[1024,1280]{1,0:T(8,128)(2,1)}, f32[1,128]{1,0:T(1,128)}, f32[1,128]{1,0:T(1,128)}) custom-call(f32[1024,1280]{1,0:T(8,128)} %get-tuple-element.308.raw_ref, bf16[768,1024]{1,0:T(8,128)(2,1)} %get-tuple-element.454.near_ref, bf16[256,1024]{1,0:T(8,128)(2,1)} %get-tuple-element.467.last_ref, ...), custom_call_target="tpu_custom_call" | custom-call | flops 99999997952 | bytes 1 | tf_op jit(solution)/shard_map/project_back/pallas_call | solution.py:176
  810.2 9.7 %matmul_tn.3 = bf16[2048,1280]{1,0:T(8,128)(2,1)} custom-call(bf16[1024,2048]{1,0:T(8,128)(2,1)} %get-tuple-element.307.a_ref.value_ref, bf16[1024,1280]{1,0:T(8,128)(2,1)} %get-tuple-element.479.b_ref), custom_call_target="tpu_custom_call" | custom-call | flops 1 | bytes 1 | tf_op jit(solution)/shard_map/matmul_tn/pallas_call | solution.py:176
  (483 shorter events, 460.3 us)
Async XLA Ops:
  8.0 113.8 %all-gather.4.cloned.1.call-start = ((), (), s32[]{:S(2)}) async-start(), calls=%async_computation.24 | async-start | bytes 5242880 | tf_op jit(solution)/shard_map/all_gather | solution.py:854
  8.1 31.2 %collective-permute-start = (bf16[512,512]{1,0:T(8,128)(2,1)}, bf16[512,512]{1,0:T(8,128)(2,1)S(1)}, u32[]{:S(2)}, u32[]{:S(2)}) collective-permute-start(bf16[512,512]{1,0:T(8,128)(2,1)} %param.20), channel_id=1, source_target_pairs={{0,8},{8,0},{16,24},{24,16},{1,9},{9,1},{17,25},{25,17},{2,10},{10... | collective-permute-start | bytes 1572872 | tf_op jit(solution)/shard_map/ppermute | solution.py:132
  41.8 36.0 %collective-permute-start.3 = (bf16[2048,512]{1,0:T(8,128)(2,1)}, bf16[2048,512]{1,0:T(8,128)(2,1)}, u32[]{:S(2)}, u32[]{:S(2)}) collective-permute-start(bf16[2048,512]{1,0:T(8,128)(2,1)} %bitcast.4), channel_id=1, source_target_pairs={{1,0},{0,1},{3,2},{2,3},{5,4},{4,5},{7,6},{6,7},{9,8},{8,9},{11,10... | collective-permute-start | bytes 6291464 | tf_op jit(solution)/shard_map/ppermute | solution.py:140
  101.8 35.7 %collective-permute-start.11 = (bf16[256,2048]{1,0:T(8,128)(2,1)S(1)}, bf16[256,2048]{1,0:T(8,128)(2,1)S(1)}, u32[]{:S(2)}, u32[]{:S(2)}) collective-permute-start(bf16[256,2048]{1,0:T(8,128)(2,1)S(1)} %copy-done.10), channel_id=1, source_target_pairs={{0,2},{2,4},{4,6},{1,3},{3,5},{5,7},{8,10},{10,12},{12,14},{9,11},... | collective-permute-start | bytes 3145736 | tf_op jit(solution)/shard_map/ppermute | solution.py:68
  105.7 31.8 %collective-permute-start.12 = (bf16[256,2048]{1,0:T(8,128)(2,1)S(1)}, bf16[256,2048]{1,0:T(8,128)(2,1)S(1)}, u32[]{:S(2)}, u32[]{:S(2)}) collective-permute-start(bf16[256,2048]{1,0:T(8,128)(2,1)S(1)} %copy-done.10), channel_id=1, source_target_pairs={{2,0},{4,2},{6,4},{3,1},{5,3},{7,5},{10,8},{12,10},{14,12},{11,9},... | collective-permute-start | bytes 3145736 | tf_op jit(solution)/shard_map/ppermute | solution.py:69
  116.9 31.7 %all-to-all-start.2 = ((bf16[8,64,2048]{2,1,0:T(8,128)(2,1)}), bf16[8,64,2048]{2,1,0:T(8,128)(2,1)}, u32[]{:S(2)}, u32[]{:S(2)}) async-start(bf16[8,64,2048]{2,1,0:T(8,128)(2,1)} %bitcast.314), calls=%async_computation.2 | async-start | bytes 4194304 | tf_op jit(solution)/shard_map/all_to_all | solution.py:875
  121.3 64.6 %all-gather.6.cloned.1.call-start = ((), (), s32[]{:S(2)}) async-start(), calls=%async_computation.25 | async-start | bytes 4718592 | tf_op jit(solution)/shard_map/all_gather | solution.py:889
  138.6 33.6 %collective-permute-start.14 = (bf16[256,2048]{1,0:T(8,128)(2,1)S(1)}, bf16[256,2048]{1,0:T(8,128)(2,1)S(1)}, u32[]{:S(2)}, u32[]{:S(2)}) collective-permute-start(bf16[256,2048]{1,0:T(8,128)(2,1)S(1)} %collective-permute-done.11.refs_0_), channel_id=1, source_target_pairs={{2,4},{4,6},{3,5},{5,7},{10,12},{12,14},{11,13},{13,15},{18,20},{2... | collective-permute-start | bytes 3145736 | tf_op jit(solution)/shard_map/ppermute | solution.py:75
  139.3 32.9 %collective-permute-start.15 = (bf16[256,2048]{1,0:T(8,128)(2,1)}, bf16[256,2048]{1,0:T(8,128)(2,1)S(1)}, u32[]{:S(2)}, u32[]{:S(2)}) collective-permute-start(bf16[256,2048]{1,0:T(8,128)(2,1)} %copy-done.26), channel_id=1, source_target_pairs={{4,2},{2,0},{5,3},{3,1},{12,10},{10,8},{13,11},{11,9},{20,18},{18,... | collective-permute-start | bytes 3145736 | tf_op jit(solution)/shard_map/ppermute | solution.py:76
  148.6 50.4 %all-to-all-start.3 = ((bf16[8,64,2048]{2,1,0:T(8,128)(2,1)}), bf16[8,64,2048]{2,1,0:T(8,128)(2,1)}, u32[]{:S(2)}, u32[]{:S(2)}) async-start(bf16[8,64,2048]{2,1,0:T(8,128)(2,1)} %bitcast.319), calls=%async_computation.3 | async-start | bytes 4194304 | tf_op jit(solution)/shard_map/all_to_all | solution.py:875
  153.0 134.0 %reduce-scatter.4.cloned.1.call-start = ((), (), s32[]{:S(2)}) async-start(), calls=%async_computation.26 | async-start | bytes 5242880 | tf_op jit(solution)/shard_map/reduce_scatter | solution.py:951
  205.0 33.1 %all-to-all-start.4 = ((bf16[8,64,2048]{2,1,0:T(8,128)(2,1)}), bf16[8,64,2048]{2,1,0:T(8,128)(2,1)}, u32[]{:S(2)}, u32[]{:S(2)}) async-start(bf16[8,64,2048]{2,1,0:T(8,128)(2,1)} %bitcast.324), calls=%async_computation.5 | async-start | bytes 4194304 | tf_op jit(solution)/shard_map/all_to_all | solution.py:875
  295.7 39.0 %all-to-all-start.7 = ((bf16[8,64,2048]{2,1,0:T(8,128)(2,1)}), bf16[8,64,2048]{2,1,0:T(8,128)(2,1)}, u32[]{:S(2)}, u32[]{:S(2)}) async-start(bf16[8,64,2048]{2,1,0:T(8,128)(2,1)} %bitcast.313), calls=%async_computation.8 | async-start | bytes 4194304 | tf_op jit(solution)/shard_map/all_to_all | solution.py:875
  334.7 33.7 %all-to-all-start.8 = ((bf16[8,64,2048]{2,1,0:T(8,128)(2,1)}), bf16[8,64,2048]{2,1,0:T(8,128)(2,1)}, u32[]{:S(2)}, u32[]{:S(2)}) async-start(bf16[8,64,2048]{2,1,0:T(8,128)(2,1)} %bitcast.317), calls=%async_computation.9 | async-start | bytes 4194304 | tf_op jit(solution)/shard_map/all_to_all | solution.py:875
  368.5 30.4 %all-to-all-start.9 = ((bf16[8,64,2048]{2,1,0:T(8,128)(2,1)}), bf16[8,64,2048]{2,1,0:T(8,128)(2,1)S(1)}, u32[]{:S(2)}, u32[]{:S(2)}) async-start(bf16[8,64,2048]{2,1,0:T(8,128)(2,1)} %bitcast.318), calls=%async_computation.10 | async-start | bytes 4194304 | tf_op jit(solution)/shard_map/all_to_all | solution.py:875
  400.3 31.0 %all-to-all-start.10 = ((bf16[8,64,2048]{2,1,0:T(8,128)(2,1)}), bf16[8,64,2048]{2,1,0:T(8,128)(2,1)}, u32[]{:S(2)}, u32[]{:S(2)}) async-start(bf16[8,64,2048]{2,1,0:T(8,128)(2,1)} %bitcast.322), calls=%async_computation.11 | async-start | bytes 4194304 | tf_op jit(solution)/shard_map/all_to_all | solution.py:875
  443.9 30.6 %all-to-all-start.11 = ((bf16[8,64,2048]{2,1,0:T(8,128)(2,1)}), bf16[8,64,2048]{2,1,0:T(8,128)(2,1)S(1)}, u32[]{:S(2)}, u32[]{:S(2)}) async-start(bf16[8,64,2048]{2,1,0:T(8,128)(2,1)} %bitcast.339), calls=%async_computation.12 | async-start | bytes 4194304 | tf_op jit(solution)/shard_map/all_to_all | solution.py:875
  487.6 31.4 %collective-permute-start.22 = (bf16[256,2048]{1,0:T(8,128)(2,1)S(1)}, bf16[256,2048]{1,0:T(8,128)(2,1)}, u32[]{:S(2)}, u32[]{:S(2)}) collective-permute-start(bf16[256,2048]{1,0:T(8,128)(2,1)S(1)} %copy-done.5), channel_id=1, source_target_pairs={{0,2},{6,4},{1,3},{7,5},{8,10},{14,12},{9,11},{15,13},{16,18},{22,... | collective-permute-start | bytes 3145736 | tf_op jit(solution)/shard_map/ppermute | solution.py:90
  542.3 31.0 %all-to-all-start.14 = ((bf16[8,64,2048]{2,1,0:T(8,128)(2,1)}), bf16[8,64,2048]{2,1,0:T(8,128)(2,1)}, u32[]{:S(2)}, u32[]{:S(2)}) async-start(bf16[8,64,2048]{2,1,0:T(8,128)(2,1)} %bitcast.333), calls=%async_computation.15 | async-start | bytes 4194304 | tf_op jit(solution)/shard_map/all_to_all | solution.py:875
  557.2 36.5 %collective-permute-start.25 = (bf16[256,2048]{1,0:T(8,128)(2,1)}, bf16[256,2048]{1,0:T(8,128)(2,1)S(1)}, u32[]{:S(2)}, u32[]{:S(2)}) collective-permute-start(bf16[256,2048]{1,0:T(8,128)(2,1)} %get-tuple-element.392), channel_id=1, source_target_pairs={{0,2},{2,4},{4,6},{1,3},{3,5},{5,7},{8,10},{10,12},{12,14},{9,11},... | collective-permute-start | bytes 3145736 | tf_op jit(solution)/shard_map/ppermute | solution.py:102
  562.7 31.0 %collective-permute-start.26 = (bf16[256,2048]{1,0:T(8,128)(2,1)}, bf16[256,2048]{1,0:T(8,128)(2,1)S(1)}, u32[]{:S(2)}, u32[]{:S(2)}) collective-permute-start(bf16[256,2048]{1,0:T(8,128)(2,1)} %get-tuple-element.393), channel_id=1, source_target_pairs={{6,4},{4,2},{2,0},{7,5},{5,3},{3,1},{14,12},{12,10},{10,8},{15,13}... | collective-permute-start | bytes 3145736 | tf_op jit(solution)/shard_map/ppermute | solution.py:103
  577.4 104.7 %all-gather.8.cloned.1.call-start = ((), (), s32[]{:S(2)}) async-start(), calls=%async_computation.27 | async-start | bytes 5242880 | tf_op jit(solution)/shard_map/all_gather | solution.py:1055
  601.4 30.2 %all-to-all-start.16 = ((bf16[8,64,2048]{2,1,0:T(8,128)(2,1)}), bf16[8,64,2048]{2,1,0:T(8,128)(2,1)S(1)}, u32[]{:S(2)}, u32[]{:S(2)}) async-start(bf16[8,64,2048]{2,1,0:T(8,128)(2,1)} %bitcast.335), calls=%async_computation.17 | async-start | bytes 4194304 | tf_op jit(solution)/shard_map/all_to_all | solution.py:875
  664.4 80.2 %all-to-all-start.18 = ((bf16[8,64,2048]{2,1,0:T(8,128)(2,1)}), bf16[8,64,2048]{2,1,0:T(8,128)(2,1)}, u32[]{:S(2)}, u32[]{:S(2)}) async-start(bf16[8,64,2048]{2,1,0:T(8,128)(2,1)} %bitcast.334), calls=%async_computation.19 | async-start | bytes 4194304 | tf_op jit(solution)/shard_map/all_to_all | solution.py:875
  668.8 104.0 %reduce-scatter.6.cloned.1.call-start = ((), (), s32[]{:S(2)}) async-start(), calls=%async_computation.28 | async-start | bytes 4718592 | tf_op jit(solution)/shard_map/reduce_scatter | solution.py:1076
  712.1 32.5 %collective-permute-start.28 = (bf16[256,2048]{1,0:T(8,128)(2,1)}, bf16[256,2048]{1,0:T(8,128)(2,1)S(1)}, u32[]{:S(2)}, u32[]{:S(2)}) collective-permute-start(bf16[256,2048]{1,0:T(8,128)(2,1)} %get-tuple-element.451), channel_id=1, source_target_pairs={{0,2},{2,4},{1,3},{3,5},{8,10},{10,12},{9,11},{11,13},{16,18},{18,... | collective-permute-start | bytes 3145736 | tf_op jit(solution)/shard_map/ppermute | solution.py:95
  794.8 30.2 %all-to-all-start.19 = ((bf16[8,64,2048]{2,1,0:T(8,128)(2,1)}), bf16[8,64,2048]{2,1,0:T(8,128)(2,1)S(1)}, u32[]{:S(2)}, u32[]{:S(2)}) async-start(bf16[8,64,2048]{2,1,0:T(8,128)(2,1)} %bitcast.332), calls=%async_computation.21 | async-start | bytes 4194304 | tf_op jit(solution)/shard_map/all_to_all | solution.py:875
  798.4 93.5 %reduce-scatter.8.cloned.1.call-start = ((), (), s32[]{:S(2)}) async-start(), calls=%async_computation.29 | async-start | bytes 5242880 | tf_op jit(solution)/shard_map/reduce_scatter | solution.py:1099
  802.0 30.3 %collective-permute-start.36 = (bf16[32,2048]{1,0:T(8,128)(2,1)}, bf16[32,2048]{1,0:T(8,128)(2,1)}, u32[]{:S(2)}, u32[]{:S(2)}) collective-permute-start(bf16[32,2048]{1,0:T(8,128)(2,1)} %get-tuple-element.515), channel_id=1, source_target_pairs={{0,4},{2,6},{4,0},{6,2},{1,5},{3,7},{5,1},{7,3},{8,12},{10,14},{12... | collective-permute-start | bytes 393224 | tf_op jit(solution)/shard_map/ppermute | solution.py:122
  802.6 31.2 %collective-permute-start.37 = (bf16[32,2048]{1,0:T(8,128)(2,1)}, bf16[32,2048]{1,0:T(8,128)(2,1)S(1)}, u32[]{:S(2)}, u32[]{:S(2)}) collective-permute-start(bf16[32,2048]{1,0:T(8,128)(2,1)} %get-tuple-element.514), channel_id=1, source_target_pairs={{0,6},{2,4},{4,2},{6,0},{1,7},{3,5},{5,3},{7,1},{8,14},{10,12},{12... | collective-permute-start | bytes 393224 | tf_op jit(solution)/shard_map/ppermute | solution.py:122
  838.7 31.7 %collective-permute-start.49 = (bf16[32,2048]{1,0:T(8,128)(2,1)}, bf16[32,2048]{1,0:T(8,128)(2,1)}, u32[]{:S(2)}, u32[]{:S(2)}) collective-permute-start(bf16[32,2048]{1,0:T(8,128)(2,1)} %get-tuple-element.507), channel_id=1, source_target_pairs={{0,24},{8,16},{16,8},{24,0},{1,25},{9,17},{17,9},{25,1},{2,26},{10... | collective-permute-start | bytes 393224 | tf_op jit(solution)/shard_map/ppermute | solution.py:122
  847.5 42.4 %all-to-all-start.20 = ((f32[32,1,2432]{2,1,0:T(1,128)}), f32[32,1,2432]{2,1,0:T(1,128)S(1)}, u32[]{:S(2)}, u32[]{:S(2)}) async-start(f32[32,1,2432]{2,1,0:T(1,128)} %copy.210), calls=%async_computation.23 | async-start | bytes 622592 | tf_op jit(solution)/shard_map/all_to_all | solution.py:1127
  (108 other events, 1417.9 us)
Sparse Core Ops, SparseCore 0:
  24.5 92.6 all-gather.3
  201.2 77.6 reduce-scatter.3
  601.5 77.1 all-gather.7
  801.3 87.6 reduce-scatter.7
Sparse Core Ops, SparseCore 1:
  137.7 48.2 all-gather.5
  717.4 51.5 reduce-scatter.5

commit v6 on v5

--- a/solution.py
+++ b/solution.py
@@ -307,7 +307,7 @@
 
 def add_and_norm(x, gain, terms):
     tokens, width = x.shape
-    step = min(tokens, 64)
+    step = min(tokens, 128)
     tile = pl.BlockSpec((step, width), lambda i: (i, 0))
     return run(
         _norm_kernel,
@@ -348,7 +348,7 @@
 
 def norm_back(value, gain, above, terms, logit_grad=None, router=None):
     tokens, width = value.shape
-    step = min(tokens, 64)
+    step = min(tokens, 128)
     tile = pl.BlockSpec((step, width), lambda i: (i, 0))
     operands, specs = [value, gain, above], [tile, full(1, width), tile]
     outs, out_specs = [((tokens, width), F32)], [tile]

time: 918 us -> 915 us (level)
  transfers between devices with their start and end apart: 77 -> 77, of which waited for: 31 -> 30; matrix products, arithmetic and copies ran while one was open for 12% -> 12% of each run, Pallas kernels for 32% -> 32%
where the time goes in v6:
time: 915 us; the launch traced here: 901 us
  Pallas kernels  335 us (37%)
  waiting for transfers between devices  234 us (26%)
  starting transfers between devices  176 us (19%)
  local copies, waits for them, and re-layouts  78.3 us (9%)
  other arithmetic  41.8 us (5%)
  between operations  30.6 us (3%)
    pallas_call x45, Pallas kernels, run(): pl.pallas_call(kernel, grid_spec=pltpu.PrefetchScalarGridSpec(num_scalar_...  335 us
    all_to_all x17, waiting for transfers between devices, to_plane(): return lax.all_to_all(rows, PLANE, split_axis=0, concat_axis=0, tiled=True)  141 us
    all_to_all x17, starting transfers between devices, to_plane(): return lax.all_to_all(rows, PLANE, split_axis=0, concat_axis=0, tiled=True)  70.4 us
    ppermute x12, starting transfers between devices, exchange(): got = lax.ppermute(piece, axis, [(i, i ^ k) for i in range(size)])  22.3 us
    unnamed x133, local copies, waits for them, and re-layouts  19 us
  transfers between devices with their start and end apart: 77, of which 30 were waited for; matrix products, arithmetic and copies ran while one was open for 12% of the time, Pallas kernels for 32%

profile of v6, /device:TPU:0, one launch (start us, length us, event | category | flops | bytes accessed | tf_op | source)
XLA Modules:
  0.0 901.5 jit_solution(8548646218396930790)
XLA Ops:
  63.1 13.0 %collective-permute-done.9 = bf16[512,384]{1,0:T(8,128)(2,1)S(1)} collective-permute-done((bf16[512,384]{1,0:T(8,128)(2,1)S(1)}, bf16[512,384]{1,0:T(8,128)(2,1)S(1)}, u32[]{:S(2)}, u32[]{:S(2)}) %collective-permute-start.9) | collective-permute-done | bytes 393248 | tf_op jit(solution)/shard_map/ppermute | solution.py:132
  121.5 13.3 %project.1 = (bf16[1024,2048]{1,0:T(8,128)(2,1)}, f32[1024,1280]{1,0:T(8,128)}, bf16[1024,1024]{1,0:T(8,128)(2,1)}, bf16[1024,256]{1,0:T(8,128)(2,1)}) custom-call(bf16[1024,2048]{1,0:T(8,128)(2,1)} %all-gather.4.cloned.1.call-done.x_ref, f32[1,2048]{1,0:T(1,128)} %bitcast.370, bf16[2048,1280]{1,0:T(8,128)(2,1)} %pad_maximum_fusion.w_ref, ...), custom_call_target="tpu_custom_call" | custom-call | flops 99999997952 | bytes 1 | tf_op jit(solution)/shard_map/project/pallas_call | solution.py:176
  153.4 19.1 %attend.1 = (bf16[1024,1024]{1,0:T(8,128)(2,1)}, f32[8,1024,128]{2,1,0:T(8,128)}) custom-call(s32[8]{0:T(128)S(1)} %pad_add_fusion.table, bf16[1024,256]{1,0:T(8,128)(2,1)} %get-tuple-element.277.refs_0_, bf16[1024,256]{1,0:T(8,128)(2,1)} %collective-permute-done.13.refs_1_, bf16[1024,1024]{1,0:T(8,128)(2,1)} %get-tuple-element.279.refs_2_, ...), custom_call_target="tpu_custom_call" | custom-call | flops 99999997952 | bytes 1 | tf_op jit(solution)/shard_map/attend/pallas_call | solution.py:176
  175.3 10.9 %all-gather.6.cloned.1.call-done = bf16[1024,2048]{1,0:T(8,128)(2,1)} async-done(((bf16[128,2048]{1,0:T(8,128)(2,1)}), bf16[1024,2048]{1,0:T(8,128)(2,1)}) %all-gather.6.cloned.1.call-update) | async-done | bytes 4194320 | tf_op jit(solution)/shard_map/all_gather | solution.py:889
  191.0 8.4 matmul_nn.5
  217.0 21.5 %all-to-all-done.4 = bf16[8,64,2048]{2,1,0:T(8,128)(2,1)} async-done(((bf16[8,64,2048]{2,1,0:T(8,128)(2,1)}), bf16[8,64,2048]{2,1,0:T(8,128)(2,1)}, u32[]{:S(2)}, u32[]{:S(2)}) %all-to-all-start.4) | async-done | bytes 2097184 | tf_op jit(solution)/shard_map/all_to_all | solution.py:875
  256.2 16.2 %all-to-all-done.5 = bf16[8,64,2048]{2,1,0:T(8,128)(2,1)S(1)} async-done(((bf16[8,64,2048]{2,1,0:T(8,128)(2,1)}), bf16[8,64,2048]{2,1,0:T(8,128)(2,1)S(1)}, u32[]{:S(2)}, u32[]{:S(2)}) %all-to-all-start.5) | async-done | bytes 2097184 | tf_op jit(solution)/shard_map/all_to_all | solution.py:875
  310.7 13.5 %collective-permute-done.17.refs_0_ = bf16[256,2048]{1,0:T(8,128)(2,1)S(1)} collective-permute-done((bf16[256,2048]{1,0:T(8,128)(2,1)S(1)}, bf16[256,2048]{1,0:T(8,128)(2,1)S(1)}, u32[]{:S(2)}, u32[]{:S(2)}) %collective-permute-start.17) | collective-permute-done | bytes 1048608 | tf_op jit(solution)/shard_map/ppermute | solution.py:68
  339.0 12.6 %expert.4 = (bf16[512,2048]{1,0:T(8,128)(2,1)}, bf16[512,768]{1,0:T(8,128)(2,1)}, bf16[512,768]{1,0:T(8,128)(2,1)}, bf16[512,768]{1,0:T(8,128)(2,1)}, f32[512,1]{1,0:T(8,128)}) custom-call(bf16[512,2048]{1,0:T(8,128)(2,1)} %bitcast.79.x_ref.refs_0_, f32[512,768]{1,0:T(8,128)} %matmul_nt.5.pulled_ref, bf16[512,128]{1,0:T(8,128)(2,1)} %bitcast.359, ...), custom_call_target="tpu_custom_call" | custom-call | flops 99999997952 | bytes 1 | tf_op jit(solution)/shard_map/expert/pallas_call | solution.py:176
  351.6 8.3 collective-permute-done.20.refs_3_.refs_1_
  371.2 12.7 %expert.5 = (bf16[512,2048]{1,0:T(8,128)(2,1)}, bf16[512,768]{1,0:T(8,128)(2,1)}, bf16[512,768]{1,0:T(8,128)(2,1)}, bf16[512,768]{1,0:T(8,128)(2,1)}, f32[512,1]{1,0:T(8,128)}) custom-call(bf16[512,2048]{1,0:T(8,128)(2,1)} %bitcast.83.x_ref.refs_1_, f32[512,768]{1,0:T(8,128)} %matmul_nt.6.pulled_ref, bf16[512,128]{1,0:T(8,128)(2,1)} %bitcast.358, ...), custom_call_target="tpu_custom_call" | custom-call | flops 99999997952 | bytes 1 | tf_op jit(solution)/shard_map/expert/pallas_call | solution.py:176
  383.9 8.0 collective-permute-done.21.refs_2_
  403.7 12.6 %expert.6 = (bf16[512,2048]{1,0:T(8,128)(2,1)}, bf16[512,768]{1,0:T(8,128)(2,1)}, bf16[512,768]{1,0:T(8,128)(2,1)}, bf16[512,768]{1,0:T(8,128)(2,1)}, f32[512,1]{1,0:T(8,128)}) custom-call(bf16[512,2048]{1,0:T(8,128)(2,1)} %bitcast.296, f32[512,768]{1,0:T(8,128)} %matmul_nt.7.pulled_ref, bf16[512,128]{1,0:T(8,128)(2,1)} %bitcast.357, ...), custom_call_target="tpu_custom_call" | custom-call | flops 99999997952 | bytes 1 | tf_op jit(solution)/shard_map/expert/pallas_call | solution.py:176
  416.4 14.0 %all-to-all-done.10 = bf16[8,64,2048]{2,1,0:T(8,128)(2,1)} async-done(((bf16[8,64,2048]{2,1,0:T(8,128)(2,1)}), bf16[8,64,2048]{2,1,0:T(8,128)(2,1)}, u32[]{:S(2)}, u32[]{:S(2)}) %all-to-all-start.10) | async-done | bytes 2097184 | tf_op jit(solution)/shard_map/all_to_all | solution.py:875
  430.4 12.6 %expert.7 = (bf16[512,2048]{1,0:T(8,128)(2,1)}, bf16[512,768]{1,0:T(8,128)(2,1)}, bf16[512,768]{1,0:T(8,128)(2,1)}, bf16[512,768]{1,0:T(8,128)(2,1)}, f32[512,1]{1,0:T(8,128)}) custom-call(bf16[512,2048]{1,0:T(8,128)(2,1)} %bitcast.87.x_ref.refs_3_, f32[512,768]{1,0:T(8,128)} %matmul_nt.8.pulled_ref, bf16[512,128]{1,0:T(8,128)(2,1)} %bitcast.356, ...), custom_call_target="tpu_custom_call" | custom-call | flops 99999997952 | bytes 1 | tf_op jit(solution)/shard_map/expert/pallas_call | solution.py:176
  458.4 14.8 %all-to-all-done.11 = bf16[8,64,2048]{2,1,0:T(8,128)(2,1)S(1)} async-done(((bf16[8,64,2048]{2,1,0:T(8,128)(2,1)}), bf16[8,64,2048]{2,1,0:T(8,128)(2,1)S(1)}, u32[]{:S(2)}, u32[]{:S(2)}) %all-to-all-start.11) | async-done | bytes 2097184 | tf_op jit(solution)/shard_map/all_to_all | solution.py:875
  486.3 6.5 collective-permute-start.22
  492.8 15.4 %all-to-all-done.12 = bf16[8,64,2048]{2,1,0:T(8,128)(2,1)S(1)} async-done(((bf16[8,64,2048]{2,1,0:T(8,128)(2,1)}), bf16[8,64,2048]{2,1,0:T(8,128)(2,1)S(1)}, u32[]{:S(2)}, u32[]{:S(2)}) %all-to-all-start.12) | async-done | bytes 2097184 | tf_op jit(solution)/shard_map/all_to_all | solution.py:875
  529.0 10.8 %all-to-all-done.13 = bf16[8,64,2048]{2,1,0:T(8,128)(2,1)S(1)} async-done(((bf16[8,64,2048]{2,1,0:T(8,128)(2,1)}), bf16[8,64,2048]{2,1,0:T(8,128)(2,1)S(1)}, u32[]{:S(2)}, u32[]{:S(2)}) %all-to-all-start.13) | async-done | bytes 2097184 | tf_op jit(solution)/shard_map/all_to_all | solution.py:875
  563.0 9.5 %all-to-all-done.14 = bf16[8,64,2048]{2,1,0:T(8,128)(2,1)} async-done(((bf16[8,64,2048]{2,1,0:T(8,128)(2,1)}), bf16[8,64,2048]{2,1,0:T(8,128)(2,1)}, u32[]{:S(2)}, u32[]{:S(2)}) %all-to-all-start.14) | async-done | bytes 2097184 | tf_op jit(solution)/shard_map/all_to_all | solution.py:875
  580.1 11.2 %all-to-all-done.15 = f32[32,1,64]{2,1,0:T(1,128)S(1)} async-done(((f32[32,1,64]{2,1,0:T(1,128)}), f32[32,1,64]{2,1,0:T(1,128)S(1)}, u32[]{:S(2)}, u32[]{:S(2)}) %all-to-all-start.15) | async-done | bytes 8224 | tf_op jit(solution)/shard_map/all_to_all | solution.py:1035
  603.6 13.1 %contract_chunks.3 = f32[768,2048]{1,0:T(8,128)} custom-call(bf16[512,768]{1,0:T(8,128)(2,1)} %get-tuple-element.412.a_ref.refs_0_, bf16[512,768]{1,0:T(8,128)(2,1)} %get-tuple-element.413.a_ref.refs_1_, bf16[512,768]{1,0:T(8,128)(2,1)} %get-tuple-element.414.a_ref.refs_2_, bf16[512,768]{1,0:T(8,128)(2,1)} %get-tuple-element.415.a_ref.refs_3_, ...), custom_call_target="tpu_custom_call" | custom-call | flops 1 | bytes 1 | tf_op jit(solution)/shard_map/contract_chunks/pallas_call | solution.py:176
  617.7 12.5 %all-to-all-done.16 = bf16[8,64,2048]{2,1,0:T(8,128)(2,1)S(1)} async-done(((bf16[8,64,2048]{2,1,0:T(8,128)(2,1)}), bf16[8,64,2048]{2,1,0:T(8,128)(2,1)S(1)}, u32[]{:S(2)}, u32[]{:S(2)}) %all-to-all-start.16) | async-done | bytes 2097184 | tf_op jit(solution)/shard_map/all_to_all | solution.py:875
  638.7 13.1 %contract_chunks.4 = f32[2048,768]{1,0:T(8,128)} custom-call(bf16[512,2048]{1,0:T(8,128)(2,1)} %bitcast.79.x_ref.refs_0_, bf16[512,2048]{1,0:T(8,128)(2,1)} %bitcast.83.x_ref.refs_1_, bf16[512,2048]{1,0:T(8,128)(2,1)} %bitcast.297, bf16[512,2048]{1,0:T(8,128)(2,1)} %bitcast.87.x_ref.refs_3_, bf16[512,768]{1,0:T(8,128)(2,1)} %get-tuple-element.424.refs_4_, ...), custom_call_target="tpu_custom_call" | custom-call | flops 1 | bytes 1 | tf_op jit(solution)/shard_map/contract_chunks/pallas_call | solution.py:176
  651.7 10.0 %all-to-all-done.17 = bf16[8,64,2048]{2,1,0:T(8,128)(2,1)S(1)} async-done(((bf16[8,64,2048]{2,1,0:T(8,128)(2,1)}), bf16[8,64,2048]{2,1,0:T(8,128)(2,1)S(1)}, u32[]{:S(2)}, u32[]{:S(2)}) %all-to-all-start.17) | async-done | bytes 2097184 | tf_op jit(solution)/shard_map/all_to_all | solution.py:875
  667.5 13.1 %contract_chunks.5 = f32[2048,768]{1,0:T(8,128)} custom-call(bf16[512,2048]{1,0:T(8,128)(2,1)} %bitcast.79.x_ref.refs_0_, bf16[512,2048]{1,0:T(8,128)(2,1)} %bitcast.83.x_ref.refs_1_, bf16[512,2048]{1,0:T(8,128)(2,1)} %bitcast.298, bf16[512,2048]{1,0:T(8,128)(2,1)} %bitcast.87.x_ref.refs_3_, bf16[512,768]{1,0:T(8,128)(2,1)} %get-tuple-element.433.refs_4_, ...), custom_call_target="tpu_custom_call" | custom-call | flops 1 | bytes 1 | tf_op jit(solution)/shard_map/contract_chunks/pallas_call | solution.py:176
  682.8 8.6 matmul_nt.9.refs_3_
  691.4 8.5 matmul_tn.2
  715.9 27.3 %attend_back.2 = (bf16[768,1024]{1,0:T(8,128)(2,1)}, f32[1024,256]{1,0:T(8,128)}, f32[1024,256]{1,0:T(8,128)}) custom-call(s32[8]{0:T(128)S(1)} %pad_add_fusion.table, bf16[1024,256]{1,0:T(8,128)(2,1)} %get-tuple-element.277.refs_0_, bf16[1024,256]{1,0:T(8,128)(2,1)} %collective-permute-done.13.refs_1_, bf16[1024,1024]{1,0:T(8,128)(2,1)} %get-tuple-element.279.refs_2_, ...), custom_call_target="tpu_custom_call" | custom-call | flops 99999997952 | bytes 1 | tf_op jit(solution)/shard_map/attend_back/pallas_call | solution.py:176
  753.8 17.3 %attend_back.3 = (bf16[256,1024]{1,0:T(8,128)(2,1)}, f32[1024,256]{1,0:T(8,128)}, f32[1024,256]{1,0:T(8,128)}) custom-call(s32[8]{0:T(128)S(1)} %pad_add_fusion.table, bf16[1024,256]{1,0:T(8,128)(2,1)} %get-tuple-element.277.refs_0_, bf16[1024,256]{1,0:T(8,128)(2,1)} %collective-permute-done.13.refs_1_, bf16[1024,1024]{1,0:T(8,128)(2,1)} %get-tuple-element.279.refs_2_, ...), custom_call_target="tpu_custom_call" | custom-call | flops 99999997952 | bytes 1 | tf_op jit(solution)/shard_map/attend_back/pallas_call | solution.py:176
  779.0 14.3 %project_back.1 = (bf16[1024,2048]{1,0:T(8,128)(2,1)}, bf16[1024,1280]{1,0:T(8,128)(2,1)}, f32[1,128]{1,0:T(1,128)}, f32[1,128]{1,0:T(1,128)}) custom-call(f32[1024,1280]{1,0:T(8,128)} %get-tuple-element.308.raw_ref, bf16[768,1024]{1,0:T(8,128)(2,1)} %get-tuple-element.454.near_ref, bf16[256,1024]{1,0:T(8,128)(2,1)} %get-tuple-element.467.last_ref, ...), custom_call_target="tpu_custom_call" | custom-call | flops 99999997952 | bytes 1 | tf_op jit(solution)/shard_map/project_back/pallas_call | solution.py:176
  808.8 9.7 %matmul_tn.3 = bf16[2048,1280]{1,0:T(8,128)(2,1)} custom-call(bf16[1024,2048]{1,0:T(8,128)(2,1)} %get-tuple-element.307.a_ref.value_ref, bf16[1024,1280]{1,0:T(8,128)(2,1)} %get-tuple-element.479.b_ref), custom_call_target="tpu_custom_call" | custom-call | flops 1 | bytes 1 | tf_op jit(solution)/shard_map/matmul_tn/pallas_call | solution.py:176
  (483 shorter events, 458.5 us)
Async XLA Ops:
  8.0 113.5 %all-gather.4.cloned.1.call-start = ((), (), s32[]{:S(2)}) async-start(), calls=%async_computation.24 | async-start | bytes 5242880 | tf_op jit(solution)/shard_map/all_gather | solution.py:854
  8.1 31.2 %collective-permute-start = (bf16[512,512]{1,0:T(8,128)(2,1)}, bf16[512,512]{1,0:T(8,128)(2,1)S(1)}, u32[]{:S(2)}, u32[]{:S(2)}) collective-permute-start(bf16[512,512]{1,0:T(8,128)(2,1)} %param.20), channel_id=1, source_target_pairs={{0,8},{8,0},{16,24},{24,16},{1,9},{9,1},{17,25},{25,17},{2,10},{10... | collective-permute-start | bytes 1572872 | tf_op jit(solution)/shard_map/ppermute | solution.py:132
  41.8 36.0 %collective-permute-start.3 = (bf16[2048,512]{1,0:T(8,128)(2,1)}, bf16[2048,512]{1,0:T(8,128)(2,1)}, u32[]{:S(2)}, u32[]{:S(2)}) collective-permute-start(bf16[2048,512]{1,0:T(8,128)(2,1)} %bitcast.4), channel_id=1, source_target_pairs={{1,0},{0,1},{3,2},{2,3},{5,4},{4,5},{7,6},{6,7},{9,8},{8,9},{11,10... | collective-permute-start | bytes 6291464 | tf_op jit(solution)/shard_map/ppermute | solution.py:140
  101.8 35.5 %collective-permute-start.11 = (bf16[256,2048]{1,0:T(8,128)(2,1)S(1)}, bf16[256,2048]{1,0:T(8,128)(2,1)S(1)}, u32[]{:S(2)}, u32[]{:S(2)}) collective-permute-start(bf16[256,2048]{1,0:T(8,128)(2,1)S(1)} %copy-done.10), channel_id=1, source_target_pairs={{0,2},{2,4},{4,6},{1,3},{3,5},{5,7},{8,10},{10,12},{12,14},{9,11},... | collective-permute-start | bytes 3145736 | tf_op jit(solution)/shard_map/ppermute | solution.py:68
  105.7 31.6 %collective-permute-start.12 = (bf16[256,2048]{1,0:T(8,128)(2,1)S(1)}, bf16[256,2048]{1,0:T(8,128)(2,1)S(1)}, u32[]{:S(2)}, u32[]{:S(2)}) collective-permute-start(bf16[256,2048]{1,0:T(8,128)(2,1)S(1)} %copy-done.10), channel_id=1, source_target_pairs={{2,0},{4,2},{6,4},{3,1},{5,3},{7,5},{10,8},{12,10},{14,12},{11,9},... | collective-permute-start | bytes 3145736 | tf_op jit(solution)/shard_map/ppermute | solution.py:69
  116.9 32.1 %all-to-all-start.2 = ((bf16[8,64,2048]{2,1,0:T(8,128)(2,1)}), bf16[8,64,2048]{2,1,0:T(8,128)(2,1)}, u32[]{:S(2)}, u32[]{:S(2)}) async-start(bf16[8,64,2048]{2,1,0:T(8,128)(2,1)} %bitcast.314), calls=%async_computation.2 | async-start | bytes 4194304 | tf_op jit(solution)/shard_map/all_to_all | solution.py:875
  121.3 65.0 %all-gather.6.cloned.1.call-start = ((), (), s32[]{:S(2)}) async-start(), calls=%async_computation.25 | async-start | bytes 4718592 | tf_op jit(solution)/shard_map/all_gather | solution.py:889
  138.3 34.2 %collective-permute-start.14 = (bf16[256,2048]{1,0:T(8,128)(2,1)S(1)}, bf16[256,2048]{1,0:T(8,128)(2,1)S(1)}, u32[]{:S(2)}, u32[]{:S(2)}) collective-permute-start(bf16[256,2048]{1,0:T(8,128)(2,1)S(1)} %collective-permute-done.11.refs_0_), channel_id=1, source_target_pairs={{2,4},{4,6},{3,5},{5,7},{10,12},{12,14},{11,13},{13,15},{18,20},{2... | collective-permute-start | bytes 3145736 | tf_op jit(solution)/shard_map/ppermute | solution.py:75
  139.0 33.5 %collective-permute-start.15 = (bf16[256,2048]{1,0:T(8,128)(2,1)}, bf16[256,2048]{1,0:T(8,128)(2,1)S(1)}, u32[]{:S(2)}, u32[]{:S(2)}) collective-permute-start(bf16[256,2048]{1,0:T(8,128)(2,1)} %copy-done.26), channel_id=1, source_target_pairs={{4,2},{2,0},{5,3},{3,1},{12,10},{10,8},{13,11},{11,9},{20,18},{18,... | collective-permute-start | bytes 3145736 | tf_op jit(solution)/shard_map/ppermute | solution.py:76
  149.0 50.4 %all-to-all-start.3 = ((bf16[8,64,2048]{2,1,0:T(8,128)(2,1)}), bf16[8,64,2048]{2,1,0:T(8,128)(2,1)}, u32[]{:S(2)}, u32[]{:S(2)}) async-start(bf16[8,64,2048]{2,1,0:T(8,128)(2,1)} %bitcast.319), calls=%async_computation.3 | async-start | bytes 4194304 | tf_op jit(solution)/shard_map/all_to_all | solution.py:875
  153.3 134.0 %reduce-scatter.4.cloned.1.call-start = ((), (), s32[]{:S(2)}) async-start(), calls=%async_computation.26 | async-start | bytes 5242880 | tf_op jit(solution)/shard_map/reduce_scatter | solution.py:951
  205.4 33.1 %all-to-all-start.4 = ((bf16[8,64,2048]{2,1,0:T(8,128)(2,1)}), bf16[8,64,2048]{2,1,0:T(8,128)(2,1)}, u32[]{:S(2)}, u32[]{:S(2)}) async-start(bf16[8,64,2048]{2,1,0:T(8,128)(2,1)} %bitcast.324), calls=%async_computation.5 | async-start | bytes 4194304 | tf_op jit(solution)/shard_map/all_to_all | solution.py:875
  295.1 39.0 %all-to-all-start.7 = ((bf16[8,64,2048]{2,1,0:T(8,128)(2,1)}), bf16[8,64,2048]{2,1,0:T(8,128)(2,1)}, u32[]{:S(2)}, u32[]{:S(2)}) async-start(bf16[8,64,2048]{2,1,0:T(8,128)(2,1)} %bitcast.313), calls=%async_computation.8 | async-start | bytes 4194304 | tf_op jit(solution)/shard_map/all_to_all | solution.py:875
  334.2 33.3 %all-to-all-start.8 = ((bf16[8,64,2048]{2,1,0:T(8,128)(2,1)}), bf16[8,64,2048]{2,1,0:T(8,128)(2,1)}, u32[]{:S(2)}, u32[]{:S(2)}) async-start(bf16[8,64,2048]{2,1,0:T(8,128)(2,1)} %bitcast.317), calls=%async_computation.9 | async-start | bytes 4194304 | tf_op jit(solution)/shard_map/all_to_all | solution.py:875
  367.5 30.3 %all-to-all-start.9 = ((bf16[8,64,2048]{2,1,0:T(8,128)(2,1)}), bf16[8,64,2048]{2,1,0:T(8,128)(2,1)S(1)}, u32[]{:S(2)}, u32[]{:S(2)}) async-start(bf16[8,64,2048]{2,1,0:T(8,128)(2,1)} %bitcast.318), calls=%async_computation.10 | async-start | bytes 4194304 | tf_op jit(solution)/shard_map/all_to_all | solution.py:875
  399.2 31.2 %all-to-all-start.10 = ((bf16[8,64,2048]{2,1,0:T(8,128)(2,1)}), bf16[8,64,2048]{2,1,0:T(8,128)(2,1)}, u32[]{:S(2)}, u32[]{:S(2)}) async-start(bf16[8,64,2048]{2,1,0:T(8,128)(2,1)} %bitcast.322), calls=%async_computation.11 | async-start | bytes 4194304 | tf_op jit(solution)/shard_map/all_to_all | solution.py:875
  443.0 30.2 %all-to-all-start.11 = ((bf16[8,64,2048]{2,1,0:T(8,128)(2,1)}), bf16[8,64,2048]{2,1,0:T(8,128)(2,1)S(1)}, u32[]{:S(2)}, u32[]{:S(2)}) async-start(bf16[8,64,2048]{2,1,0:T(8,128)(2,1)} %bitcast.339), calls=%async_computation.12 | async-start | bytes 4194304 | tf_op jit(solution)/shard_map/all_to_all | solution.py:875
  486.3 31.4 %collective-permute-start.22 = (bf16[256,2048]{1,0:T(8,128)(2,1)S(1)}, bf16[256,2048]{1,0:T(8,128)(2,1)}, u32[]{:S(2)}, u32[]{:S(2)}) collective-permute-start(bf16[256,2048]{1,0:T(8,128)(2,1)S(1)} %copy-done.5), channel_id=1, source_target_pairs={{0,2},{6,4},{1,3},{7,5},{8,10},{14,12},{9,11},{15,13},{16,18},{22,... | collective-permute-start | bytes 3145736 | tf_op jit(solution)/shard_map/ppermute | solution.py:90
  541.0 31.4 %all-to-all-start.14 = ((bf16[8,64,2048]{2,1,0:T(8,128)(2,1)}), bf16[8,64,2048]{2,1,0:T(8,128)(2,1)}, u32[]{:S(2)}, u32[]{:S(2)}) async-start(bf16[8,64,2048]{2,1,0:T(8,128)(2,1)} %bitcast.333), calls=%async_computation.15 | async-start | bytes 4194304 | tf_op jit(solution)/shard_map/all_to_all | solution.py:875
  556.0 36.9 %collective-permute-start.25 = (bf16[256,2048]{1,0:T(8,128)(2,1)}, bf16[256,2048]{1,0:T(8,128)(2,1)S(1)}, u32[]{:S(2)}, u32[]{:S(2)}) collective-permute-start(bf16[256,2048]{1,0:T(8,128)(2,1)} %get-tuple-element.392), channel_id=1, source_target_pairs={{0,2},{2,4},{4,6},{1,3},{3,5},{5,7},{8,10},{10,12},{12,14},{9,11},... | collective-permute-start | bytes 3145736 | tf_op jit(solution)/shard_map/ppermute | solution.py:102
  561.7 31.2 %collective-permute-start.26 = (bf16[256,2048]{1,0:T(8,128)(2,1)}, bf16[256,2048]{1,0:T(8,128)(2,1)S(1)}, u32[]{:S(2)}, u32[]{:S(2)}) collective-permute-start(bf16[256,2048]{1,0:T(8,128)(2,1)} %get-tuple-element.393), channel_id=1, source_target_pairs={{6,4},{4,2},{2,0},{7,5},{5,3},{3,1},{14,12},{12,10},{10,8},{15,13}... | collective-permute-start | bytes 3145736 | tf_op jit(solution)/shard_map/ppermute | solution.py:103
  576.5 104.0 %all-gather.8.cloned.1.call-start = ((), (), s32[]{:S(2)}) async-start(), calls=%async_computation.27 | async-start | bytes 5242880 | tf_op jit(solution)/shard_map/all_gather | solution.py:1055
  600.0 30.2 %all-to-all-start.16 = ((bf16[8,64,2048]{2,1,0:T(8,128)(2,1)}), bf16[8,64,2048]{2,1,0:T(8,128)(2,1)S(1)}, u32[]{:S(2)}, u32[]{:S(2)}) async-start(bf16[8,64,2048]{2,1,0:T(8,128)(2,1)} %bitcast.335), calls=%async_computation.17 | async-start | bytes 4194304 | tf_op jit(solution)/shard_map/all_to_all | solution.py:875
  663.0 80.2 %all-to-all-start.18 = ((bf16[8,64,2048]{2,1,0:T(8,128)(2,1)}), bf16[8,64,2048]{2,1,0:T(8,128)(2,1)}, u32[]{:S(2)}, u32[]{:S(2)}) async-start(bf16[8,64,2048]{2,1,0:T(8,128)(2,1)} %bitcast.334), calls=%async_computation.19 | async-start | bytes 4194304 | tf_op jit(solution)/shard_map/all_to_all | solution.py:875
  667.4 103.7 %reduce-scatter.6.cloned.1.call-start = ((), (), s32[]{:S(2)}) async-start(), calls=%async_computation.28 | async-start | bytes 4718592 | tf_op jit(solution)/shard_map/reduce_scatter | solution.py:1076
  710.5 32.7 %collective-permute-start.28 = (bf16[256,2048]{1,0:T(8,128)(2,1)}, bf16[256,2048]{1,0:T(8,128)(2,1)S(1)}, u32[]{:S(2)}, u32[]{:S(2)}) collective-permute-start(bf16[256,2048]{1,0:T(8,128)(2,1)} %get-tuple-element.451), channel_id=1, source_target_pairs={{0,2},{2,4},{1,3},{3,5},{8,10},{10,12},{9,11},{11,13},{16,18},{18,... | collective-permute-start | bytes 3145736 | tf_op jit(solution)/shard_map/ppermute | solution.py:95
  793.3 30.3 %all-to-all-start.19 = ((bf16[8,64,2048]{2,1,0:T(8,128)(2,1)}), bf16[8,64,2048]{2,1,0:T(8,128)(2,1)S(1)}, u32[]{:S(2)}, u32[]{:S(2)}) async-start(bf16[8,64,2048]{2,1,0:T(8,128)(2,1)} %bitcast.332), calls=%async_computation.21 | async-start | bytes 4194304 | tf_op jit(solution)/shard_map/all_to_all | solution.py:875
  796.9 93.4 %reduce-scatter.8.cloned.1.call-start = ((), (), s32[]{:S(2)}) async-start(), calls=%async_computation.29 | async-start | bytes 5242880 | tf_op jit(solution)/shard_map/reduce_scatter | solution.py:1099
  800.6 30.3 %collective-permute-start.36 = (bf16[32,2048]{1,0:T(8,128)(2,1)}, bf16[32,2048]{1,0:T(8,128)(2,1)}, u32[]{:S(2)}, u32[]{:S(2)}) collective-permute-start(bf16[32,2048]{1,0:T(8,128)(2,1)} %get-tuple-element.515), channel_id=1, source_target_pairs={{0,4},{2,6},{4,0},{6,2},{1,5},{3,7},{5,1},{7,3},{8,12},{10,14},{12... | collective-permute-start | bytes 393224 | tf_op jit(solution)/shard_map/ppermute | solution.py:122
  801.0 31.4 %collective-permute-start.37 = (bf16[32,2048]{1,0:T(8,128)(2,1)}, bf16[32,2048]{1,0:T(8,128)(2,1)S(1)}, u32[]{:S(2)}, u32[]{:S(2)}) collective-permute-start(bf16[32,2048]{1,0:T(8,128)(2,1)} %get-tuple-element.514), channel_id=1, source_target_pairs={{0,6},{2,4},{4,2},{6,0},{1,7},{3,5},{5,3},{7,1},{8,14},{10,12},{12... | collective-permute-start | bytes 393224 | tf_op jit(solution)/shard_map/ppermute | solution.py:122
  837.2 31.6 %collective-permute-start.49 = (bf16[32,2048]{1,0:T(8,128)(2,1)}, bf16[32,2048]{1,0:T(8,128)(2,1)}, u32[]{:S(2)}, u32[]{:S(2)}) collective-permute-start(bf16[32,2048]{1,0:T(8,128)(2,1)} %get-tuple-element.507), channel_id=1, source_target_pairs={{0,24},{8,16},{16,8},{24,0},{1,25},{9,17},{17,9},{25,1},{2,26},{10... | collective-permute-start | bytes 393224 | tf_op jit(solution)/shard_map/ppermute | solution.py:122
  846.0 42.3 %all-to-all-start.20 = ((f32[32,1,2432]{2,1,0:T(1,128)}), f32[32,1,2432]{2,1,0:T(1,128)S(1)}, u32[]{:S(2)}, u32[]{:S(2)}) async-start(f32[32,1,2432]{2,1,0:T(1,128)} %copy.210), calls=%async_computation.23 | async-start | bytes 622592 | tf_op jit(solution)/shard_map/all_to_all | solution.py:1127
  (108 other events, 1416.8 us)
Sparse Core Ops, SparseCore 0:
  24.5 92.6 all-gather.3
  201.5 77.5 reduce-scatter.3
  600.1 77.1 all-gather.7
  799.9 87.6 reduce-scatter.7
Sparse Core Ops, SparseCore 1:
  137.4 48.8 all-gather.5
  716.0 51.5 reduce-scatter.5
